TPU v7x, 32 devices: a whole 2x2x4 slice. The times are simulated.
32 devices in a mesh: rows: 8 (over z, x), tensor: 2 (over core), groups: 2 (over y).
Axes of the slice: x: 2, y: 2, z: 4, core: 2. Of those that a mesh axis runs over, the one named last changes fastest.
Arguments:
- effects: float32 [4096, 1024], P(('groups', 'rows'), 'tensor'), parts along dimension 0, may hold values from -8 to 8
Outputs:
- basis: float32 [4096, 1024], P(('groups', 'rows'), 'tensor'), parts along dimension 0
- triangle: float32 [2048, 1024], P('groups', 'tensor'), parts along dimension 0
There are 2 independent parts, one for each index of `groups`. A program takes and returns all parts, laid end to end along the dimension named above; each array names one. Nothing has to cross between parts.
All inputs are finite; a program needn't handle non-finite values.
Results may differ from a plain program's by a relative error of at most 0.000075.
Values sent between devices are 32-bit elements; how exact they have to be, the bound alone decides.
No kernel may reach another device: no remote copies, remote signals or barrier semaphores. Data moves between devices by JAX's collectives and lax.ppermute only.
A program may use at most 64 MiB of HBM per device.

v0:
```python
import jax
import jax.numpy as jnp
from jax import lax
from jax.sharding import PartitionSpec as P


def shards(effects):
    whole = lax.all_gather(effects, "tensor", axis=1, tiled=True)
    width = effects.shape[1]
    own_block = jnp.dot(
        effects.T, whole, precision=lax.Precision.HIGHEST, preferred_element_type=jnp.float32
    )
    summed = lax.psum(own_block, "rows")
    gram = lax.all_gather(summed, "tensor", axis=0, tiled=True)
    lower = jnp.linalg.cholesky(gram)
    total = effects.shape[0] * lax.axis_size("rows")
    scale = jnp.sqrt(jnp.float32(total))
    full_width = whole.shape[1]
    start = lax.axis_index("tensor") * width
    position = lax.broadcasted_iota(jnp.int32, (full_width, width), 0)
    column_id = lax.broadcasted_iota(jnp.int32, (full_width, width), 1) + start
    identity_cols = jnp.where(position == column_id, jnp.float32(1.0), jnp.float32(0.0))
    inverse_cols = lax.linalg.triangular_solve(
        lower, identity_cols, left_side=True, lower=True, transpose_a=True
    )
    own_solved = jnp.dot(
        whole, inverse_cols, precision=lax.Precision.HIGHEST, preferred_element_type=jnp.float32
    )
    basis = own_solved * scale
    own_lower = lax.dynamic_slice_in_dim(lower, start, width, 0)
    triangle = own_lower.T / scale
    return (basis, triangle)


def solution(mesh):
    in_specs = (P(("groups", "rows"), "tensor"),)
    out_specs = (P(("groups", "rows"), "tensor"), P("groups", "tensor"))
    return jax.shard_map(shards, mesh=mesh, in_specs=in_specs, out_specs=out_specs, check_vma=False)
```

profile of v0, /device:TPU:0, one launch (start us, length us, event | category | flops | bytes accessed | tf_op | source)
XLA Modules:
  0.0 496.8 jit_solution(6415215567255886843)
XLA Ops:
  7.9 13.4 %all-gather.3.cloned.1.call-done = f32[256,1024]{1,0:T(8,128)} async-done(((f32[256,512]{1,0:T(8,128)}), f32[256,1024]{1,0:T(8,128)}) %all-gather.3.cloned.1.call-update) | async-done | bytes 1048592 | tf_op jit(solution)/shard_map/all_gather | solution.py:8
  21.3 4.6 fusion.65
  26.0 103.1 %all-reduce.3.cloned.1.call-done = f32[512,1024]{0,1:T(8,128)} async-done(((f32[512,1024]{0,1:T(8,128)}), f32[512,1024]{0,1:T(8,128)}) %all-reduce.3.cloned.1.call-update) | async-done | bytes 2097168 | tf_op jit(solution)/shard_map/psum | solution.py:13
  129.2 1.7 fusion.2
  130.8 13.2 %all-gather.5.cloned.1.call-done = f32[1024,1024]{0,1:T(8,128)} async-done(((f32[512,1024]{0,1:T(8,128)}), f32[1024,1024]{0,1:T(8,128)}) %all-gather.5.cloned.1.call-update) | async-done | bytes 4194320 | tf_op jit(solution)/shard_map/all_gather | solution.py:14
  144.1 5.5 %copy.4 = f32[1024,1024]{1,0:T(8,128)} copy(f32[1024,1024]{0,1:T(8,128)} %all-gather.5.cloned.1.call-done) | data formatting | bytes 8388608 | tf_op jit(solution)/shard_map/all_gather | solution.py:14
  149.6 4.4 fusion
  154.0 1.9 copy-done
  155.9 11.7 %cholesky.223 = f32[128,128]{1,0:T(8,128)S(1)} custom-call(f32[128,128]{1,0:T(8,128)S(1)} %cholesky.580), custom_call_target="Cholesky" | custom-call | tf_op jit(solution)/shard_map/jit(cholesky)/cholesky | solution.py:15
  167.7 9.8 %custom-call.62 = f32[1,128,128]{1,2,0:T(8,128)S(1)} custom-call(f32[1,128,128]{2,1,0:T(8,128)S(1)} %get-tuple-element.45), custom_call_target="InvertDiagBlocksLowerTriangular" | custom-call | tf_op jit(solution)/shard_map/jit(cholesky)/cholesky | solution.py:15
  177.5 2.5 cholesky.255
  180.0 2.4 constant_dynamic-update-slice_fusion.32
  183.9 11.9 %cholesky.244 = f32[128,128]{1,0:T(8,128)S(1)} custom-call(f32[128,128]{1,0:T(8,128)S(1)} %cholesky.584), custom_call_target="Cholesky" | custom-call | tf_op jit(solution)/shard_map/jit(cholesky)/cholesky | solution.py:15
  196.5 9.8 %custom-call.63 = f32[1,128,128]{1,2,0:T(8,128)S(1)} custom-call(f32[1,128,128]{2,1,0:T(8,128)S(1)} %get-tuple-element.42), custom_call_target="InvertDiagBlocksLowerTriangular" | custom-call | tf_op jit(solution)/shard_map/jit(cholesky)/cholesky | solution.py:15
  207.6 2.1 convolution_subtract_fusion.1
  209.7 11.7 %cholesky.468 = f32[128,128]{1,0:T(8,128)S(1)} custom-call(f32[128,128]{1,0:T(8,128)S(1)} %cholesky.589), custom_call_target="Cholesky" | custom-call | tf_op jit(solution)/shard_map/jit(cholesky)/cholesky | solution.py:15
  222.7 9.8 %custom-call.64 = f32[1,128,128]{1,2,0:T(8,128)S(1)} custom-call(f32[1,128,128]{2,1,0:T(8,128)S(1)} %get-tuple-element.39), custom_call_target="InvertDiagBlocksLowerTriangular" | custom-call | tf_op jit(solution)/shard_map/jit(cholesky)/cholesky | solution.py:15
  233.7 2.3 convolution_subtract_fusion.2
  236.0 12.1 %cholesky.487 = f32[128,128]{1,0:T(8,128)S(1)} custom-call(f32[128,128]{1,0:T(8,128)S(1)} %cholesky.594), custom_call_target="Cholesky" | custom-call | tf_op jit(solution)/shard_map/jit(cholesky)/cholesky | solution.py:15
  249.4 9.8 %custom-call.65 = f32[1,128,128]{1,2,0:T(8,128)S(1)} custom-call(f32[1,128,128]{2,1,0:T(8,128)S(1)} %get-tuple-element.36), custom_call_target="InvertDiagBlocksLowerTriangular" | custom-call | tf_op jit(solution)/shard_map/jit(cholesky)/cholesky | solution.py:15
  260.4 2.3 convolution_subtract_fusion.10
  262.7 11.7 %cholesky.506 = f32[128,128]{1,0:T(8,128)S(1)} custom-call(f32[128,128]{1,0:T(8,128)S(1)} %cholesky.599), custom_call_target="Cholesky" | custom-call | tf_op jit(solution)/shard_map/jit(cholesky)/cholesky | solution.py:15
  275.7 9.9 %custom-call.66 = f32[1,128,128]{1,2,0:T(8,128)S(1)} custom-call(f32[1,128,128]{2,1,0:T(8,128)S(1)} %get-tuple-element.33), custom_call_target="InvertDiagBlocksLowerTriangular" | custom-call | tf_op jit(solution)/shard_map/jit(cholesky)/cholesky | solution.py:15
  286.7 2.3 convolution_subtract_fusion.11
  289.0 11.7 %cholesky.526 = f32[128,128]{1,0:T(8,128)S(1)} custom-call(f32[128,128]{1,0:T(8,128)S(1)} %cholesky.604), custom_call_target="Cholesky" | custom-call | tf_op jit(solution)/shard_map/jit(cholesky)/cholesky | solution.py:15
  302.1 9.8 %custom-call.67 = f32[1,128,128]{1,2,0:T(8,128)S(1)} custom-call(f32[1,128,128]{2,1,0:T(8,128)S(1)} %get-tuple-element.30), custom_call_target="InvertDiagBlocksLowerTriangular" | custom-call | tf_op jit(solution)/shard_map/jit(cholesky)/cholesky | solution.py:15
  312.8 2.0 convolution_subtract_fusion.12
  314.8 11.9 %cholesky.546 = f32[128,128]{1,0:T(8,128)S(1)} custom-call(f32[128,128]{1,0:T(8,128)S(1)} %cholesky.609), custom_call_target="Cholesky" | custom-call | tf_op jit(solution)/shard_map/jit(cholesky)/cholesky | solution.py:15
  328.0 9.8 %custom-call.68 = f32[1,128,128]{1,2,0:T(8,128)S(1)} custom-call(f32[1,128,128]{2,1,0:T(8,128)S(1)} %get-tuple-element.27), custom_call_target="InvertDiagBlocksLowerTriangular" | custom-call | tf_op jit(solution)/shard_map/jit(cholesky)/cholesky | solution.py:15
  338.7 1.8 convolution_subtract_fusion.13
  340.5 11.7 %cholesky.564 = f32[128,128]{1,0:T(8,128)S(1)} custom-call(f32[128,128]{1,0:T(8,128)S(1)} %convolution_subtract_fusion.13), custom_call_target="Cholesky" | custom-call | tf_op jit(solution)/shard_map/jit(cholesky)/cholesky | solution.py:15
  359.2 4.8 fusion.1
  364.3 1.8 copy.6
  366.1 22.9 %while.1 = (s32[]{:T(128)}, f32[1024,1024]{1,0:T(8,128)}, s32[8,2]{0,1:T(2,128)S(1)}, f32[8,128,128]{2,1,0:T(8,128)S(1)}, s32[]{:T(128)}) while((s32[]{:T(128)}, f32[1024,1024]{1,0:T(8,128)}, s32[8,2]{0,1:T(2,128)S(1)}, f32[8,128,128]{2,1,0:T(8,128)S(1)}, s32[]{:T(128)}) %tuple.44), condition=%wide.while_cond, body=%wide.while_body.sunk | while | flops 2 | bytes 131189 | solution.py:23
  366.7 2.3 bitcast_dynamic-update-slice_fusion.2
  369.6 2.2 bitcast_dynamic-update-slice_fusion.2
  372.5 2.2 bitcast_dynamic-update-slice_fusion.2
  375.3 2.2 bitcast_dynamic-update-slice_fusion.2
  378.2 2.2 bitcast_dynamic-update-slice_fusion.2
  381.1 2.2 bitcast_dynamic-update-slice_fusion.2
  383.9 2.2 bitcast_dynamic-update-slice_fusion.2
  386.8 2.2 bitcast_dynamic-update-slice_fusion.2
  388.9 78.8 %custom-call.69 = f32[8,128,128]{1,2,0:T(8,128)S(1)} custom-call(f32[8,128,128]{2,1,0:T(8,128)S(1)} %get-tuple-element.9), custom_call_target="InvertDiagBlocksLowerTriangular" | custom-call | tf_op jit(solution)/shard_map/triangular_solve | solution.py:23
  474.6 1.7 convolution_subtract_fusion.9
  476.8 1.9 convolution_subtract_fusion.4
  479.3 2.1 convolution_subtract_fusion.7
  481.9 2.3 convolution_subtract_fusion.3
  485.4 3.5 fusion.3
  (95 shorter events, 33.5 us)
Async XLA Ops:
  7.2 14.1 %all-gather.3.cloned.1.call-start = ((), (), s32[]{:S(2)}) async-start(), calls=%async_computation | async-start | bytes 1572864 | tf_op jit(solution)/shard_map/all_gather | solution.py:8
  7.9 121.2 %all-reduce.3.cloned.1.call-start = ((), (), s32[]{:S(2)}) async-start(), calls=%async_computation.1 | async-start | bytes 4194304 | tf_op jit(solution)/shard_map/psum | solution.py:13
  25.9 118.2 %all-gather.5.cloned.1.call-start = ((), (), s32[]{:S(2)}) async-start(), calls=%async_computation.2 | async-start | bytes 6291456 | tf_op jit(solution)/shard_map/all_gather | solution.py:14
  154.0 1.9 copy-start
  366.1 104.8 %copy-start.1 = (f32[1024,512]{1,0:T(8,128)S(1)}, f32[1024,512]{1,0:T(8,128)}, u32[]{:S(2)}) copy-start(f32[1024,512]{1,0:T(8,128)} %fusion.2) | copy-start | bytes 6291460
  484.2 1.2 copy-start.2
Sparse Core Ops, SparseCore 0:
  9.5 11.7 all-gather.2
  26.0 103.0 all-reduce.2
  130.6 13.3 all-gather.4
where the time goes:
time: 501 us; the launch traced here: 497 us
  other arithmetic  262 us (52%)
  waiting for transfers between devices  130 us (26%)
  matrix products  47.3 us (9%)
  local copies, waits for them, and re-layouts  36.6 us (7%)
  between operations  19.8 us (4%)
    another operation x30, other arithmetic, shards(): lower = jnp.linalg.cholesky(gram)  172 us
    psum x1, waiting for transfers between devices, shards(): summed = lax.psum(own_block, 'rows')  103 us
    another operation x3, other arithmetic, shards(): lax.linalg.triangular_solve(lower, identity_cols, left_side=True, lower=T...  83.7 us
    another operation x14, matrix products, shards(): lower = jnp.linalg.cholesky(gram)  23.1 us
    another operation x24, local copies, waits for them, and re-layouts  22.7 us
    another operation x15, matrix products, shards(): lax.linalg.triangular_solve(lower, identity_cols, left_side=True, lower=T...  16.2 us
    all_gather x1, waiting for transfers between devices, shards(): whole = lax.all_gather(effects, 'tensor', axis=1, tiled=True)  13.4 us
    all_gather x1, waiting for transfers between devices, shards(): gram = lax.all_gather(summed, 'tensor', axis=0, tiled=True)  13.2 us
  transfers between devices with their start and end apart: 3, of which 3 were waited for; matrix products, arithmetic and copies ran while one was open for 0% of the time, Pallas kernels for 0%

commit v1 on v0

v1 whole, which is shorter than its diff:
```python
import functools

import jax
import jax.numpy as jnp
from jax import lax
from jax.experimental import pallas as pl
from jax.experimental.pallas import tpu as pltpu
from jax.sharding import PartitionSpec as P

F32 = jnp.float32
HIGHEST = lax.Precision.HIGHEST
NB = 128
SUB = 8


def dot(a, b, dims=((1,), (0,))):
    return lax.dot_general(a, b, (dims, ((), ())), precision=HIGHEST, preferred_element_type=F32)


def row_of(x, k):
    return jnp.broadcast_to(x[k : k + 1, :], x.shape)


def lane_of(x, j):
    return jnp.broadcast_to(x[:, j : j + 1], x.shape)


def factor_block(rows, put_upper, put_inverse):
    lane = lax.broadcasted_iota(jnp.int32, (SUB, NB), 1)
    sub = lax.broadcasted_iota(jnp.int32, (SUB, NB), 0)
    rows = list(rows)
    count = len(rows)
    for g in range(count):
        first = SUB * g
        raw = rows[g]
        cols = [lane_of(raw, first + k) for k in range(SUB)]
        below = {h: [lane_of(rows[h], first + k) for k in range(SUB)] for h in range(g + 1, count)}
        in_group = (lane >= first) & (lane < first + SUB)
        right = raw
        left = jnp.where(in_group, jnp.where(lane - first == sub, F32(1), F32(0)), raw)
        upper = jnp.zeros_like(raw)
        inverse = jnp.zeros_like(raw)
        for k in range(SUB):
            mine = sub == k
            pivot = row_of(cols[k], k)
            recip = 1.0 / pivot
            root = lax.rsqrt(pivot)
            right_k, left_k = row_of(right, k), row_of(left, k)
            upper = jnp.where(mine, right_k * root, upper)
            inverse = jnp.where(mine, left_k * root, inverse)

            def eliminate(x, x_k):
                scaled = x_k * recip
                return jnp.where(mine, scaled, x - cols[k] * scaled)

            for m in range(k + 1, SUB):
                cols[m] = eliminate(cols[m], row_of(cols[m], k))
            right, left = eliminate(right, right_k), eliminate(left, left_k)
        put_upper(g, jnp.where(lane >= sub + first, upper, F32(0)))
        put_inverse(g, jnp.where(lane <= sub + first, inverse, F32(0)))
        solved = jnp.where(lane < first + SUB, left, right)
        solved_rows = [row_of(solved, k) for k in range(SUB)]
        for h in range(g + 1, count):
            p = [below[h][k] * solved_rows[k] for k in range(SUB)]
            total = ((p[0] + p[1]) + (p[2] + p[3])) + ((p[4] + p[5]) + (p[6] + p[7]))
            rows[h] = jnp.where(in_group, F32(0), rows[h]) - total


def pairs(n):
    return [(i, j) for i in range(n) for j in range(i, n)]


def gram_diag_kernel(own_ref, out_ref):
    blocks = own_ref.shape[1] // NB
    for at, (i, j) in enumerate(pairs(blocks)):
        out_ref[at * NB : (at + 1) * NB, :] = dot(
            own_ref[:, i * NB : (i + 1) * NB], own_ref[:, j * NB : (j + 1) * NB], ((0,), (0,))
        )


def gram_cross_kernel(first_ref, second_ref, out_ref):
    for i in range(first_ref.shape[1] // NB):
        for j in range(second_ref.shape[1] // NB):
            at = i * (second_ref.shape[1] // NB) + j
            out_ref[at * NB : (at + 1) * NB, :] = dot(
                first_ref[:, i * NB : (i + 1) * NB], second_ref[:, j * NB : (j + 1) * NB], ((0,), (0,))
            )


def solve_kernel(scale, t_ref, pay0_ref, pay1_ref, e0_ref, e1_ref, basis_ref, tri_ref, a_ref, e_ref, inv_ref):
    width = e0_ref.shape[1]
    half = width // NB
    n = 2 * half
    diag = pairs(half)

    def block(r, c):
        return slice(r * NB, (r + 1) * NB), slice(c * NB, (c + 1) * NB)

    for at, (i, j) in enumerate(diag):
        a_ref[block(i, j)] = pay0_ref[at * NB : (at + 1) * NB, :]
        a_ref[block(half + i, half + j)] = pay1_ref[at * NB : (at + 1) * NB, :]
    at = len(diag)
    for i in range(half):
        for j in range(half // 2):
            piece = slice(at * NB, (at + 1) * NB)
            a_ref[block(i, half + j)] = pay0_ref[piece, :]
            a_ref[block(i, half + half // 2 + j)] = pay1_ref[piece, :]
            at += 1
    e_ref[:, :width] = e0_ref[...]
    e_ref[:, width:] = e1_ref[...]

    for k in range(n):
        here = slice(k * NB, (k + 1) * NB)
        rest = slice((k + 1) * NB, n * NB)
        rows = [a_ref[k * NB + SUB * h : k * NB + SUB * (h + 1), here] for h in range(NB // SUB)]

        def put_upper(g, v):
            a_ref[k * NB + SUB * g : k * NB + SUB * (g + 1), here] = v

        def put_inverse(g, v):
            inv_ref[SUB * g : SUB * (g + 1), :] = v

        factor_block(rows, put_upper, put_inverse)
        inverse = inv_ref[...]
        solved = dot(e_ref[:, here], inverse.T)
        e_ref[:, here] = solved
        if k + 1 < n:
            upper = dot(inverse, a_ref[here, rest])
            a_ref[here, rest] = upper
            lower = upper.T
            for i in range(k + 1, n):
                off = (i - k - 1) * NB
                cols = slice(i * NB, n * NB)
                a_ref[i * NB : (i + 1) * NB, cols] -= dot(lower[off : off + NB, :], upper[:, off:])
            e_ref[:, rest] -= dot(solved, upper)

    start = pl.multiple_of(t_ref[0] * width, NB)
    basis_ref[...] = e_ref[:, pl.ds(start, width)] * scale
    for r in range(n):
        for c in range(half):
            col = t_ref[0] * half + c
            value = a_ref[r * NB : (r + 1) * NB, pl.ds(pl.multiple_of(col * NB, NB), NB)]
            tri_ref[r * NB : (r + 1) * NB, c * NB : (c + 1) * NB] = jnp.where(r <= col, value / scale, F32(0))


def sum_rows(payload, n):
    me = lax.axis_index("rows")
    parity, far = me % 2, me // 2
    nfar = n // 2
    size = payload.shape[0] // 2
    piece = size // nfar
    pair = [(i, i ^ 1) for i in range(n)]
    keep = lax.dynamic_slice_in_dim(payload, parity * size, size)
    send = lax.dynamic_slice_in_dim(payload, (1 - parity) * size, size)
    mine = keep + lax.ppermute(send, "rows", pair)

    def to(s):
        return [(i, 2 * ((i // 2) ^ s) + i % 2) for i in range(n)]

    total = lax.dynamic_slice_in_dim(mine, far * piece, piece)
    for s in range(1, nfar):
        part = lax.dynamic_slice_in_dim(mine, (far ^ s) * piece, piece)
        total = total + lax.ppermute(part, "rows", to(s))
    gathered = jnp.zeros_like(mine)
    gathered = lax.dynamic_update_slice_in_dim(gathered, total, far * piece, 0)
    for s in range(1, nfar):
        gathered = lax.dynamic_update_slice_in_dim(gathered, lax.ppermute(total, "rows", to(s)), (far ^ s) * piece, 0)
    other = lax.ppermute(gathered, "rows", pair)
    first = jnp.where(parity == 0, gathered, other)
    second = jnp.where(parity == 0, other, gathered)
    return jnp.concatenate([first, second])


def shards(n_rows, effects):
    rows, width = effects.shape
    cols = 2 * width
    half = width // NB
    n_diag, n_cross = half * (half + 1) // 2, half * half // 2
    t = lax.axis_index("tensor")
    swap = [(0, 1), (1, 0)]
    other = lax.ppermute(effects, "tensor", swap)
    diag = pl.pallas_call(
        gram_diag_kernel,
        out_shape=jax.ShapeDtypeStruct((n_diag * NB, NB), F32),
        cost_estimate=pl.CostEstimate(flops=12 * rows * n_diag * NB * NB, bytes_accessed=4 * rows * width, transcendentals=0),
        name="gram_diag",
    )(effects)
    e0 = jnp.where(t == 0, effects, other)
    e1 = jnp.where(t == 0, other, effects)
    cross = pl.pallas_call(
        gram_cross_kernel,
        out_shape=jax.ShapeDtypeStruct((n_cross * NB, NB), F32),
        name="gram_cross",
    )(e0, lax.dynamic_slice_in_dim(e1, t * (width // 2), width // 2, 1))
    payload = sum_rows(jnp.concatenate([diag, cross]), n_rows)
    payload_other = lax.ppermute(payload, "tensor", swap)
    pay0 = jnp.where(t == 0, payload, payload_other)
    pay1 = jnp.where(t == 0, payload_other, payload)
    scale = float(rows * n_rows) ** 0.5
    vmem = pl.BlockSpec(memory_space=pltpu.VMEM)
    return pl.pallas_call(
        functools.partial(solve_kernel, scale),
        out_shape=(jax.ShapeDtypeStruct((rows, width), F32), jax.ShapeDtypeStruct((cols, width), F32)),
        in_specs=[pl.BlockSpec(memory_space=pltpu.SMEM)] + [vmem] * 4,
        out_specs=(vmem, vmem),
        scratch_shapes=[pltpu.VMEM((cols, cols), F32), pltpu.VMEM((rows, cols), F32), pltpu.VMEM((NB, NB), F32)],
        compiler_params=pltpu.CompilerParams(vmem_limit_bytes=48 * 2**20),
        name="cholesky_solve",
    )(t.reshape(1).astype(jnp.int32), pay0, pay1, e0, e1)


def solution(mesh):
    spec = P(("groups", "rows"), "tensor")
    return jax.shard_map(
        functools.partial(shards, mesh.shape["rows"]),
        mesh=mesh,
        in_specs=(spec,),
        out_specs=(spec, P("groups", "tensor")),
        check_vma=False,
    )
```

time: 501 us -> 122 us (0.24)
  other arithmetic: 262 us -> 2.92 us
  waiting for transfers between devices: 130 us -> 49.9 us
  Pallas kernels: 0 us -> 53.3 us
  matrix products: 47.3 us -> 0 us
  local copies, waits for them, and re-layouts: 36.6 us -> 0.86 us
  between operations: 19.8 us -> 0.75 us
  starting transfers between devices: 0.12 us -> 12.6 us
    another operation x33 -> x0, other arithmetic: 256 us -> none  [the longest x30 172 us: shards(): lower = jnp.linalg.cholesky(gram)]
    psum x1 -> x0, waiting for transfers between devices: 103 us -> none  [shards(): summed = lax.psum(own_block, 'rows')]
    pallas_call x0 -> x3, Pallas kernels: none -> 53.3 us  [the longest x1 47.1 us: shards(): pl.pallas_call(functools.partial(solve_kernel, scale), out_shape=(jax.Sha...]
    ppermute x0 -> x10, waiting for transfers between devices: none -> 49.9 us  [the longest x1 13.9 us: sum_rows(): mine = keep + lax.ppermute(send, 'rows', pair)]
    another operation x29 -> x0, matrix products: 39.3 us -> none  [the longest x14 23.1 us: shards(): lower = jnp.linalg.cholesky(gram)]
    all_gather x2 -> x0, waiting for transfers between devices: 26.6 us -> none  [the longest x1 13.4 us: shards(): whole = lax.all_gather(effects, 'tensor', axis=1, tiled=True)]
    another operation x37 -> x0, local copies, waits for them, and re-layouts: 25.3 us -> none
    ppermute x0 -> x10, starting transfers between devices: none -> 12.6 us  [the longest x3 5.61 us: sum_rows(): total = total + lax.ppermute(part, 'rows', to(s))]
  transfers between devices with their start and end apart: 3 -> 10, of which waited for: 3 -> 8; matrix products, arithmetic and copies ran while one was open for 0% -> 0% of each run, Pallas kernels for 0% -> 3%
where the time goes in v1:
time: 122 us; the launch traced here: 120 us
  Pallas kernels  53.3 us (44%)
  waiting for transfers between devices  49.9 us (41%)
  starting transfers between devices  12.6 us (10%)
  other arithmetic  2.92 us (2%)
    pallas_call x1, Pallas kernels, shards(): pl.pallas_call(functools.partial(solve_kernel, scale), out_shape=(jax.Sha...  47.1 us
    ppermute x1, waiting for transfers between devices, sum_rows(): mine = keep + lax.ppermute(send, 'rows', pair)  13.9 us
    ppermute x3, waiting for transfers between devices, sum_rows(): total = total + lax.ppermute(part, 'rows', to(s))  12.9 us
    ppermute x1, waiting for transfers between devices, sum_rows(): other = lax.ppermute(gathered, 'rows', pair)  10.9 us
    ppermute x3, waiting for transfers between devices, sum_rows(): lax.ppermute(total, 'rows', to(s))  9.34 us
    ppermute x3, starting transfers between devices, sum_rows(): total = total + lax.ppermute(part, 'rows', to(s))  5.61 us
    ppermute x3, starting transfers between devices, sum_rows(): lax.ppermute(total, 'rows', to(s))  4.44 us
    pallas_call x1, Pallas kernels, shards(): pl.pallas_call(gram_diag_kernel, out_shape=jax.ShapeDtypeStruct((n_diag *...  3.19 us
  transfers between devices with their start and end apart: 10, of which 8 were waited for; matrix products, arithmetic and copies ran while one was open for 0% of the time, Pallas kernels for 3%

profile of v1, /device:TPU:0, one launch (start us, length us, event | category | flops | bytes accessed | tf_op | source)
XLA Modules:
  0.0 120.2 jit_solution(11303395578059209045)
XLA Ops:
  0.6 0.0 copy-start.3
  0.6 0.5 collective-permute-start
  1.2 3.2 %gram_diag.1 = f32[1280,128]{1,0:T(8,128)} custom-call(f32[256,512]{1,0:T(8,128)} %own_ref.1), custom_call_target="tpu_custom_call" | custom-call | flops 503316480 | bytes 524288 | tf_op jit(solution)/shard_map/gram_diag/pallas_call | solution.py:182
  4.3 0.0 collective-permute-done
  4.3 0.0 copy-done.3
  4.4 0.9 broadcast_select_fusion.4
  5.3 0.0 copy-start.2
  5.3 0.7 constant_dynamic-slice_fusion.3.second_ref
  6.0 3.0 %gram_cross.1 = f32[1024,128]{1,0:T(8,128)} custom-call(f32[256,512]{1,0:T(8,128)} %get-tuple-element.9.first_ref.e0_ref, f32[256,256]{1,0:T(8,128)} %constant_dynamic-slice_fusion.3.second_ref), custom_call_target="tpu_custom_call" | custom-call | tf_op jit(solution)/shard_map/gram_cross/pallas_call | solution.py:190
  9.0 0.0 copy-done.2
  9.0 0.0 copy-start.1
  9.0 1.3 %fusion = f32[1152,128]{1,0:T(8,128)S(1)} fusion(s32[]{:T(128)S(6)} %select_n.80, f32[1280,128]{1,0:T(8,128)S(1)} %copy-done.2, f32[1024,128]{1,0:T(8,128)} %gram_cross.1), kind=kLoop, calls=%fused_computation.5 | loop fusion | flops 147456 | bytes 1769476 | tf_op jit(solution)/shard_map/concatenate | solution.py:195
  10.3 1.5 %collective-permute-start.1 = (f32[1152,128]{1,0:T(8,128)S(1)}, f32[1152,128]{1,0:T(8,128)S(1)}, u32[]{:S(2)}, u32[]{:S(2)}) collective-permute-start(f32[1152,128]{1,0:T(8,128)S(1)} %fusion), channel_id=1, source_target_pairs={{0,4},{4,0},{8,12},{12,8},{16,20},{20,16},{24,28},{28,24},{1,5},{5... | collective-permute-start | bytes 1769480 | tf_op jit(solution)/shard_map/ppermute | solution.py:155
  11.8 13.9 %collective-permute-done.1 = f32[1152,128]{1,0:T(8,128)S(1)} collective-permute-done((f32[1152,128]{1,0:T(8,128)S(1)}, f32[1152,128]{1,0:T(8,128)S(1)}, u32[]{:S(2)}, u32[]{:S(2)}) %collective-permute-start.1) | collective-permute-done | bytes 589856 | tf_op jit(solution)/shard_map/ppermute | solution.py:155
  25.7 0.0 copy-done.1
  25.7 0.3 fusion.2
  26.1 3.0 %collective-permute-start.2 = (f32[288,128]{1,0:T(8,128)S(1)}, f32[288,128]{1,0:T(8,128)S(1)}, u32[]{:S(2)}, u32[]{:S(2)}) collective-permute-start(f32[288,128]{1,0:T(8,128)S(1)} %get-tuple-element.10), channel_id=1, source_target_pairs={{0,8},{4,12},{8,0},{12,4},{16,24},{20,28},{24,16},{28,20},{1,9},{5... | collective-permute-start | bytes 442376 | tf_op jit(solution)/shard_map/ppermute | solution.py:163
  29.1 2.5 %collective-permute-start.4 = (f32[288,128]{1,0:T(8,128)S(1)}, f32[288,128]{1,0:T(8,128)S(1)}, u32[]{:S(2)}, u32[]{:S(2)}) collective-permute-start(f32[288,128]{1,0:T(8,128)S(1)} %get-tuple-element.11), channel_id=1, source_target_pairs={{0,24},{4,28},{8,16},{12,20},{16,8},{20,12},{24,0},{28,4},{1,25},{... | collective-permute-start | bytes 442376 | tf_op jit(solution)/shard_map/ppermute | solution.py:163
  31.6 0.1 collective-permute-start.3
  31.7 1.3 %collective-permute-done.2 = f32[288,128]{1,0:T(8,128)S(1)} collective-permute-done((f32[288,128]{1,0:T(8,128)S(1)}, f32[288,128]{1,0:T(8,128)S(1)}, u32[]{:S(2)}, u32[]{:S(2)}) %collective-permute-start.2) | collective-permute-done | bytes 147488 | tf_op jit(solution)/shard_map/ppermute | solution.py:163
  33.1 6.6 %collective-permute-done.4 = f32[288,128]{1,0:T(8,128)S(1)} collective-permute-done((f32[288,128]{1,0:T(8,128)S(1)}, f32[288,128]{1,0:T(8,128)S(1)}, u32[]{:S(2)}, u32[]{:S(2)}) %collective-permute-start.4) | collective-permute-done | bytes 147488 | tf_op jit(solution)/shard_map/ppermute | solution.py:163
  39.6 5.0 %collective-permute-done.3 = f32[288,128]{1,0:T(8,128)S(1)} collective-permute-done((f32[288,128]{1,0:T(8,128)S(1)}, f32[288,128]{1,0:T(8,128)S(1)}, u32[]{:S(2)}, u32[]{:S(2)}) %collective-permute-start.3) | collective-permute-done | bytes 147488 | tf_op jit(solution)/shard_map/ppermute | solution.py:163
  44.7 0.1 collective-permute-start.5
  44.8 3.2 %collective-permute-start.6 = (f32[288,128]{1,0:T(8,128)S(1)}, f32[288,128]{1,0:T(8,128)S(1)}, u32[]{:S(2)}, u32[]{:S(2)}) collective-permute-start(f32[288,128]{1,0:T(8,128)S(1)} %get-tuple-element.3), channel_id=1, source_target_pairs={{0,16},{4,20},{8,24},{12,28},{16,0},{20,4},{24,8},{28,12},{1,17},{... | collective-permute-start | bytes 442376 | tf_op jit(solution)/shard_map/ppermute | solution.py:167
  48.0 1.2 collective-permute-start.7
  49.1 2.3 %collective-permute-done.5 = f32[288,128]{1,0:T(8,128)S(1)} collective-permute-done((f32[288,128]{1,0:T(8,128)S(1)}, f32[288,128]{1,0:T(8,128)S(1)}, u32[]{:S(2)}, u32[]{:S(2)}) %collective-permute-start.5) | collective-permute-done | bytes 147488 | tf_op jit(solution)/shard_map/ppermute | solution.py:167
  51.4 7.1 %collective-permute-done.6 = f32[288,128]{1,0:T(8,128)S(1)} collective-permute-done((f32[288,128]{1,0:T(8,128)S(1)}, f32[288,128]{1,0:T(8,128)S(1)}, u32[]{:S(2)}, u32[]{:S(2)}) %collective-permute-start.6) | collective-permute-done | bytes 147488 | tf_op jit(solution)/shard_map/ppermute | solution.py:167
  58.5 0.0 collective-permute-done.7
  58.6 0.4 collective-permute-start.8
  59.0 10.9 %collective-permute-done.8 = f32[1152,128]{1,0:T(8,128)S(1)} collective-permute-done((f32[1152,128]{1,0:T(8,128)S(1)}, f32[1152,128]{1,0:T(8,128)S(1)}, u32[]{:S(2)}, u32[]{:S(2)}) %collective-permute-start.8) | collective-permute-done | bytes 589856 | tf_op jit(solution)/shard_map/ppermute | solution.py:168
  69.9 0.1 broadcast_select_fusion.3
  70.0 0.1 pad_maximum_fusion
  70.0 0.0 copy-start
  70.1 0.1 collective-permute-start.9
  70.1 2.8 %collective-permute-done.9 = f32[2304,128]{1,0:T(8,128)S(1)} collective-permute-done((f32[2304,128]{1,0:T(8,128)S(1)}, f32[2304,128]{1,0:T(8,128)S(1)}, u32[]{:S(2)}, u32[]{:S(2)}) %collective-permute-start.9) | collective-permute-done | bytes 1179680 | tf_op jit(solution)/shard_map/ppermute | solution.py:196
  73.0 0.2 broadcast_select_fusion
  73.1 0.0 copy-done
  73.1 47.1 %cholesky_solve.1 = (f32[256,512]{1,0:T(8,128)}, f32[1024,512]{1,0:T(8,128)}) custom-call(s32[1]{0:T(128)} %bitcast.t_ref, f32[2304,128]{1,0:T(8,128)S(1)} %get-tuple-element.5.pay0_ref, f32[2304,128]{1,0:T(8,128)S(1)} %get-tuple-element.4.pay1_ref, f32[256,512]{1,0:T(8,128)S(1)} %copy-done, f32[256,512]{1,0:T(8,128)S(1)} %get-tuple-element.8.e1_ref), custom_call_target="tpu_custom_call" | custom-call | tf_op jit(solution)/shard_map/cholesky_solve/pallas_call | solution.py:201
  (6 shorter events, 0.2 us)
Async XLA Ops:
  0.6 3.7 %copy-start.3 = (f32[256,512]{1,0:T(8,128)S(1)}, f32[256,512]{1,0:T(8,128)}, u32[]{:S(2)}) copy-start(f32[256,512]{1,0:T(8,128)} %own_ref.1) | copy-start | bytes 1572868
  0.6 3.7 %collective-permute-start = (f32[256,512]{1,0:T(8,128)}, f32[256,512]{1,0:T(8,128)S(1)}, u32[]{:S(2)}, u32[]{:S(2)}) collective-permute-start(f32[256,512]{1,0:T(8,128)} %own_ref.1), channel_id=1, source_target_pairs={{0,2},{2,0},{1,3},{3,1},{4,6},{6,4},{5,7},{7,5},{8,10},{10,8},{9,1... | collective-permute-start | bytes 1572872 | tf_op jit(solution)/shard_map/ppermute | solution.py:181
  5.3 3.7 %copy-start.2 = (f32[1280,128]{1,0:T(8,128)S(1)}, f32[1280,128]{1,0:T(8,128)}, u32[]{:S(2)}) copy-start(f32[1280,128]{1,0:T(8,128)} %gram_diag.1) | copy-start | bytes 1966084
  9.0 16.8 %copy-start.1 = (f32[1024,128]{1,0:T(8,128)S(1)}, f32[1024,128]{1,0:T(8,128)}, u32[]{:S(2)}) copy-start(f32[1024,128]{1,0:T(8,128)} %gram_cross.1) | copy-start | bytes 1572868
  10.3 15.4 %collective-permute-start.1 = (f32[1152,128]{1,0:T(8,128)S(1)}, f32[1152,128]{1,0:T(8,128)S(1)}, u32[]{:S(2)}, u32[]{:S(2)}) collective-permute-start(f32[1152,128]{1,0:T(8,128)S(1)} %fusion), channel_id=1, source_target_pairs={{0,4},{4,0},{8,12},{12,8},{16,20},{20,16},{24,28},{28,24},{1,5},{5... | collective-permute-start | bytes 1769480 | tf_op jit(solution)/shard_map/ppermute | solution.py:155
  26.1 6.9 %collective-permute-start.2 = (f32[288,128]{1,0:T(8,128)S(1)}, f32[288,128]{1,0:T(8,128)S(1)}, u32[]{:S(2)}, u32[]{:S(2)}) collective-permute-start(f32[288,128]{1,0:T(8,128)S(1)} %get-tuple-element.10), channel_id=1, source_target_pairs={{0,8},{4,12},{8,0},{12,4},{16,24},{20,28},{24,16},{28,20},{1,9},{5... | collective-permute-start | bytes 442376 | tf_op jit(solution)/shard_map/ppermute | solution.py:163
  29.1 10.5 %collective-permute-start.4 = (f32[288,128]{1,0:T(8,128)S(1)}, f32[288,128]{1,0:T(8,128)S(1)}, u32[]{:S(2)}, u32[]{:S(2)}) collective-permute-start(f32[288,128]{1,0:T(8,128)S(1)} %get-tuple-element.11), channel_id=1, source_target_pairs={{0,24},{4,28},{8,16},{12,20},{16,8},{20,12},{24,0},{28,4},{1,25},{... | collective-permute-start | bytes 442376 | tf_op jit(solution)/shard_map/ppermute | solution.py:163
  31.6 13.0 %collective-permute-start.3 = (f32[288,128]{1,0:T(8,128)S(1)}, f32[288,128]{1,0:T(8,128)S(1)}, u32[]{:S(2)}, u32[]{:S(2)}) collective-permute-start(f32[288,128]{1,0:T(8,128)S(1)} %get-tuple-element.12), channel_id=1, source_target_pairs={{0,16},{4,20},{8,24},{12,28},{16,0},{20,4},{24,8},{28,12},{1,17},{... | collective-permute-start | bytes 442376 | tf_op jit(solution)/shard_map/ppermute | solution.py:163
  44.7 6.7 %collective-permute-start.5 = (f32[288,128]{1,0:T(8,128)S(1)}, f32[288,128]{1,0:T(8,128)S(1)}, u32[]{:S(2)}, u32[]{:S(2)}) collective-permute-start(f32[288,128]{1,0:T(8,128)S(1)} %get-tuple-element.3), channel_id=1, source_target_pairs={{0,8},{4,12},{8,0},{12,4},{16,24},{20,28},{24,16},{28,20},{1,9},{5... | collective-permute-start | bytes 442376 | tf_op jit(solution)/shard_map/ppermute | solution.py:167
  44.8 13.7 %collective-permute-start.6 = (f32[288,128]{1,0:T(8,128)S(1)}, f32[288,128]{1,0:T(8,128)S(1)}, u32[]{:S(2)}, u32[]{:S(2)}) collective-permute-start(f32[288,128]{1,0:T(8,128)S(1)} %get-tuple-element.3), channel_id=1, source_target_pairs={{0,16},{4,20},{8,24},{12,28},{16,0},{20,4},{24,8},{28,12},{1,17},{... | collective-permute-start | bytes 442376 | tf_op jit(solution)/shard_map/ppermute | solution.py:167
  48.0 10.6 %collective-permute-start.7 = (f32[288,128]{1,0:T(8,128)S(1)}, f32[288,128]{1,0:T(8,128)S(1)}, u32[]{:S(2)}, u32[]{:S(2)}) collective-permute-start(f32[288,128]{1,0:T(8,128)S(1)} %get-tuple-element.3), channel_id=1, source_target_pairs={{0,24},{4,28},{8,16},{12,20},{16,8},{20,12},{24,0},{28,4},{1,25},{... | collective-permute-start | bytes 442376 | tf_op jit(solution)/shard_map/ppermute | solution.py:167
  58.6 11.3 %collective-permute-start.8 = (f32[1152,128]{1,0:T(8,128)S(1)}, f32[1152,128]{1,0:T(8,128)S(1)}, u32[]{:S(2)}, u32[]{:S(2)}) collective-permute-start(f32[1152,128]{1,0:T(8,128)S(1)} %constant_dynamic-update-slice_fusion), channel_id=1, source_target_pairs={{0,4},{4,0},{8,12},{12,8},{16,20},{20,16},{24,28},{28,24},{1,5},{5... | collective-permute-start | bytes 1769480 | tf_op jit(solution)/shard_map/ppermute | solution.py:168
  70.0 3.1 %copy-start = (f32[256,512]{1,0:T(8,128)S(1)}, f32[256,512]{1,0:T(8,128)}, u32[]{:S(2)}) copy-start(f32[256,512]{1,0:T(8,128)} %get-tuple-element.9.first_ref.e0_ref) | copy-start | bytes 1572868
  70.1 2.9 %collective-permute-start.9 = (f32[2304,128]{1,0:T(8,128)S(1)}, f32[2304,128]{1,0:T(8,128)S(1)}, u32[]{:S(2)}, u32[]{:S(2)}) collective-permute-start(f32[2304,128]{1,0:T(8,128)S(1)} %pad_maximum_fusion), channel_id=1, source_target_pairs={{0,2},{2,0},{1,3},{3,1},{4,6},{6,4},{5,7},{7,5},{8,10},{10,8},{9,1... | collective-permute-start | bytes 3538952 | tf_op jit(solution)/shard_map/ppermute | solution.py:196

commit v2 on v0

v2 whole, which is shorter than its diff:
```python
import functools

import jax
import jax.numpy as jnp
from jax import lax
from jax.experimental import pallas as pl
from jax.experimental.pallas import tpu as pltpu
from jax.sharding import PartitionSpec as P

F32 = jnp.float32
BF16 = jnp.bfloat16
NB = 128
SUB = 8
PANEL = 4


def split(x):
    high = x.astype(BF16)
    rest = x - high.astype(F32)
    mid = rest.astype(BF16)
    return high, mid, (rest - mid.astype(F32)).astype(BF16)


def left_parts(x):
    h, m, l = split(x)
    return jnp.concatenate([h, h, m, m, h, l], axis=1)


def right_parts(x):
    h, m, l = split(x)
    return jnp.concatenate([h, m, h, m, l, h], axis=0)


def product(left, right):
    return jnp.dot(left, right, preferred_element_type=F32)


def row_of(x, k):
    return jnp.broadcast_to(x[k : k + 1, :], x.shape)


def lane_of(x, j):
    return jnp.broadcast_to(x[:, j : j + 1], x.shape)


def total_of(terms):
    terms = list(terms)
    while len(terms) > 1:
        terms = [terms[i] + terms[i + 1] if i + 1 < len(terms) else terms[i] for i in range(0, len(terms), 2)]
    return terms[0]


def factor_block(rows, put_upper, put_inverse):
    lane = lax.broadcasted_iota(jnp.int32, (SUB, NB), 1)
    sub = lax.broadcasted_iota(jnp.int32, (SUB, NB), 0)
    mine = [sub == k for k in range(SUB)]
    zero = jnp.zeros((SUB, NB), F32)
    rows = list(rows)
    count = len(rows)
    for p in range(0, count, PANEL):
        for g in range(p, p + PANEL, 2):
            b = SUB * g
            col0 = [lane_of(rows[g], b + k) for k in range(SUB)]
            col1 = [lane_of(rows[g + 1], b + k) for k in range(2 * SUB)]
            others = list(range(g + 2, p + PANEL)) + list(range(p, g))
            factors = {h: [lane_of(rows[h], b + k) for k in range(2 * SUB)] for h in others}
            group = (lane >= b) & (lane < b + 2 * SUB)
            a0, a1 = rows[g], rows[g + 1]
            w0 = jnp.where(group, jnp.where(lane - b == sub, F32(1), F32(0)), a0)
            w1 = jnp.where(group, jnp.where(lane - b - SUB == sub, F32(1), F32(0)), a1)

            pivots, upper, inverse = zero, a0, w0
            for k in range(SUB):
                pivot = row_of(col0[k], k)
                recip = 1.0 / pivot
                c0 = jnp.where(mine[k], F32(0), col0[k]) * recip
                c1 = col1[k] * recip
                pivots = jnp.where(mine[k], pivot, pivots)
                upper = jnp.where(mine[k], a0, upper)
                inverse = jnp.where(mine[k], w0, inverse)
                for m in range(k + 1, SUB):
                    s = row_of(col0[m], k)
                    col0[m] = col0[m] - c0 * s
                    col1[m] = col1[m] - c1 * s
                for m in range(SUB):
                    col1[SUB + m] = col1[SUB + m] - c1 * row_of(col1[k], m)
                a, w = row_of(a0, k), row_of(w0, k)
                a0, a1, w0, w1 = a0 - c0 * a, a1 - c1 * a, w0 - c0 * w, w1 - c1 * w
            recips, roots = 1.0 / pivots, lax.rsqrt(pivots)
            put_upper(g, jnp.where(lane >= sub + b, upper * roots, F32(0)))
            put_inverse(g, jnp.where(lane <= sub + b, inverse * roots, F32(0)))
            a0, w0 = a0 * recips, w0 * recips
            above = [lane_of(a0, b + SUB + k) for k in range(SUB)]

            pivots, upper, inverse = zero, a1, w1
            for k in range(SUB):
                pivot = row_of(col1[SUB + k], k)
                recip = 1.0 / pivot
                c1 = jnp.where(mine[k], F32(0), col1[SUB + k]) * recip
                pivots = jnp.where(mine[k], pivot, pivots)
                upper = jnp.where(mine[k], a1, upper)
                inverse = jnp.where(mine[k], w1, inverse)
                for m in range(k + 1, SUB):
                    col1[SUB + m] = col1[SUB + m] - c1 * row_of(col1[SUB + m], k)
                a1, w1 = a1 - c1 * row_of(a1, k), w1 - c1 * row_of(w1, k)
            recips, roots = 1.0 / pivots, lax.rsqrt(pivots)
            put_upper(g + 1, jnp.where(lane >= sub + b + SUB, upper * roots, F32(0)))
            put_inverse(g + 1, jnp.where(lane <= sub + b + SUB, inverse * roots, F32(0)))

            left = lane < b + 2 * SUB
            solved1 = jnp.where(left, w1, a1) * recips
            solved0 = jnp.where(left, w0, a0)
            lower_rows = [row_of(solved1, k) for k in range(SUB)]
            solved0 = solved0 - total_of(above[k] * lower_rows[k] for k in range(SUB))
            solved = [row_of(solved0, k) for k in range(SUB)] + lower_rows
            rows[g], rows[g + 1] = solved0, solved1
            for h in others:
                rows[h] = jnp.where(group, F32(0), rows[h]) - total_of(f * s for f, s in zip(factors[h], solved))
        end = p + PANEL
        if end < count:
            panel = jnp.concatenate([rows[h] if p <= h < end else zero for h in range(count)], axis=0)
            below = jnp.concatenate(rows[end:], axis=0)
            lanes = lax.broadcasted_iota(jnp.int32, below.shape, 1)
            in_panel = (lanes >= SUB * p) & (lanes < SUB * end)
            below = jnp.where(in_panel, F32(0), below) - product(left_parts(below), right_parts(panel))
            for i in range(end, count):
                rows[i] = below[SUB * (i - end) : SUB * (i - end + 1), :]


def pairs(n):
    return [(i, j) for i in range(n) for j in range(i, n)]


def at(i, size=NB):
    return slice(i * size, (i + 1) * size)


def gram_diag_kernel(own_ref, out_ref):
    n = own_ref.shape[1] // NB
    right = right_parts(own_ref[...])
    done = 0
    for i in range(n):
        row = product(left_parts(own_ref[:, at(i)].T), right[:, i * NB :])
        for j in range(n - i):
            out_ref[at(done), :] = row[:, at(j)]
            done += 1


def gram_cross_kernel(s_ref, diag_ref, own_ref, other_ref, keep_ref, send_ref, first_ref, second_ref, all_ref):
    width = own_ref.shape[1]
    half = width // 2

    @pl.when(s_ref[0] == 0)
    def _():
        first_ref[...] = own_ref[...]
        second_ref[...] = other_ref[:, :half]

    @pl.when(s_ref[0] != 0)
    def _():
        first_ref[...] = other_ref[...]
        second_ref[...] = own_ref[:, half:]

    done = diag_ref.shape[0] // NB
    all_ref[: done * NB, :] = diag_ref[...]
    right = right_parts(second_ref[...])
    for i in range(width // NB):
        row = product(left_parts(first_ref[:, at(i)].T), right)
        for j in range(half // NB):
            all_ref[at(done), :] = row[:, at(j)]
            done += 1
    size = keep_ref.shape[0]
    keep_ref[...] = all_ref[pl.ds(pl.multiple_of(s_ref[1] * size, SUB), size), :]
    send_ref[...] = all_ref[pl.ds(pl.multiple_of((1 - s_ref[1]) * size, SUB), size), :]


def solve_kernel(
    scale, s_ref, mine_a, mine_b, sib_a, sib_b, own_ref, other_ref, basis_ref, tri_ref, pay_ref, a_ref, e_ref, inv_ref
):
    width = own_ref.shape[1]
    half = width // NB
    n = 2 * half
    size = mine_a.shape[0]
    t = s_ref[0]

    def put(core, bit, ref):
        pay_ref[core, pl.ds(pl.multiple_of(bit * size, SUB), size), :] = ref[...]

    put(t, s_ref[1], mine_a)
    put(t, 1 - s_ref[1], mine_b)
    put(1 - t, s_ref[2], sib_a)
    put(1 - t, 1 - s_ref[2], sib_b)
    e_ref[:, pl.ds(pl.multiple_of(t * width, NB), width)] = own_ref[...]
    e_ref[:, pl.ds(pl.multiple_of((1 - t) * width, NB), width)] = other_ref[...]

    where = {}
    for number, (i, j) in enumerate(pairs(half)):
        where[i, j] = (0, number)
        where[half + i, half + j] = (1, number)
    number = len(pairs(half))
    for i in range(half):
        for j in range(half // 2):
            where[i, half + j] = (0, number)
            where[i, half + half // 2 + j] = (1, number)
            number += 1

    def gram(i, j):
        core, number = where[i, j]
        return pay_ref[core, at(number), :]

    for k in range(n):
        here = at(k)
        source = gram(k, k) if k == 0 else a_ref[here, here]
        rows = [source[at(h, SUB), :] for h in range(NB // SUB)]

        def put_upper(g, v):
            a_ref[k * NB + SUB * g : k * NB + SUB * (g + 1), here] = v

        def put_inverse(g, v):
            inv_ref[at(g, SUB), :] = v

        factor_block(rows, put_upper, put_inverse)
        if k:
            a_ref[here, : k * NB] = jnp.zeros((NB, k * NB), F32)
        inverse = inv_ref[...]
        inverse_left = left_parts(inverse)
        solved = product(left_parts(e_ref[:, here]), right_parts(inverse.T))
        if k + 1 < n:
            rest = slice((k + 1) * NB, n * NB)
            uppers, lowers, rights = {}, {}, {}
            for j in range(k + 1, n):
                uppers[j] = product(inverse_left, right_parts(gram(k, j) if k == 0 else a_ref[here, at(j)]))
                lowers[j] = left_parts(uppers[j].T)
                rights[j] = right_parts(uppers[j])
                a_ref[here, at(j)] = uppers[j]
            for i in range(k + 1, n):
                right = jnp.concatenate([rights[j] for j in range(i, n)], axis=1)
                update = product(lowers[i], right)
                for j in range(i, n):
                    old = gram(i, j) if k == 0 else a_ref[at(i), at(j)]
                    a_ref[at(i), at(j)] = old - update[:, at(j - i)]
            e_ref[:, rest] -= product(left_parts(solved), jnp.concatenate([rights[j] for j in range(k + 1, n)], axis=1))
        e_ref[:, here] = solved * scale
        tri_ref[here, :] = a_ref[here, pl.ds(pl.multiple_of(t * width, NB), width)] * (1.0 / scale)

    basis_ref[...] = e_ref[:, pl.ds(pl.multiple_of(t * width, NB), width)]


def shards(n_rows, effects):
    rows, width = effects.shape
    cols = 2 * width
    half = width // NB
    n_diag, n_cross = half * (half + 1) // 2, half * half // 2
    size = (n_diag + n_cross) * NB // 2
    t = lax.axis_index("tensor")
    me = lax.axis_index("rows")
    swap = [(0, 1), (1, 0)]

    steps = n_rows.bit_length() - 1
    masks = [[1 << j for j in range(steps)] for _ in range(2)]
    if steps > 1:
        masks[1][0], masks[1][1] = masks[1][1], masks[1][0]

    def exchange(x, j):
        perm = [(2 * r + c, 2 * (r ^ masks[c][j]) + c) for r in range(n_rows) for c in range(2)]
        return lax.ppermute(x, ("rows", "tensor"), perm)

    def bit(j, core):
        return jnp.where(core == 0, (me // masks[0][j]) % 2, (me // masks[1][j]) % 2)

    vmem = pl.BlockSpec(memory_space=pltpu.VMEM)
    smem = pl.BlockSpec(memory_space=pltpu.SMEM)
    params = pltpu.CompilerParams(vmem_limit_bytes=48 * 2**20)
    scalars = jnp.stack([t, bit(0, t), bit(0, 1 - t)]).astype(jnp.int32)

    other = lax.ppermute(effects, "tensor", swap)
    diag = pl.pallas_call(
        gram_diag_kernel,
        out_shape=jax.ShapeDtypeStruct((n_diag * NB, NB), F32),
        cost_estimate=pl.CostEstimate(flops=12 * rows * n_diag * NB * NB, bytes_accessed=4 * rows * width, transcendentals=0),
        compiler_params=params,
        name="gram_diag",
    )(effects)
    part = jax.ShapeDtypeStruct((size, NB), F32)
    keep, send = pl.pallas_call(
        gram_cross_kernel,
        out_shape=(part, part),
        in_specs=[smem, vmem, vmem, vmem],
        out_specs=(vmem, vmem),
        scratch_shapes=[pltpu.VMEM((rows, width), F32), pltpu.VMEM((rows, width // 2), F32), pltpu.VMEM((2 * size, NB), F32)],
        compiler_params=params,
        name="gram_cross",
    )(scalars, diag, effects, other)

    total = keep + exchange(send, 0)
    for j in range(1, steps):
        piece = total.shape[0] // 2
        v = bit(j, t)
        sent = lax.dynamic_slice_in_dim(total, (1 - v) * piece, piece)
        total = lax.dynamic_slice_in_dim(total, v * piece, piece) + exchange(sent, j)
    for j in range(steps - 1, 0, -1):
        got = exchange(total, j)
        v = bit(j, t)
        total = jnp.concatenate([jnp.where(v == 0, total, got), jnp.where(v == 0, got, total)])
    mine_b = exchange(total, 0)
    sib_a = lax.ppermute(total, "tensor", swap)
    sib_b = lax.ppermute(mine_b, "tensor", swap)

    scale = float(rows * n_rows) ** 0.5
    return pl.pallas_call(
        functools.partial(solve_kernel, scale),
        out_shape=(jax.ShapeDtypeStruct((rows, width), F32), jax.ShapeDtypeStruct((cols, width), F32)),
        in_specs=[smem] + [vmem] * 6,
        out_specs=(vmem, vmem),
        scratch_shapes=[
            pltpu.VMEM((2, 2 * size, NB), F32),
            pltpu.VMEM((cols, cols), F32),
            pltpu.VMEM((rows, cols), F32),
            pltpu.VMEM((NB, NB), F32),
        ],
        compiler_params=params,
        name="cholesky_solve",
    )(scalars, total, mine_b, sib_a, sib_b, effects, other)


def solution(mesh):
    spec = P(("groups", "rows"), "tensor")
    return jax.shard_map(
        functools.partial(shards, mesh.shape["rows"]),
        mesh=mesh,
        in_specs=(spec,),
        out_specs=(spec, P("groups", "tensor")),
        check_vma=False,
    )
```

time: 501 us -> 91.1 us (0.18)
  other arithmetic: 262 us -> 0.37 us
  waiting for transfers between devices: 130 us -> 43.9 us
  matrix products: 47.3 us -> 0 us
  local copies, waits for them, and re-layouts: 36.6 us -> 1.21 us
  Pallas kernels: 0 us -> 34.2 us
  between operations: 19.8 us -> 0.71 us
  starting transfers between devices: 0.12 us -> 10.4 us
    another operation x33 -> x1, other arithmetic: 256 us -> 0.08 us  [shards(): scalars = jnp.stack([t, bit(0, t), bit(0, 1 - t)]).astype(jnp.int32)]
    psum x1 -> x0, waiting for transfers between devices: 103 us -> none  [shards(): summed = lax.psum(own_block, 'rows')]
    ppermute x0 -> x9, waiting for transfers between devices: none -> 43.9 us  [the longest x6 41.9 us: exchange(): return lax.ppermute(x, ('rows', 'tensor'), perm)]
    another operation x29 -> x0, matrix products: 39.3 us -> none  [the longest x14 23.1 us: shards(): lower = jnp.linalg.cholesky(gram)]
    pallas_call x0 -> x3, Pallas kernels: none -> 34.2 us  [the longest x1 32 us: shards(): pl.pallas_call(functools.partial(solve_kernel, scale), out_shape=(jax.Sha...]
    all_gather x2 -> x0, waiting for transfers between devices: 26.6 us -> none  [the longest x1 13.4 us: shards(): whole = lax.all_gather(effects, 'tensor', axis=1, tiled=True)]
    another operation x37 -> x0, local copies, waits for them, and re-layouts: 25.3 us -> none
    ppermute x0 -> x9, starting transfers between devices: none -> 10.4 us  [the longest x6 9.91 us: exchange(): return lax.ppermute(x, ('rows', 'tensor'), perm)]
  transfers between devices with their start and end apart: 3 -> 9, of which waited for: 3 -> 7; matrix products, arithmetic and copies ran while one was open for 0% -> 0% of each run, Pallas kernels for 0% -> 1%
where the time goes in v2:
time: 91.1 us; the launch traced here: 90.9 us
  waiting for transfers between devices  43.9 us (48%)
  Pallas kernels  34.2 us (38%)
  starting transfers between devices  10.4 us (11%)
  local copies, waits for them, and re-layouts  1.21 us (1%)
    ppermute x6, waiting for transfers between devices, exchange(): return lax.ppermute(x, ('rows', 'tensor'), perm)  41.9 us
    pallas_call x1, Pallas kernels, shards(): pl.pallas_call(functools.partial(solve_kernel, scale), out_shape=(jax.Sha...  32 us
    ppermute x6, starting transfers between devices, exchange(): return lax.ppermute(x, ('rows', 'tensor'), perm)  9.91 us
    ppermute x1, waiting for transfers between devices, shards(): sib_b = lax.ppermute(mine_b, 'tensor', swap)  2 us
  transfers between devices with their start and end apart: 9, of which 7 were waited for; matrix products, arithmetic and copies ran while one was open for 0% of the time, Pallas kernels for 1%

profile of v2, /device:TPU:0, one launch (start us, length us, event | category | flops | bytes accessed | tf_op | source)
XLA Modules:
  0.0 90.9 jit_solution(3418937039281245545)
XLA Ops:
  0.6 0.5 collective-permute-start
  1.1 0.0 copy-start
  1.1 1.0 %copy-done = f32[256,512]{1,0:T(8,128)S(1)} copy-done((f32[256,512]{1,0:T(8,128)S(1)}, f32[256,512]{1,0:T(8,128)}, u32[]{:S(2)}) %copy-start) | copy-done | bytes 524312
  2.2 0.0 copy-start.1
  2.2 0.8 gram_diag.1.diag_ref
  3.0 0.1 pad_add_fusion.s_ref
  3.1 0.0 collective-permute-done.other_ref
  3.1 0.1 copy-done.1
  3.2 1.3 %gram_cross.1 = (f32[1152,128]{1,0:T(8,128)S(1)}, f32[1152,128]{1,0:T(8,128)S(1)}) custom-call(s32[3]{0:T(128)S(1)} %pad_add_fusion.s_ref, f32[1280,128]{1,0:T(8,128)S(1)} %gram_diag.1.diag_ref, f32[256,512]{1,0:T(8,128)S(1)} %copy-done.1, f32[256,512]{1,0:T(8,128)S(1)} %collective-permute-done.other_ref), custom_call_target="tpu_custom_call" | custom-call | tf_op jit(solution)/shard_map/gram_cross/pallas_call | solution.py:284
  4.6 2.6 %collective-permute-start.1 = (f32[1152,128]{1,0:T(8,128)S(1)}, f32[1152,128]{1,0:T(8,128)S(1)}, u32[]{:S(2)}, u32[]{:S(2)}) collective-permute-start(f32[1152,128]{1,0:T(8,128)S(1)} %get-tuple-element.5), channel_id=1, source_target_pairs={{0,4},{2,10},{4,0},{6,14},{8,12},{10,2},{12,8},{14,6},{16,20},{18,... | collective-permute-start | bytes 1769480 | tf_op jit(solution)/shard_map/ppermute | solution.py:265
  7.2 7.9 %collective-permute-done.1 = f32[1152,128]{1,0:T(8,128)S(1)} collective-permute-done((f32[1152,128]{1,0:T(8,128)S(1)}, f32[1152,128]{1,0:T(8,128)S(1)}, u32[]{:S(2)}, u32[]{:S(2)}) %collective-permute-start.1) | collective-permute-done | bytes 589856 | tf_op jit(solution)/shard_map/ppermute | solution.py:265
  15.0 0.1 add.46
  15.2 2.2 %collective-permute-start.2 = (f32[576,128]{1,0:T(8,128)S(1)}, f32[576,128]{1,0:T(8,128)S(1)}, u32[]{:S(2)}, u32[]{:S(2)}) collective-permute-start(f32[576,128]{1,0:T(8,128)S(1)} %constant_dynamic-slice_fusion.1), channel_id=1, source_target_pairs={{0,8},{2,6},{4,12},{6,2},{8,0},{10,14},{12,4},{14,10},{16,24},{18,... | collective-permute-start | bytes 884744 | tf_op jit(solution)/shard_map/ppermute | solution.py:265
  17.3 4.7 %collective-permute-done.2 = f32[576,128]{1,0:T(8,128)S(1)} collective-permute-done((f32[576,128]{1,0:T(8,128)S(1)}, f32[576,128]{1,0:T(8,128)S(1)}, u32[]{:S(2)}, u32[]{:S(2)}) %collective-permute-start.2) | collective-permute-done | bytes 294944 | tf_op jit(solution)/shard_map/ppermute | solution.py:265
  22.1 3.1 %collective-permute-start.3 = (f32[288,128]{1,0:T(8,128)S(1)}, f32[288,128]{1,0:T(8,128)S(1)}, u32[]{:S(2)}, u32[]{:S(2)}) collective-permute-start(f32[288,128]{1,0:T(8,128)S(1)} %constant_dynamic-slice_fusion), channel_id=1, source_target_pairs={{0,16},{2,18},{4,20},{6,22},{8,24},{10,26},{12,28},{14,30},{16,0},... | collective-permute-start | bytes 442376 | tf_op jit(solution)/shard_map/ppermute | solution.py:265
  25.2 5.9 %collective-permute-done.3 = f32[288,128]{1,0:T(8,128)S(1)} collective-permute-done((f32[288,128]{1,0:T(8,128)S(1)}, f32[288,128]{1,0:T(8,128)S(1)}, u32[]{:S(2)}, u32[]{:S(2)}) %collective-permute-start.3) | collective-permute-done | bytes 147488 | tf_op jit(solution)/shard_map/ppermute | solution.py:265
  31.1 0.3 collective-permute-start.4
  31.4 8.5 %collective-permute-done.4 = f32[288,128]{1,0:T(8,128)S(1)} collective-permute-done((f32[288,128]{1,0:T(8,128)S(1)}, f32[288,128]{1,0:T(8,128)S(1)}, u32[]{:S(2)}, u32[]{:S(2)}) %collective-permute-start.4) | collective-permute-done | bytes 147488 | tf_op jit(solution)/shard_map/ppermute | solution.py:265
  40.0 0.1 collective-permute-start.5
  40.0 6.7 %collective-permute-done.5 = f32[576,128]{1,0:T(8,128)S(1)} collective-permute-done((f32[576,128]{1,0:T(8,128)S(1)}, f32[576,128]{1,0:T(8,128)S(1)}, u32[]{:S(2)}, u32[]{:S(2)}) %collective-permute-start.5) | collective-permute-done | bytes 294944 | tf_op jit(solution)/shard_map/ppermute | solution.py:265
  46.7 0.1 broadcast_select_fusion.1
  46.9 1.7 %collective-permute-start.6 = (f32[1152,128]{1,0:T(8,128)S(1)}, f32[1152,128]{1,0:T(8,128)S(1)}, u32[]{:S(2)}, u32[]{:S(2)}) collective-permute-start(f32[1152,128]{1,0:T(8,128)S(1)} %pad_maximum_fusion.mine_a), channel_id=1, source_target_pairs={{0,4},{2,10},{4,0},{6,14},{8,12},{10,2},{12,8},{14,6},{16,20},{18,... | collective-permute-start | bytes 1769480 | tf_op jit(solution)/shard_map/ppermute | solution.py:265
  48.5 0.0 collective-permute-start.7
  48.5 8.3 %collective-permute-done.6.mine_b = f32[1152,128]{1,0:T(8,128)S(1)} collective-permute-done((f32[1152,128]{1,0:T(8,128)S(1)}, f32[1152,128]{1,0:T(8,128)S(1)}, u32[]{:S(2)}, u32[]{:S(2)}) %collective-permute-start.6) | collective-permute-done | bytes 589856 | tf_op jit(solution)/shard_map/ppermute | solution.py:265
  56.8 0.0 collective-permute-start.8
  56.8 0.0 collective-permute-done.7.sib_a
  56.8 2.0 %collective-permute-done.8.sib_b = f32[1152,128]{1,0:T(8,128)S(1)} collective-permute-done((f32[1152,128]{1,0:T(8,128)S(1)}, f32[1152,128]{1,0:T(8,128)S(1)}, u32[]{:S(2)}, u32[]{:S(2)}) %collective-permute-start.8) | collective-permute-done | bytes 589856 | tf_op jit(solution)/shard_map/ppermute | solution.py:306
  58.8 32.0 %cholesky_solve.1 = (f32[256,512]{1,0:T(8,128)}, f32[1024,512]{1,0:T(8,128)}) custom-call(s32[3]{0:T(128)S(1)} %pad_add_fusion.s_ref, f32[1152,128]{1,0:T(8,128)S(1)} %pad_maximum_fusion.mine_a, f32[1152,128]{1,0:T(8,128)S(1)} %collective-permute-done.6.mine_b, f32[1152,128]{1,0:T(8,128)S(1)} %collective-permute-done.7.sib_a, ...), custom_call_target="tpu_custom_call" | custom-call | tf_op jit(solution)/shard_map/cholesky_solve/pallas_call | solution.py:309
  (7 shorter events, 0.2 us)
Async XLA Ops:
  0.6 2.5 %collective-permute-start = (f32[256,512]{1,0:T(8,128)}, f32[256,512]{1,0:T(8,128)S(1)}, u32[]{:S(2)}, u32[]{:S(2)}) collective-permute-start(f32[256,512]{1,0:T(8,128)} %own_ref.5), channel_id=1, source_target_pairs={{0,2},{2,0},{1,3},{3,1},{4,6},{6,4},{5,7},{7,5},{8,10},{10,8},{9,1... | collective-permute-start | bytes 1572872 | tf_op jit(solution)/shard_map/ppermute | solution.py:275
  1.1 1.0 %copy-start = (f32[256,512]{1,0:T(8,128)S(1)}, f32[256,512]{1,0:T(8,128)}, u32[]{:S(2)}) copy-start(f32[256,512]{1,0:T(8,128)} %own_ref.5) | copy-start | bytes 1572868
  2.2 1.0 %copy-start.1 = (f32[256,512]{1,0:T(8,128)S(1)}, f32[256,512]{1,0:T(8,128)}, u32[]{:S(2)}) copy-start(f32[256,512]{1,0:T(8,128)} %own_ref.5) | copy-start | bytes 1572868
  4.6 10.5 %collective-permute-start.1 = (f32[1152,128]{1,0:T(8,128)S(1)}, f32[1152,128]{1,0:T(8,128)S(1)}, u32[]{:S(2)}, u32[]{:S(2)}) collective-permute-start(f32[1152,128]{1,0:T(8,128)S(1)} %get-tuple-element.5), channel_id=1, source_target_pairs={{0,4},{2,10},{4,0},{6,14},{8,12},{10,2},{12,8},{14,6},{16,20},{18,... | collective-permute-start | bytes 1769480 | tf_op jit(solution)/shard_map/ppermute | solution.py:265
  15.2 6.9 %collective-permute-start.2 = (f32[576,128]{1,0:T(8,128)S(1)}, f32[576,128]{1,0:T(8,128)S(1)}, u32[]{:S(2)}, u32[]{:S(2)}) collective-permute-start(f32[576,128]{1,0:T(8,128)S(1)} %constant_dynamic-slice_fusion.1), channel_id=1, source_target_pairs={{0,8},{2,6},{4,12},{6,2},{8,0},{10,14},{12,4},{14,10},{16,24},{18,... | collective-permute-start | bytes 884744 | tf_op jit(solution)/shard_map/ppermute | solution.py:265
  22.1 9.0 %collective-permute-start.3 = (f32[288,128]{1,0:T(8,128)S(1)}, f32[288,128]{1,0:T(8,128)S(1)}, u32[]{:S(2)}, u32[]{:S(2)}) collective-permute-start(f32[288,128]{1,0:T(8,128)S(1)} %constant_dynamic-slice_fusion), channel_id=1, source_target_pairs={{0,16},{2,18},{4,20},{6,22},{8,24},{10,26},{12,28},{14,30},{16,0},... | collective-permute-start | bytes 442376 | tf_op jit(solution)/shard_map/ppermute | solution.py:265
  31.1 8.8 %collective-permute-start.4 = (f32[288,128]{1,0:T(8,128)S(1)}, f32[288,128]{1,0:T(8,128)S(1)}, u32[]{:S(2)}, u32[]{:S(2)}) collective-permute-start(f32[288,128]{1,0:T(8,128)S(1)} %dynamic-slice_add_fusion.1), channel_id=1, source_target_pairs={{0,16},{2,18},{4,20},{6,22},{8,24},{10,26},{12,28},{14,30},{16,0},... | collective-permute-start | bytes 442376 | tf_op jit(solution)/shard_map/ppermute | solution.py:265
  40.0 6.8 %collective-permute-start.5 = (f32[576,128]{1,0:T(8,128)S(1)}, f32[576,128]{1,0:T(8,128)S(1)}, u32[]{:S(2)}, u32[]{:S(2)}) collective-permute-start(f32[576,128]{1,0:T(8,128)S(1)} %pad_maximum_fusion.1), channel_id=1, source_target_pairs={{0,8},{2,6},{4,12},{6,2},{8,0},{10,14},{12,4},{14,10},{16,24},{18,... | collective-permute-start | bytes 884744 | tf_op jit(solution)/shard_map/ppermute | solution.py:265
  46.9 9.9 %collective-permute-start.6 = (f32[1152,128]{1,0:T(8,128)S(1)}, f32[1152,128]{1,0:T(8,128)S(1)}, u32[]{:S(2)}, u32[]{:S(2)}) collective-permute-start(f32[1152,128]{1,0:T(8,128)S(1)} %pad_maximum_fusion.mine_a), channel_id=1, source_target_pairs={{0,4},{2,10},{4,0},{6,14},{8,12},{10,2},{12,8},{14,6},{16,20},{18,... | collective-permute-start | bytes 1769480 | tf_op jit(solution)/shard_map/ppermute | solution.py:265
  48.5 8.3 %collective-permute-start.7 = (f32[1152,128]{1,0:T(8,128)S(1)}, f32[1152,128]{1,0:T(8,128)S(1)}, u32[]{:S(2)}, u32[]{:S(2)}) collective-permute-start(f32[1152,128]{1,0:T(8,128)S(1)} %pad_maximum_fusion.mine_a), channel_id=1, source_target_pairs={{0,2},{2,0},{1,3},{3,1},{4,6},{6,4},{5,7},{7,5},{8,10},{10,8},{9,1... | collective-permute-start | bytes 1769480 | tf_op jit(solution)/shard_map/ppermute | solution.py:305
  56.8 2.0 %collective-permute-start.8 = (f32[1152,128]{1,0:T(8,128)S(1)}, f32[1152,128]{1,0:T(8,128)S(1)}, u32[]{:S(2)}, u32[]{:S(2)}) collective-permute-start(f32[1152,128]{1,0:T(8,128)S(1)} %collective-permute-done.6.mine_b), channel_id=1, source_target_pairs={{0,2},{2,0},{1,3},{3,1},{4,6},{6,4},{5,7},{7,5},{8,10},{10,8},{9,1... | collective-permute-start | bytes 1769480 | tf_op jit(solution)/shard_map/ppermute | solution.py:306

commit v3 on v2

v3 whole, which is shorter than its diff:
```python
import functools

import jax
import jax.numpy as jnp
from jax import lax
from jax.experimental import pallas as pl
from jax.experimental.pallas import tpu as pltpu
from jax.sharding import PartitionSpec as P

F32 = jnp.float32
BF16 = jnp.bfloat16
NB = 128
SUB = 8


def split(x):
    high = x.astype(BF16)
    rest = x - high.astype(F32)
    mid = rest.astype(BF16)
    return high, mid, (rest - mid.astype(F32)).astype(BF16)


def left_parts(x):
    h, m, l = split(x)
    return jnp.concatenate([h, h, m, m, h, l], axis=1)


def right_parts(x):
    h, m, l = split(x)
    return jnp.concatenate([h, m, h, m, l, h], axis=0)


def product(left, right):
    return jnp.dot(left, right, preferred_element_type=F32)


def row_of(x, k):
    return jnp.broadcast_to(x[k : k + 1, :], x.shape)


def lane_of(x, j):
    return jnp.broadcast_to(x[:, j : j + 1], x.shape)


def total_of(terms):
    terms = list(terms)
    while len(terms) > 1:
        terms = [terms[i] + terms[i + 1] if i + 1 < len(terms) else terms[i] for i in range(0, len(terms), 2)]
    return terms[0]


def eliminate(cols, below, parts, mine):
    zero = jnp.zeros_like(cols[0])
    pivots = zero
    taken = [x[0] for x in parts]
    for k in range(0, SUB, 2):
        a, b, e = row_of(cols[k], k), row_of(cols[k], k + 1), row_of(cols[k + 1], k + 1)
        det = a * e - b * b
        recip = 1.0 / a
        second = a * (1.0 / det)
        ratio = b * recip
        first_of = [jnp.where(mine[k], zero, cols[k]) * recip]
        last = jnp.where(mine[k], b, jnp.where(mine[k + 1], zero, cols[k + 1] - cols[k] * ratio))
        second_of = [last * second]
        if below is not None:
            reduced = below[k + 1] - below[k] * ratio
            first_of.append(below[k] * recip)
            second_of.append(reduced * second)
        pivots = jnp.where(mine[k], a, jnp.where(mine[k + 1], e - b * ratio, pivots))
        for m in range(k + 2, SUB):
            u = row_of(cols[m], k)
            w = row_of(cols[m], k + 1) - ratio * u
            cols[m] = cols[m] - first_of[0] * u - second_of[0] * w
            if below is not None:
                below[m] = below[m] - first_of[1] * u - second_of[1] * w
        if below is not None:
            for m in range(SUB):
                change = first_of[1] * row_of(below[k], m) + second_of[1] * row_of(reduced, m)
                below[SUB + m] = below[SUB + m] - change
        for i, x in enumerate(parts):
            u = row_of(x[0], k)
            w = row_of(x[0], k + 1) - ratio * u
            taken[i] = jnp.where(mine[k], x[0], jnp.where(mine[k + 1], w, taken[i]))
            for v in range(len(x)):
                x[v] = x[v] - first_of[v] * u - second_of[v] * w
    return pivots, taken


def factor_block(rows, put_upper, put_inverse):
    lane = lax.broadcasted_iota(jnp.int32, (SUB, NB), 1)
    sub = lax.broadcasted_iota(jnp.int32, (SUB, NB), 0)
    mine = [sub == k for k in range(SUB)]
    zero = jnp.zeros((SUB, NB), F32)
    rows = list(rows)
    count = len(rows)

    def emit(g, pivots, upper, inverse):
        root = lax.rsqrt(pivots)
        put_upper(g, jnp.where(lane >= sub + SUB * g, upper * root, zero))
        put_inverse(g, jnp.where(lane <= sub + SUB * g, inverse * root, zero))

    for g in range(0, count, 2):
        b = SUB * g
        col0 = [lane_of(rows[g], b + k) for k in range(SUB)]
        col1 = [lane_of(rows[g + 1], b + k) for k in range(2 * SUB)]
        near = range(g + 2, min(count, g + 4))
        factors = {h: [lane_of(rows[h], b + k) for k in range(2 * SUB)] for h in near}
        group = (lane >= b) & (lane < b + 2 * SUB)
        a = [rows[g], rows[g + 1]]
        w = [
            jnp.where(group, jnp.where(lane - b == sub, F32(1), zero), a[0]),
            jnp.where(group, jnp.where(lane - b - SUB == sub, F32(1), zero), a[1]),
        ]
        pivots, taken = eliminate(col0, col1, [a, w], mine)
        emit(g, pivots, *taken)
        recips = 1.0 / pivots
        a0, w0 = a[0] * recips, w[0] * recips
        above = [lane_of(a0, b + SUB + k) for k in range(SUB)]
        a, w = [a[1]], [w[1]]
        pivots, taken = eliminate(col1[SUB:], None, [a, w], mine)
        emit(g + 1, pivots, *taken)

        left = lane < b + 2 * SUB
        solved1 = jnp.where(left, w[0], a[0]) * (1.0 / pivots)
        lower_rows = [row_of(solved1, k) for k in range(SUB)]
        solved0 = jnp.where(left, w0, a0) - total_of(c * r for c, r in zip(above, lower_rows))
        solved = [row_of(solved0, k) for k in range(SUB)] + lower_rows
        rows[g], rows[g + 1] = solved0, solved1
        for h in near:
            rows[h] = jnp.where(group, zero, rows[h]) - total_of(f * s for f, s in zip(factors[h], solved))
        far = g + 4
        if far < count:
            panel = jnp.concatenate([rows[h] if g <= h < g + 2 else zero for h in range(count)], axis=0)
            rest = jnp.concatenate(rows[far:], axis=0)
            lanes = lax.broadcasted_iota(jnp.int32, rest.shape, 1)
            in_group = (lanes >= b) & (lanes < b + 2 * SUB)
            rest = jnp.where(in_group, F32(0), rest) - product(left_parts(rest), right_parts(panel))
            for i in range(far, count):
                rows[i] = rest[SUB * (i - far) : SUB * (i - far + 1), :]


def at(i, size=NB):
    return slice(i * size, (i + 1) * size)


def apart(n):
    return [(i, j) for i in range(n) for j in range(i + 1, n)]


def triangle_masks():
    r = lax.broadcasted_iota(jnp.int32, (NB, NB), 0)
    c = lax.broadcasted_iota(jnp.int32, (NB, NB), 1)
    return r < c, r == c


def halves(bit, all_ref, keep_ref, send_ref):
    size = keep_ref.shape[0]
    keep_ref[...] = all_ref[pl.ds(pl.multiple_of(bit * size, SUB), size), :]
    send_ref[...] = all_ref[pl.ds(pl.multiple_of((1 - bit) * size, SUB), size), :]


def gram_diag_kernel(s_ref, own_ref, keep_ref, send_ref, all_ref):
    n = own_ref.shape[1] // NB
    right = right_parts(own_ref[...])
    rows = [product(left_parts(own_ref[:, at(i)].T), right[:, i * NB :]) for i in range(n)]
    above, on = triangle_masks()
    tail = (n // 2 + len(apart(n))) * NB
    all_ref[tail:, :] = jnp.zeros((all_ref.shape[0] - tail, NB), F32)
    for i in range(0, n, 2):
        first, second = rows[i][:, :NB], rows[i + 1][:, :NB]
        all_ref[at(i // 2), :] = jnp.where(above | on, first, second)
        all_ref[tail + i // 2 : tail + i // 2 + 1, :] = jnp.sum(jnp.where(on, second, F32(0)), axis=0, keepdims=True)
    for number, (i, j) in enumerate(apart(n)):
        all_ref[at(n // 2 + number), :] = rows[i][:, at(j - i)]
    halves(s_ref[1], all_ref, keep_ref, send_ref)


def gram_cross_kernel(s_ref, own_ref, other_ref, keep_ref, send_ref, first_ref, second_ref, all_ref):
    width = own_ref.shape[1]
    half = width // 2

    @pl.when(s_ref[0] == 0)
    def _():
        first_ref[...] = own_ref[...]
        second_ref[...] = other_ref[:, :half]

    @pl.when(s_ref[0] != 0)
    def _():
        first_ref[...] = other_ref[...]
        second_ref[...] = own_ref[:, half:]

    right = right_parts(second_ref[...])
    per_row = half // NB
    for i in range(width // NB):
        row = product(left_parts(first_ref[:, at(i)].T), right)
        for j in range(per_row):
            all_ref[at(i * per_row + j), :] = row[:, at(j)]
    halves(s_ref[3], all_ref, keep_ref, send_ref)


def solve_kernel(scale, s_ref, *refs):
    sums, (own_ref, other_ref, basis_ref, tri_ref, diag_ref, cross_ref, a_ref, e_ref, inv_ref) = refs[:8], refs[8:]
    width = own_ref.shape[1]
    half = width // NB
    n = 2 * half
    t = s_ref[0]

    for pay_ref, parts, bit in ((diag_ref, sums[:4], 1), (cross_ref, sums[4:], 3)):
        size = parts[0].shape[0]
        places = ((t, s_ref[bit]), (t, 1 - s_ref[bit]), (1 - t, s_ref[bit + 1]), (1 - t, 1 - s_ref[bit + 1]))
        for (core, which), ref in zip(places, parts):
            pay_ref[core, pl.ds(pl.multiple_of(which * size, SUB), size), :] = ref[...]
    e_ref[:, pl.ds(pl.multiple_of(t * width, NB), width)] = own_ref[...]
    e_ref[:, pl.ds(pl.multiple_of((1 - t) * width, NB), width)] = other_ref[...]

    above, on = triangle_masks()
    tail = (half // 2 + len(apart(half))) * NB
    number_of = {ij: half // 2 + number for number, ij in enumerate(apart(half))}

    def gram(i, j):
        if i < half <= j:
            core, col = divmod(j - half, half // 2)
            return cross_ref[core, at(i * (half // 2) + col), :]
        core, i, j = i // half, i % half, j % half
        if i != j:
            return diag_ref[core, at(number_of[i, j]), :]
        both = diag_ref[core, at(i // 2), :]
        if i % 2 == 0:
            return jnp.where(above | on, both, both.T)
        pivots = diag_ref[core, tail + i // 2 : tail + i // 2 + 1, :]
        return jnp.where(on, pivots, jnp.where(above, both.T, both))

    for k in range(n):
        here = at(k)
        source = gram(k, k) if k == 0 else a_ref[here, here]
        rows = [source[at(h, SUB), :] for h in range(NB // SUB)]

        def put_upper(g, v):
            a_ref[k * NB + SUB * g : k * NB + SUB * (g + 1), here] = v

        def put_inverse(g, v):
            inv_ref[at(g, SUB), :] = v

        factor_block(rows, put_upper, put_inverse)
        if k:
            a_ref[here, : k * NB] = jnp.zeros((NB, k * NB), F32)
        inverse = inv_ref[...]
        inverse_left = left_parts(inverse)
        solved = product(left_parts(e_ref[:, here]), right_parts(inverse.T))
        if k + 1 < n:
            rest = slice((k + 1) * NB, n * NB)
            uppers, lowers, rights = {}, {}, {}
            for j in range(k + 1, n):
                uppers[j] = product(inverse_left, right_parts(gram(k, j) if k == 0 else a_ref[here, at(j)]))
                lowers[j] = left_parts(uppers[j].T)
                rights[j] = right_parts(uppers[j])
                a_ref[here, at(j)] = uppers[j]
            for i in range(k + 1, n):
                right = jnp.concatenate([rights[j] for j in range(i, n)], axis=1)
                update = product(lowers[i], right)
                for j in range(i, n):
                    old = gram(i, j) if k == 0 else a_ref[at(i), at(j)]
                    a_ref[at(i), at(j)] = old - update[:, at(j - i)]
            e_ref[:, rest] -= product(left_parts(solved), jnp.concatenate([rights[j] for j in range(k + 1, n)], axis=1))
        e_ref[:, here] = solved * scale
        tri_ref[here, :] = a_ref[here, pl.ds(pl.multiple_of(t * width, NB), width)] * (1.0 / scale)

    basis_ref[...] = e_ref[:, pl.ds(pl.multiple_of(t * width, NB), width)]


def shards(n_rows, effects):
    rows, width = effects.shape
    cols = 2 * width
    half = width // NB
    t = lax.axis_index("tensor")
    me = lax.axis_index("rows")
    swap = [(0, 1), (1, 0)]

    steps = n_rows.bit_length() - 1
    straight = [1 << j for j in range(steps)]
    crossed = straight[1::-1] + straight[2:]

    def bit(masks, j, core):
        return jnp.where(core == 0, (me // masks[0][j]) % 2, (me // masks[1][j]) % 2)

    def exchange(x, masks, j):
        perm = [(2 * r + c, 2 * (r ^ masks[c][j]) + c) for r in range(n_rows) for c in range(2)]
        return lax.ppermute(x, ("rows", "tensor"), perm)

    def sum_rows(keep, send, masks):
        got = exchange(send, masks, 0)
        yield
        total = keep + got
        for j in range(1, steps):
            piece = total.shape[0] // 2
            v = bit(masks, j, t)
            if j < steps - 1:
                sent, total = (lax.dynamic_slice_in_dim(total, i * piece, piece) for i in (1 - v, v))
                got = exchange(sent, masks, j)
            else:
                got = exchange(total, masks, j)
            yield
            total = total + got
        for j in range(steps - 2, 0, -1):
            got = exchange(total, masks, j)
            yield
            v = bit(masks, j, t)
            total = jnp.concatenate([jnp.where(v == 0, total, got), jnp.where(v == 0, got, total)])
        got = exchange(total, masks, 0)
        yield
        yield total, got, lax.ppermute(total, "tensor", swap), lax.ppermute(got, "tensor", swap)

    vmem = pl.BlockSpec(memory_space=pltpu.VMEM)
    smem = pl.BlockSpec(memory_space=pltpu.SMEM)
    params = pltpu.CompilerParams(vmem_limit_bytes=48 * 2**20)
    diag_masks, cross_masks = (straight, crossed), (crossed, straight)
    scalars = jnp.stack([t] + [bit(m, 0, core) for m in (diag_masks, cross_masks) for core in (t, 1 - t)]).astype(jnp.int32)

    grain = SUB * max(n_rows // 2, 2)
    diag_rows = (half // 2 + len(apart(half))) * NB
    diag_rows += -(-(half // 2) // grain) * grain
    cross_rows = half * half // 2 * NB

    other = lax.ppermute(effects, "tensor", swap)
    part = jax.ShapeDtypeStruct((diag_rows // 2, NB), F32)
    diag = pl.pallas_call(
        gram_diag_kernel,
        out_shape=(part, part),
        in_specs=[smem, vmem],
        out_specs=(vmem, vmem),
        scratch_shapes=[pltpu.VMEM((diag_rows, NB), F32)],
        cost_estimate=pl.CostEstimate(flops=12 * rows * diag_rows * NB, bytes_accessed=4 * rows * width, transcendentals=0),
        compiler_params=params,
        name="gram_diag",
    )(scalars, effects)
    part = jax.ShapeDtypeStruct((cross_rows // 2, NB), F32)
    cross = pl.pallas_call(
        gram_cross_kernel,
        out_shape=(part, part),
        in_specs=[smem, vmem, vmem],
        out_specs=(vmem, vmem),
        scratch_shapes=[pltpu.VMEM((rows, width), F32), pltpu.VMEM((rows, width // 2), F32), pltpu.VMEM((cross_rows, NB), F32)],
        cost_estimate=pl.CostEstimate(flops=12 * rows * cross_rows * NB, bytes_accessed=8 * rows * width, transcendentals=0),
        compiler_params=params,
        name="gram_cross",
    )(scalars, effects, other)

    diag_keep, *cross = lax.optimization_barrier((diag[0], *cross))
    diag = (diag_keep, diag[1])
    sums = []
    for pair in zip(sum_rows(*diag, diag_masks), sum_rows(*cross, cross_masks)):
        sums = pair
    scale = float(rows * n_rows) ** 0.5
    return pl.pallas_call(
        functools.partial(solve_kernel, scale),
        out_shape=(jax.ShapeDtypeStruct((rows, width), F32), jax.ShapeDtypeStruct((cols, width), F32)),
        in_specs=[smem] + [vmem] * 10,
        out_specs=(vmem, vmem),
        scratch_shapes=[
            pltpu.VMEM((2, diag_rows, NB), F32),
            pltpu.VMEM((2, cross_rows, NB), F32),
            pltpu.VMEM((cols, cols), F32),
            pltpu.VMEM((rows, cols), F32),
            pltpu.VMEM((NB, NB), F32),
        ],
        compiler_params=params,
        name="cholesky_solve",
    )(scalars, *sums[0], *sums[1], effects, other)


def solution(mesh):
    spec = P(("groups", "rows"), "tensor")
    return jax.shard_map(
        functools.partial(shards, mesh.shape["rows"]),
        mesh=mesh,
        in_specs=(spec,),
        out_specs=(spec, P("groups", "tensor")),
        check_vma=False,
    )
```

time: 91.1 us -> 77.8 us (0.85)
  waiting for transfers between devices: 43.9 us -> 25.1 us
  starting transfers between devices: 10.4 us -> 17.7 us
  Pallas kernels: 34.2 us -> 31.6 us
  local copies, waits for them, and re-layouts: 1.21 us -> 2.21 us
    ppermute x6 -> x10, waiting for transfers between devices: 41.9 us -> 23.6 us  [exchange(): return lax.ppermute(x, ('rows', 'tensor'), perm)]
    ppermute x6 -> x10, starting transfers between devices: 9.91 us -> 16.6 us  [exchange(): return lax.ppermute(x, ('rows', 'tensor'), perm)]
    pallas_call x1, Pallas kernels: 32 us -> 28.9 us  [shards(): pl.pallas_call(functools.partial(solve_kernel, scale), out_shape=(jax.Sha...]
    unnamed x4 -> x6, local copies, waits for them, and re-layouts: 1.16 us -> 2.09 us
    ppermute x2 -> x4, waiting for transfers between devices: 2 us -> 1.52 us  [the longest x2 1.52 us: sum_rows(): lax.ppermute(got, 'tensor', swap)]
  transfers between devices with their start and end apart: 9 -> 15, of which waited for: 7 -> 10; matrix products, arithmetic and copies ran while one was open for 0% -> 0% of each run, Pallas kernels for 1% -> 3%
where the time goes in v3:
time: 77.8 us; the launch traced here: 77.5 us
  Pallas kernels  31.6 us (41%)
  waiting for transfers between devices  25.1 us (32%)
  starting transfers between devices  17.7 us (23%)
  local copies, waits for them, and re-layouts  2.21 us (3%)
    pallas_call x1, Pallas kernels, shards(): pl.pallas_call(functools.partial(solve_kernel, scale), out_shape=(jax.Sha...  28.9 us
    ppermute x10, waiting for transfers between devices, exchange(): return lax.ppermute(x, ('rows', 'tensor'), perm)  23.6 us
    ppermute x10, starting transfers between devices, exchange(): return lax.ppermute(x, ('rows', 'tensor'), perm)  16.6 us
    unnamed x6, local copies, waits for them, and re-layouts  2.09 us
  transfers between devices with their start and end apart: 15, of which 10 were waited for; matrix products, arithmetic and copies ran while one was open for 0% of the time, Pallas kernels for 3%

profile of v3, /device:TPU:0, one launch (start us, length us, event | category | flops | bytes accessed | tf_op | source)
XLA Modules:
  0.0 77.5 jit_solution(1779427236113425059)
XLA Ops:
  0.6 0.5 collective-permute-start
  1.1 0.1 stack.23.s_ref
  1.2 0.0 copy-start
  1.2 1.0 %copy-done = f32[256,512]{1,0:T(8,128)S(1)} copy-done((f32[256,512]{1,0:T(8,128)S(1)}, f32[256,512]{1,0:T(8,128)}, u32[]{:S(2)}) %copy-start) | copy-done | bytes 524312
  2.3 1.4 %gram_diag.1 = (f32[528,128]{1,0:T(8,128)S(1)}, f32[528,128]{1,0:T(8,128)S(1)}) custom-call(s32[5]{0:T(128)S(1)} %stack.23.s_ref, f32[256,512]{1,0:T(8,128)S(1)} %copy-done), custom_call_target="tpu_custom_call" | custom-call | flops 415236096 | bytes 524288 | tf_op jit(solution)/shard_map/gram_diag/pallas_call | solution.py:326
  3.7 2.6 %collective-permute-start.1 = (f32[528,128]{1,0:T(8,128)S(1)}, f32[528,128]{1,0:T(8,128)S(1)}, u32[]{:S(2)}, u32[]{:S(2)}) collective-permute-start(f32[528,128]{1,0:T(8,128)S(1)} %get-tuple-element.13), channel_id=1, source_target_pairs={{0,4},{2,10},{4,0},{6,14},{8,12},{10,2},{12,8},{14,6},{16,20},{18,... | collective-permute-start | bytes 811016 | tf_op jit(solution)/shard_map/ppermute | solution.py:288
  6.3 0.0 collective-permute-done.other_ref.refs_9_
  6.3 0.0 copy-start.1
  6.3 1.0 %copy-done.1 = f32[256,512]{1,0:T(8,128)S(1)} copy-done((f32[256,512]{1,0:T(8,128)S(1)}, f32[256,512]{1,0:T(8,128)}, u32[]{:S(2)}) %copy-start.1) | copy-done | bytes 524312
  7.4 1.3 %gram_cross.1 = (f32[512,128]{1,0:T(8,128)S(1)}, f32[512,128]{1,0:T(8,128)S(1)}) custom-call(s32[5]{0:T(128)S(1)} %stack.23.s_ref, f32[256,512]{1,0:T(8,128)S(1)} %copy-done.1, f32[256,512]{1,0:T(8,128)S(1)} %collective-permute-done.other_ref.refs_9_), custom_call_target="tpu_custom_call" | custom-call | flops 402653184 | bytes 1048576 | tf_op jit(solution)/shard_map/gram_cross/pallas_call | solution.py:337
  8.6 2.1 %collective-permute-done.1 = f32[528,128]{1,0:T(8,128)S(1)} collective-permute-done((f32[528,128]{1,0:T(8,128)S(1)}, f32[528,128]{1,0:T(8,128)S(1)}, u32[]{:S(2)}, u32[]{:S(2)}) %collective-permute-start.1) | collective-permute-done | bytes 270368 | tf_op jit(solution)/shard_map/ppermute | solution.py:288
  10.8 2.2 %collective-permute-start.2 = (f32[264,128]{1,0:T(8,128)S(1)}, f32[264,128]{1,0:T(8,128)S(1)}, u32[]{:S(2)}, u32[]{:S(2)}) collective-permute-start(f32[264,128]{1,0:T(8,128)S(1)} %constant_dynamic-slice_fusion.1), channel_id=1, source_target_pairs={{0,8},{2,6},{4,12},{6,2},{8,0},{10,14},{12,4},{14,10},{16,24},{18,... | collective-permute-start | bytes 405512 | tf_op jit(solution)/shard_map/ppermute | solution.py:288
  13.0 0.1 collective-permute-start.8
  13.1 2.9 %collective-permute-done.2 = f32[264,128]{1,0:T(8,128)S(1)} collective-permute-done((f32[264,128]{1,0:T(8,128)S(1)}, f32[264,128]{1,0:T(8,128)S(1)}, u32[]{:S(2)}, u32[]{:S(2)}) %collective-permute-start.2) | collective-permute-done | bytes 135200 | tf_op jit(solution)/shard_map/ppermute | solution.py:288
  16.0 0.0 copy-start.2
  16.0 3.1 %collective-permute-start.3 = (f32[264,128]{1,0:T(8,128)S(1)}, f32[264,128]{1,0:T(8,128)S(1)}, u32[]{:S(2)}, u32[]{:S(2)}) collective-permute-start(f32[264,128]{1,0:T(8,128)S(1)} %dynamic-slice_add_fusion), channel_id=1, source_target_pairs={{0,16},{2,18},{4,20},{6,22},{8,24},{10,26},{12,28},{14,30},{16,0},... | collective-permute-start | bytes 405512 | tf_op jit(solution)/shard_map/ppermute | solution.py:288
  19.1 2.3 %collective-permute-done.8 = f32[512,128]{1,0:T(8,128)S(1)} collective-permute-done((f32[512,128]{1,0:T(8,128)S(1)}, f32[512,128]{1,0:T(8,128)S(1)}, u32[]{:S(2)}, u32[]{:S(2)}) %collective-permute-start.8) | collective-permute-done | bytes 262176 | tf_op jit(solution)/shard_map/ppermute | solution.py:288
  21.4 1.0 %collective-permute-start.9 = (f32[256,128]{1,0:T(8,128)S(1)}, f32[256,128]{1,0:T(8,128)S(1)}, u32[]{:S(2)}, u32[]{:S(2)}) collective-permute-start(f32[256,128]{1,0:T(8,128)S(1)} %constant_dynamic-slice_fusion), channel_id=1, source_target_pairs={{0,4},{2,10},{4,0},{6,14},{8,12},{10,2},{12,8},{14,6},{16,20},{18,... | collective-permute-start | bytes 393224 | tf_op jit(solution)/shard_map/ppermute | solution.py:288
  22.5 0.9 %collective-permute-done.3 = f32[264,128]{1,0:T(8,128)S(1)} collective-permute-done((f32[264,128]{1,0:T(8,128)S(1)}, f32[264,128]{1,0:T(8,128)S(1)}, u32[]{:S(2)}, u32[]{:S(2)}) %collective-permute-start.3) | collective-permute-done | bytes 135200 | tf_op jit(solution)/shard_map/ppermute | solution.py:288
  23.4 3.0 %collective-permute-start.4 = (f32[264,128]{1,0:T(8,128)S(1)}, f32[264,128]{1,0:T(8,128)S(1)}, u32[]{:S(2)}, u32[]{:S(2)}) collective-permute-start(f32[264,128]{1,0:T(8,128)S(1)} %add.59), channel_id=1, source_target_pairs={{0,8},{2,6},{4,12},{6,2},{8,0},{10,14},{12,4},{14,10},{16,24},{18,... | collective-permute-start | bytes 405512 | tf_op jit(solution)/shard_map/ppermute | solution.py:288
  26.3 0.1 collective-permute-done.9
  26.5 2.4 %collective-permute-start.10 = (f32[256,128]{1,0:T(8,128)S(1)}, f32[256,128]{1,0:T(8,128)S(1)}, u32[]{:S(2)}, u32[]{:S(2)}) collective-permute-start(f32[256,128]{1,0:T(8,128)S(1)} %dynamic-slice_add_fusion.1), channel_id=1, source_target_pairs={{0,16},{2,18},{4,20},{6,22},{8,24},{10,26},{12,28},{14,30},{16,0},... | collective-permute-start | bytes 393224 | tf_op jit(solution)/shard_map/ppermute | solution.py:288
  28.9 5.6 %collective-permute-done.10 = f32[256,128]{1,0:T(8,128)S(1)} collective-permute-done((f32[256,128]{1,0:T(8,128)S(1)}, f32[256,128]{1,0:T(8,128)S(1)}, u32[]{:S(2)}, u32[]{:S(2)}) %collective-permute-start.10) | collective-permute-done | bytes 131104 | tf_op jit(solution)/shard_map/ppermute | solution.py:288
  34.5 0.9 %collective-permute-start.11 = (f32[256,128]{1,0:T(8,128)S(1)}, f32[256,128]{1,0:T(8,128)S(1)}, u32[]{:S(2)}, u32[]{:S(2)}) collective-permute-start(f32[256,128]{1,0:T(8,128)S(1)} %add.64), channel_id=1, source_target_pairs={{0,4},{2,10},{4,0},{6,14},{8,12},{10,2},{12,8},{14,6},{16,20},{18,... | collective-permute-start | bytes 393224 | tf_op jit(solution)/shard_map/ppermute | solution.py:288
  35.4 0.0 collective-permute-done.4
  35.5 1.2 %collective-permute-start.5 = (f32[528,128]{1,0:T(8,128)S(1)}, f32[528,128]{1,0:T(8,128)S(1)}, u32[]{:S(2)}, u32[]{:S(2)}) collective-permute-start(f32[528,128]{1,0:T(8,128)S(1)} %pad_maximum_fusion.refs_0_), channel_id=1, source_target_pairs={{0,4},{2,10},{4,0},{6,14},{8,12},{10,2},{12,8},{14,6},{16,20},{18,... | collective-permute-start | bytes 811016 | tf_op jit(solution)/shard_map/ppermute | solution.py:288
  36.7 3.9 %collective-permute-done.11 = f32[256,128]{1,0:T(8,128)S(1)} collective-permute-done((f32[256,128]{1,0:T(8,128)S(1)}, f32[256,128]{1,0:T(8,128)S(1)}, u32[]{:S(2)}, u32[]{:S(2)}) %collective-permute-start.11) | collective-permute-done | bytes 131104 | tf_op jit(solution)/shard_map/ppermute | solution.py:288
  40.7 0.1 collective-permute-start.12
  40.8 0.1 collective-permute-start.6
  40.9 4.4 %collective-permute-done.5.refs_1_ = f32[528,128]{1,0:T(8,128)S(1)} collective-permute-done((f32[528,128]{1,0:T(8,128)S(1)}, f32[528,128]{1,0:T(8,128)S(1)}, u32[]{:S(2)}, u32[]{:S(2)}) %collective-permute-start.5) | collective-permute-done | bytes 270368 | tf_op jit(solution)/shard_map/ppermute | solution.py:288
  45.2 0.0 collective-permute-start.7
  45.2 0.5 collective-permute-start.13
  45.7 1.4 %collective-permute-done.12.refs_5_ = f32[512,128]{1,0:T(8,128)S(1)} collective-permute-done((f32[512,128]{1,0:T(8,128)S(1)}, f32[512,128]{1,0:T(8,128)S(1)}, u32[]{:S(2)}, u32[]{:S(2)}) %collective-permute-start.12) | collective-permute-done | bytes 262176 | tf_op jit(solution)/shard_map/ppermute | solution.py:288
  47.1 0.0 collective-permute-start.14
  47.1 0.0 collective-permute-done.6.refs_2_
  47.1 0.0 collective-permute-done.13.refs_6_
  47.2 0.0 collective-permute-done.7.refs_3_
  47.2 1.5 %collective-permute-done.14.refs_7_ = f32[512,128]{1,0:T(8,128)S(1)} collective-permute-done((f32[512,128]{1,0:T(8,128)S(1)}, f32[512,128]{1,0:T(8,128)S(1)}, u32[]{:S(2)}, u32[]{:S(2)}) %collective-permute-start.14) | collective-permute-done | bytes 262176 | tf_op jit(solution)/shard_map/ppermute | solution.py:311
  48.7 0.0 copy-done.2
  48.7 28.9 %cholesky_solve.1 = (f32[256,512]{1,0:T(8,128)}, f32[1024,512]{1,0:T(8,128)}) custom-call(s32[5]{0:T(128)S(1)} %stack.23.s_ref, f32[528,128]{1,0:T(8,128)S(1)} %pad_maximum_fusion.refs_0_, f32[528,128]{1,0:T(8,128)S(1)} %collective-permute-done.5.refs_1_, f32[528,128]{1,0:T(8,128)S(1)} %collective-permute-done.6.refs_2_, ...), custom_call_target="tpu_custom_call" | custom-call | tf_op jit(solution)/shard_map/cholesky_solve/pallas_call | solution.py:354
  (12 shorter events, 0.3 us)
Async XLA Ops:
  0.6 5.7 %collective-permute-start = (f32[256,512]{1,0:T(8,128)}, f32[256,512]{1,0:T(8,128)S(1)}, u32[]{:S(2)}, u32[]{:S(2)}) collective-permute-start(f32[256,512]{1,0:T(8,128)} %refs_8_.1), channel_id=1, source_target_pairs={{0,2},{2,0},{1,3},{3,1},{4,6},{6,4},{5,7},{7,5},{8,10},{10,8},{9,1... | collective-permute-start | bytes 1572872 | tf_op jit(solution)/shard_map/ppermute | solution.py:324
  1.2 1.0 %copy-start = (f32[256,512]{1,0:T(8,128)S(1)}, f32[256,512]{1,0:T(8,128)}, u32[]{:S(2)}) copy-start(f32[256,512]{1,0:T(8,128)} %refs_8_.1) | copy-start | bytes 1572868
  3.7 7.1 %collective-permute-start.1 = (f32[528,128]{1,0:T(8,128)S(1)}, f32[528,128]{1,0:T(8,128)S(1)}, u32[]{:S(2)}, u32[]{:S(2)}) collective-permute-start(f32[528,128]{1,0:T(8,128)S(1)} %get-tuple-element.13), channel_id=1, source_target_pairs={{0,4},{2,10},{4,0},{6,14},{8,12},{10,2},{12,8},{14,6},{16,20},{18,... | collective-permute-start | bytes 811016 | tf_op jit(solution)/shard_map/ppermute | solution.py:288
  6.3 1.0 %copy-start.1 = (f32[256,512]{1,0:T(8,128)S(1)}, f32[256,512]{1,0:T(8,128)}, u32[]{:S(2)}) copy-start(f32[256,512]{1,0:T(8,128)} %refs_8_.1) | copy-start | bytes 1572868
  10.8 5.2 %collective-permute-start.2 = (f32[264,128]{1,0:T(8,128)S(1)}, f32[264,128]{1,0:T(8,128)S(1)}, u32[]{:S(2)}, u32[]{:S(2)}) collective-permute-start(f32[264,128]{1,0:T(8,128)S(1)} %constant_dynamic-slice_fusion.1), channel_id=1, source_target_pairs={{0,8},{2,6},{4,12},{6,2},{8,0},{10,14},{12,4},{14,10},{16,24},{18,... | collective-permute-start | bytes 405512 | tf_op jit(solution)/shard_map/ppermute | solution.py:288
  13.0 8.4 %collective-permute-start.8 = (f32[512,128]{1,0:T(8,128)S(1)}, f32[512,128]{1,0:T(8,128)S(1)}, u32[]{:S(2)}, u32[]{:S(2)}) collective-permute-start(f32[512,128]{1,0:T(8,128)S(1)} %get-tuple-element.15), channel_id=1, source_target_pairs={{0,8},{2,6},{4,12},{6,2},{8,0},{10,14},{12,4},{14,10},{16,24},{18,... | collective-permute-start | bytes 786440 | tf_op jit(solution)/shard_map/ppermute | solution.py:288
  16.0 32.7 %copy-start.2 = (f32[256,512]{1,0:T(8,128)S(1)}, f32[256,512]{1,0:T(8,128)}, u32[]{:S(2)}) copy-start(f32[256,512]{1,0:T(8,128)} %refs_8_.1) | copy-start | bytes 1572868
  16.0 7.3 %collective-permute-start.3 = (f32[264,128]{1,0:T(8,128)S(1)}, f32[264,128]{1,0:T(8,128)S(1)}, u32[]{:S(2)}, u32[]{:S(2)}) collective-permute-start(f32[264,128]{1,0:T(8,128)S(1)} %dynamic-slice_add_fusion), channel_id=1, source_target_pairs={{0,16},{2,18},{4,20},{6,22},{8,24},{10,26},{12,28},{14,30},{16,0},... | collective-permute-start | bytes 405512 | tf_op jit(solution)/shard_map/ppermute | solution.py:288
  21.4 5.0 %collective-permute-start.9 = (f32[256,128]{1,0:T(8,128)S(1)}, f32[256,128]{1,0:T(8,128)S(1)}, u32[]{:S(2)}, u32[]{:S(2)}) collective-permute-start(f32[256,128]{1,0:T(8,128)S(1)} %constant_dynamic-slice_fusion), channel_id=1, source_target_pairs={{0,4},{2,10},{4,0},{6,14},{8,12},{10,2},{12,8},{14,6},{16,20},{18,... | collective-permute-start | bytes 393224 | tf_op jit(solution)/shard_map/ppermute | solution.py:288
  23.4 12.1 %collective-permute-start.4 = (f32[264,128]{1,0:T(8,128)S(1)}, f32[264,128]{1,0:T(8,128)S(1)}, u32[]{:S(2)}, u32[]{:S(2)}) collective-permute-start(f32[264,128]{1,0:T(8,128)S(1)} %add.59), channel_id=1, source_target_pairs={{0,8},{2,6},{4,12},{6,2},{8,0},{10,14},{12,4},{14,10},{16,24},{18,... | collective-permute-start | bytes 405512 | tf_op jit(solution)/shard_map/ppermute | solution.py:288
  26.5 8.0 %collective-permute-start.10 = (f32[256,128]{1,0:T(8,128)S(1)}, f32[256,128]{1,0:T(8,128)S(1)}, u32[]{:S(2)}, u32[]{:S(2)}) collective-permute-start(f32[256,128]{1,0:T(8,128)S(1)} %dynamic-slice_add_fusion.1), channel_id=1, source_target_pairs={{0,16},{2,18},{4,20},{6,22},{8,24},{10,26},{12,28},{14,30},{16,0},... | collective-permute-start | bytes 393224 | tf_op jit(solution)/shard_map/ppermute | solution.py:288
  34.5 6.2 %collective-permute-start.11 = (f32[256,128]{1,0:T(8,128)S(1)}, f32[256,128]{1,0:T(8,128)S(1)}, u32[]{:S(2)}, u32[]{:S(2)}) collective-permute-start(f32[256,128]{1,0:T(8,128)S(1)} %add.64), channel_id=1, source_target_pairs={{0,4},{2,10},{4,0},{6,14},{8,12},{10,2},{12,8},{14,6},{16,20},{18,... | collective-permute-start | bytes 393224 | tf_op jit(solution)/shard_map/ppermute | solution.py:288
  35.5 9.8 %collective-permute-start.5 = (f32[528,128]{1,0:T(8,128)S(1)}, f32[528,128]{1,0:T(8,128)S(1)}, u32[]{:S(2)}, u32[]{:S(2)}) collective-permute-start(f32[528,128]{1,0:T(8,128)S(1)} %pad_maximum_fusion.refs_0_), channel_id=1, source_target_pairs={{0,4},{2,10},{4,0},{6,14},{8,12},{10,2},{12,8},{14,6},{16,20},{18,... | collective-permute-start | bytes 811016 | tf_op jit(solution)/shard_map/ppermute | solution.py:288
  40.7 6.4 %collective-permute-start.12 = (f32[512,128]{1,0:T(8,128)S(1)}, f32[512,128]{1,0:T(8,128)S(1)}, u32[]{:S(2)}, u32[]{:S(2)}) collective-permute-start(f32[512,128]{1,0:T(8,128)S(1)} %pad_maximum_fusion.1.refs_4_), channel_id=1, source_target_pairs={{0,8},{2,6},{4,12},{6,2},{8,0},{10,14},{12,4},{14,10},{16,24},{18,... | collective-permute-start | bytes 786440 | tf_op jit(solution)/shard_map/ppermute | solution.py:288
  40.8 6.4 %collective-permute-start.6 = (f32[528,128]{1,0:T(8,128)S(1)}, f32[528,128]{1,0:T(8,128)S(1)}, u32[]{:S(2)}, u32[]{:S(2)}) collective-permute-start(f32[528,128]{1,0:T(8,128)S(1)} %pad_maximum_fusion.refs_0_), channel_id=1, source_target_pairs={{0,2},{2,0},{1,3},{3,1},{4,6},{6,4},{5,7},{7,5},{8,10},{10,8},{9,1... | collective-permute-start | bytes 811016 | tf_op jit(solution)/shard_map/ppermute | solution.py:311
  45.2 1.9 %collective-permute-start.7 = (f32[528,128]{1,0:T(8,128)S(1)}, f32[528,128]{1,0:T(8,128)S(1)}, u32[]{:S(2)}, u32[]{:S(2)}) collective-permute-start(f32[528,128]{1,0:T(8,128)S(1)} %collective-permute-done.5.refs_1_), channel_id=1, source_target_pairs={{0,2},{2,0},{1,3},{3,1},{4,6},{6,4},{5,7},{7,5},{8,10},{10,8},{9,1... | collective-permute-start | bytes 811016 | tf_op jit(solution)/shard_map/ppermute | solution.py:311
  45.2 1.9 %collective-permute-start.13 = (f32[512,128]{1,0:T(8,128)S(1)}, f32[512,128]{1,0:T(8,128)S(1)}, u32[]{:S(2)}, u32[]{:S(2)}) collective-permute-start(f32[512,128]{1,0:T(8,128)S(1)} %pad_maximum_fusion.1.refs_4_), channel_id=1, source_target_pairs={{0,2},{2,0},{1,3},{3,1},{4,6},{6,4},{5,7},{7,5},{8,10},{10,8},{9,1... | collective-permute-start | bytes 786440 | tf_op jit(solution)/shard_map/ppermute | solution.py:311
  47.1 1.5 %collective-permute-start.14 = (f32[512,128]{1,0:T(8,128)S(1)}, f32[512,128]{1,0:T(8,128)S(1)}, u32[]{:S(2)}, u32[]{:S(2)}) collective-permute-start(f32[512,128]{1,0:T(8,128)S(1)} %collective-permute-done.12.refs_5_), channel_id=1, source_target_pairs={{0,2},{2,0},{1,3},{3,1},{4,6},{6,4},{5,7},{7,5},{8,10},{10,8},{9,1... | collective-permute-start | bytes 786440 | tf_op jit(solution)/shard_map/ppermute | solution.py:311

commit v4 on v3

v4 whole, which is shorter than its diff:
```python
import functools

import jax
import jax.numpy as jnp
from jax import lax
from jax.experimental import pallas as pl
from jax.experimental.pallas import tpu as pltpu
from jax.sharding import PartitionSpec as P

F32 = jnp.float32
BF16 = jnp.bfloat16
NB = 128
SUB = 8


def split(x):
    high = x.astype(BF16)
    rest = x - high.astype(F32)
    mid = rest.astype(BF16)
    return high, mid, (rest - mid.astype(F32)).astype(BF16)


def left_parts(x):
    h, m, l = split(x)
    return jnp.concatenate([h, h, m, m, h, l], axis=1)


def right_parts(x):
    h, m, l = split(x)
    return jnp.concatenate([h, m, h, m, l, h], axis=0)


def product(left, right):
    return jnp.dot(left, right, preferred_element_type=F32)


def row_of(x, k):
    return jnp.broadcast_to(x[k : k + 1, :], x.shape)


def lane_of(x, j):
    return jnp.broadcast_to(x[:, j : j + 1], x.shape)


def total_of(terms):
    terms = list(terms)
    while len(terms) > 1:
        terms = [terms[i] + terms[i + 1] if i + 1 < len(terms) else terms[i] for i in range(0, len(terms), 2)]
    return terms[0]


def eliminate(cols, below, parts, mine):
    zero = jnp.zeros_like(cols[0])
    pivots = zero
    taken = [x[0] for x in parts]
    for k in range(0, SUB, 2):
        a, b, e = row_of(cols[k], k), row_of(cols[k], k + 1), row_of(cols[k + 1], k + 1)
        det = a * e - b * b
        recip = 1.0 / a
        second = a * (1.0 / det)
        ratio = b * recip
        first_of = [jnp.where(mine[k], zero, cols[k]) * recip]
        last = jnp.where(mine[k], b, jnp.where(mine[k + 1], zero, cols[k + 1] - cols[k] * ratio))
        second_of = [last * second]
        if below is not None:
            reduced = below[k + 1] - below[k] * ratio
            first_of.append(below[k] * recip)
            second_of.append(reduced * second)
        pivots = jnp.where(mine[k], a, jnp.where(mine[k + 1], e - b * ratio, pivots))
        for m in range(k + 2, SUB):
            u = row_of(cols[m], k)
            w = row_of(cols[m], k + 1) - ratio * u
            cols[m] = cols[m] - first_of[0] * u - second_of[0] * w
            if below is not None:
                below[m] = below[m] - first_of[1] * u - second_of[1] * w
        if below is not None:
            for m in range(SUB):
                change = first_of[1] * row_of(below[k], m) + second_of[1] * row_of(reduced, m)
                below[SUB + m] = below[SUB + m] - change
        for i, x in enumerate(parts):
            u = row_of(x[0], k)
            w = row_of(x[0], k + 1) - ratio * u
            taken[i] = jnp.where(mine[k], x[0], jnp.where(mine[k + 1], w, taken[i]))
            for v in range(len(x)):
                x[v] = x[v] - first_of[v] * u - second_of[v] * w
    return pivots, taken


def factor_block(rows, put_upper, put_inverse):
    lane = lax.broadcasted_iota(jnp.int32, (SUB, NB), 1)
    sub = lax.broadcasted_iota(jnp.int32, (SUB, NB), 0)
    mine = [sub == k for k in range(SUB)]
    zero = jnp.zeros((SUB, NB), F32)
    rows = list(rows)
    count = len(rows)

    def emit(g, pivots, upper, inverse):
        root = lax.rsqrt(pivots)
        put_upper(g, jnp.where(lane >= sub + SUB * g, upper * root, zero))
        put_inverse(g, jnp.where(lane <= sub + SUB * g, inverse * root, zero))

    for g in range(0, count, 2):
        b = SUB * g
        col0 = [lane_of(rows[g], b + k) for k in range(SUB)]
        col1 = [lane_of(rows[g + 1], b + k) for k in range(2 * SUB)]
        near = range(g + 2, min(count, g + 4))
        factors = {h: [lane_of(rows[h], b + k) for k in range(2 * SUB)] for h in near}
        group = (lane >= b) & (lane < b + 2 * SUB)
        a = [rows[g], rows[g + 1]]
        w = [
            jnp.where(group, jnp.where(lane - b == sub, F32(1), zero), a[0]),
            jnp.where(group, jnp.where(lane - b - SUB == sub, F32(1), zero), a[1]),
        ]
        pivots, taken = eliminate(col0, col1, [a, w], mine)
        emit(g, pivots, *taken)
        recips = 1.0 / pivots
        a0, w0 = a[0] * recips, w[0] * recips
        above = [lane_of(a0, b + SUB + k) for k in range(SUB)]
        a, w = [a[1]], [w[1]]
        pivots, taken = eliminate(col1[SUB:], None, [a, w], mine)
        emit(g + 1, pivots, *taken)

        left = lane < b + 2 * SUB
        solved1 = jnp.where(left, w[0], a[0]) * (1.0 / pivots)
        lower_rows = [row_of(solved1, k) for k in range(SUB)]
        solved0 = jnp.where(left, w0, a0) - total_of(c * r for c, r in zip(above, lower_rows))
        solved = [row_of(solved0, k) for k in range(SUB)] + lower_rows
        rows[g], rows[g + 1] = solved0, solved1
        for h in near:
            rows[h] = jnp.where(group, zero, rows[h]) - total_of(f * s for f, s in zip(factors[h], solved))
        far = g + 4
        if far < count:
            panel = jnp.concatenate([rows[h] if g <= h < g + 2 else zero for h in range(count)], axis=0)
            rest = jnp.concatenate(rows[far:], axis=0)
            lanes = lax.broadcasted_iota(jnp.int32, rest.shape, 1)
            in_group = (lanes >= b) & (lanes < b + 2 * SUB)
            rest = jnp.where(in_group, F32(0), rest) - product(left_parts(rest), right_parts(panel))
            for i in range(far, count):
                rows[i] = rest[SUB * (i - far) : SUB * (i - far + 1), :]


def at(i, size=NB):
    return slice(i * size, (i + 1) * size)


def apart(n):
    return [(i, j) for i in range(n) for j in range(i + 1, n)]


def triangle_masks():
    r = lax.broadcasted_iota(jnp.int32, (NB, NB), 0)
    c = lax.broadcasted_iota(jnp.int32, (NB, NB), 1)
    return r < c, r == c


def halves(bit, all_ref, keep_ref, send_ref):
    size = keep_ref.shape[0]
    keep_ref[...] = all_ref[pl.ds(pl.multiple_of(bit * size, SUB), size), :]
    send_ref[...] = all_ref[pl.ds(pl.multiple_of((1 - bit) * size, SUB), size), :]


def square_layout(n):
    packs, offs = n // 4, len(apart(n)) // 2
    place = {(i, i): ((i // 2) // packs, (i // 2) % packs) for i in range(n)}
    place.update({ij: (number // offs, packs + number % offs) for number, ij in enumerate(apart(n))})
    return place, packs + offs


def square_products(core, start, left_of, right, out_ref):
    n = right.shape[1] // NB
    place, tail = square_layout(n)
    above, on = triangle_masks()
    for i in range(n):
        mine = [j for j in range(i, n) if place[i, j][0] == core]
        if not mine:
            continue
        row = product(left_of(i), right[:, mine[0] * NB :])
        for j in mine:
            block = row[:, at(j - mine[0])]
            where = slice(start + place[i, j][1] * NB, start + (place[i, j][1] + 1) * NB)
            if i != j:
                out_ref[where, :] = block
            elif i % 2 == 0:
                even = block
            else:
                out_ref[where, :] = jnp.where(above | on, even, block)
                pivots = jnp.sum(jnp.where(on, block, F32(0)), axis=0, keepdims=True)
                row_at = start + tail * NB + place[i, j][1]
                out_ref[row_at : row_at + 1, :] = pivots


def square_blocks(ref, start, n):
    above, on = triangle_masks()
    place, tail = square_layout(n)

    def block(i, j):
        core, number = place[i, j]
        both = ref[core, start + number * NB : start + (number + 1) * NB, :]
        if i != j:
            return both
        if i % 2 == 0:
            return jnp.where(above | on, both, both.T)
        row_at = start + tail * NB + number
        return jnp.where(on, ref[core, row_at : row_at + 1, :], jnp.where(above, both.T, both))

    return block


def copy_kernel(x_ref, out_ref):
    out_ref[...] = x_ref[...]


def gram_first_kernel(s_ref, own_ref, other_ref, keep_ref, send_ref, all_ref):
    all_ref[...] = jnp.zeros_like(all_ref)
    for core, e_ref in ((0, own_ref), (1, other_ref)):

        @pl.when(s_ref[0] == core)
        def _():
            square_products(core, 0, lambda i: left_parts(e_ref[:, at(i)].T), right_parts(e_ref[...]), all_ref)

    halves(s_ref[1], all_ref, keep_ref, send_ref)


def gram_second_kernel(s_ref, own_ref, other_ref, keep_ref, send_ref, all_ref):
    width = own_ref.shape[1]
    half = width // 2
    per_row = half // NB
    behind = width // NB * per_row * NB
    all_ref[behind:, :] = jnp.zeros((all_ref.shape[0] - behind, NB), F32)
    for core, first_ref, second_ref in ((0, own_ref, other_ref), (1, other_ref, own_ref)):

        @pl.when(s_ref[0] == core)
        def _():
            right = right_parts(second_ref[...])
            for i in range(width // NB):
                row = product(left_parts(first_ref[:, at(i)].T), right[:, core * half : (core + 1) * half])
                for j in range(per_row):
                    all_ref[at(i * per_row + j), :] = row[:, at(j)]
            square_products(core, behind, lambda i: left_parts(second_ref[:, at(i)].T), right, all_ref)

    halves(s_ref[3], all_ref, keep_ref, send_ref)


def gather_halves(t, s_ref, bit, parts, out_ref):
    size = parts[0].shape[0]
    places = ((t, s_ref[bit]), (t, 1 - s_ref[bit]), (1 - t, s_ref[bit + 1]), (1 - t, 1 - s_ref[bit + 1]))
    for (core, which), ref in zip(places, parts):
        out_ref[core, pl.ds(pl.multiple_of(which * size, SUB), size), :] = ref[...]


def factor_step(k, n, read, upper_ref, inv_ref, write):
    source = read(k, k)

    def put_upper(g, v):
        upper_ref[at(g, SUB), at(k)] = v

    def put_inverse(g, v):
        inv_ref[at(g, SUB), :] = v

    factor_block([source[at(h, SUB), :] for h in range(NB // SUB)], put_upper, put_inverse)
    if k:
        upper_ref[:, : k * NB] = jnp.zeros((NB, k * NB), F32)
    inverse = inv_ref[...]
    lowers, rights = {}, {}
    if k + 1 < n:
        inverse_left = left_parts(inverse)
        for j in range(k + 1, n):
            upper = product(inverse_left, right_parts(read(k, j)))
            lowers[j] = left_parts(upper.T)
            rights[j] = right_parts(upper)
            upper_ref[:, at(j)] = upper
        for i in range(k + 1, n):
            update = product(lowers[i], jnp.concatenate([rights[j] for j in range(i, n)], axis=1))
            for j in range(i, n):
                write(i, j, read(i, j) - update[:, at(j - i)])
    return inverse, lowers, rights


def invert_step(k, n, inverse, lowers, read, write, out_ref):
    left = left_parts(inverse)
    row = [product(left, right_parts(read(k, j))) for j in range(k)] + [inverse]
    for j, block in enumerate(row):
        out_ref[:, at(j)] = block
    if k + 1 < n:
        out_ref[:, (k + 1) * NB :] = jnp.zeros((NB, (n - k - 1) * NB), F32)
        right = right_parts(jnp.concatenate(row, axis=1))
        for i in range(k + 1, n):
            update = product(lowers[i], right)
            for j in range(k + 1):
                write(i, j, (read(i, j) if j < k else F32(0)) - update[:, at(j)])


def solve_columns(first, own_ref, other_ref, row_refs, out_refs, start):
    for k, row_ref, out_ref in zip(range(start, start + len(row_refs)), row_refs, out_refs):
        depth = (k + 1) * NB
        effects = jnp.where(first, own_ref[:, :depth], other_ref[:, :depth])
        out_ref[...] = product(left_parts(effects), right_parts(row_ref[:, :depth].T))


def start_kernel(ks, s_ref, p0, p1, p2, p3, *refs):
    sums_ref = refs[-1]
    n = refs[0].shape[1] // NB
    gather_halves(s_ref[0], s_ref, 1, (p0, p1, p2, p3), sums_ref)
    row_steps(ks, n, square_blocks(sums_ref, 0, n), None, *refs[:-1])


def next_kernel(ks, before, s_ref, own_ref, other_ref, *refs):
    row_refs, (rest_in, inv_rest_in), refs = refs[: len(before)], refs[len(before) : len(before) + 2], refs[len(before) + 2 :]
    n = own_ref.shape[1] // NB
    solve_columns(s_ref[0] == 0, own_ref, other_ref, row_refs, refs[: len(before)], before[0])

    def gram(i, j):
        return rest_in[at(i), at(j)]

    def inv_gram(i, j):
        return inv_rest_in[at(i), at(j)]

    row_steps(ks, n, gram, inv_gram, *refs[len(before) :])


def row_steps(ks, n, gram, inv_gram, *refs):
    rest_ref, inv_rest_ref, inv_ref = refs[3 * len(ks) :]

    def rest(i, j):
        return rest_ref[at(i), at(j)]

    def inv_rest(i, j):
        return inv_rest_ref[at(i), at(j)]

    for number, k in enumerate(ks):
        sources = (gram, inv_gram) if number == 0 else (rest, inv_rest)
        one_step(k, n, *sources, *refs[number : 3 * len(ks) : len(ks)], rest_ref, inv_rest_ref, inv_ref)


def one_step(k, n, gram, inv_gram, upper_ref, left_ref, row_ref, rest_ref, inv_rest_ref, inv_ref):
    def write(i, j, v):
        rest_ref[at(i), at(j)] = v

    def inv_write(i, j, v):
        inv_rest_ref[at(i), at(j)] = v

    inverse, lowers, _ = factor_step(k, n, gram, upper_ref, inv_ref, write)
    invert_step(k, n, inverse, lowers, inv_gram, inv_write, row_ref)
    left_ref[...] = left_parts(row_ref[:, : (k + 1) * NB])


def last_kernel(scale, s_ref, *refs):
    parts, (own_ref, other_ref), refs = refs[:4], refs[4:6], refs[6:]
    width = own_ref.shape[1]
    n = width // NB
    upper_refs, left_refs, first_refs, refs = refs[:n], refs[n : 2 * n], refs[2 * n : 3 * n - 1], refs[3 * n - 1 :]
    inv_row_ref, basis_ref, tri_ref, sums_ref, cross_upper_ref, work_ref, row_ref, e_ref, inv_ref, column_ref = refs
    t = s_ref[0]
    gather_halves(t, s_ref, 3, parts, sums_ref)
    gram = square_blocks(sums_ref, n * (n // 2) * NB, n)
    inverse_lefts = [ref[...] for ref in left_refs]
    lowers, rights = [], []
    for j in range(n):
        core, col = divmod(j, n // 2)
        parts = split(jnp.concatenate([sums_ref[core, at(i * (n // 2) + col), :] for i in range(n)], axis=0))
        column = []
        for k in range(n):
            h, m, l = (x[: (k + 1) * NB, :] for x in parts)
            column.append(product(inverse_lefts[k], jnp.concatenate([h, m, h, m, l, h], axis=0)))
            cross_upper_ref[at(k), at(j)] = column[k]
        column = jnp.concatenate(column, axis=0)
        lowers.append(left_parts(column.T))
        rights.append(right_parts(column))
    for i in range(n):
        update = product(lowers[i], jnp.concatenate(rights[i:], axis=1))
        for j in range(i, n):
            work_ref[at(i), at(j)] = gram(i, j) - update[:, at(j - i)]
    solve_columns(t == 0, own_ref, other_ref, [inv_row_ref], [column_ref], n - 1)
    first_refs = (*first_refs, column_ref)
    solved = jnp.concatenate([ref[...] for ref in first_refs], axis=1)
    effects = jnp.where(t == 0, other_ref[...], own_ref[...])
    e_ref[...] = effects - product(left_parts(solved), jnp.concatenate(rights, axis=1))

    def read(i, j):
        return work_ref[at(i), at(j)]

    def write(i, j, v):
        work_ref[at(i), at(j)] = v

    first = t == 0
    for k in range(n):
        tri_ref[at(k), :] = jnp.where(first, upper_refs[k][...], cross_upper_ref[at(k), :]) * (1.0 / scale)
    for k in range(n):
        inverse, _, rights = factor_step(k, n, read, row_ref, inv_ref, write)
        solved = product(left_parts(e_ref[:, at(k)]), right_parts(inverse.T))
        if k + 1 < n:
            later = jnp.concatenate([rights[j] for j in range(k + 1, n)], axis=1)
            e_ref[:, (k + 1) * NB :] -= product(left_parts(solved), later)
        basis_ref[:, at(k)] = jnp.where(first, first_refs[k][...], solved) * scale
        tri_ref[at(n + k), :] = jnp.where(first, F32(0), row_ref[...] * (1.0 / scale))


def shards(n_rows, effects):
    rows, width = effects.shape
    cols = 2 * width
    half = width // NB
    t = lax.axis_index("tensor")
    me = lax.axis_index("rows")
    swap = [(0, 1), (1, 0)]

    steps = n_rows.bit_length() - 1
    straight = [1 << j for j in range(steps)]
    crossed = straight[1::-1] + straight[2:]

    def bit(masks, j, core):
        return jnp.where(core == 0, (me // masks[0][j]) % 2, (me // masks[1][j]) % 2)

    def exchange(x, masks, j):
        perm = [(2 * r + c, 2 * (r ^ masks[c][j]) + c) for r in range(n_rows) for c in range(2)]
        return lax.ppermute(x, ("rows", "tensor"), perm)

    def sum_rows(keep, send, masks):
        def tie(got, gate):
            return got if gate is None else lax.optimization_barrier((got, gate))[0]

        got = exchange(send, masks, 0)
        total = keep + tie(got, (yield keep))
        for j in range(1, steps - 1):
            piece = total.shape[0] // 2
            v = bit(masks, j, t)
            sent, total = (lax.dynamic_slice_in_dim(total, i * piece, piece) for i in (1 - v, v))
            got = exchange(sent, masks, j)
            total = total + tie(got, (yield total))
        got = exchange(total, masks, steps - 1)
        total = total + tie(got, (yield total))
        for j in range(steps - 2, 0, -1):
            got = exchange(total, masks, j)
            got = tie(got, (yield total))
            v = bit(masks, j, t)
            total = jnp.concatenate([jnp.where(v == 0, total, got), jnp.where(v == 0, got, total)])
        got = exchange(total, masks, 0)
        got = tie(got, (yield total))
        yield total, got, lax.ppermute(total, "tensor", swap), lax.ppermute(got, "tensor", swap)

    vmem = pl.BlockSpec(memory_space=pltpu.VMEM)
    smem = pl.BlockSpec(memory_space=pltpu.SMEM)
    params = pltpu.CompilerParams(vmem_limit_bytes=20 * 2**20)

    def array(*shape):
        return jax.ShapeDtypeStruct(shape, F32)

    def call(kernel, name, out_shape, scratch, *args):
        scalar = [a.dtype == jnp.int32 for a in args]
        return pl.pallas_call(
            kernel,
            out_shape=out_shape,
            in_specs=[smem if s else vmem for s in scalar],
            out_specs=tuple(vmem for _ in out_shape),
            scratch_shapes=[pltpu.VMEM(shape, F32) for shape in scratch],
            cost_estimate=pl.CostEstimate(flops=0, bytes_accessed=0, transcendentals=0),
            compiler_params=params,
            name=name,
        )(*args)

    first_masks, second_masks = (straight, crossed), (crossed, straight)
    scalars = jnp.stack([t] + [bit(m, 0, core) for m in (first_masks, second_masks) for core in (t, 1 - t)]).astype(jnp.int32)

    grain = SUB * max(n_rows // 2, 2)
    first_rows = square_layout(half)[1] * NB
    second_rows = first_rows + half * half // 2 * NB
    first_rows, second_rows = (x + -(-(half // 4) // grain) * grain for x in (first_rows, second_rows))

    other = lax.ppermute(effects, "tensor", swap)
    def halves_of(size):
        return (array(size // 2, NB),) * 2

    (own,) = call(copy_kernel, "own_copy", (array(rows, width),), [], effects)
    first = call(gram_first_kernel, "gram_first", halves_of(first_rows), [(first_rows, NB)], scalars, own, other)
    second = call(gram_second_kernel, "gram_second", halves_of(second_rows), [(second_rows, NB)], scalars, own, other)
    first_keep, *second = lax.optimization_barrier((first[0], *second))
    one, two = sum_rows(first_keep, first[1], first_masks), sum_rows(*second, second_masks)
    next(one), next(two)
    stages = 2 * steps - 1
    for i in range(stages):
        first_sums = one.send(None)
        if i >= 2:
            two.send(None)

    uppers, lefts, inverse_rows, solved = [], [], [], []
    rest = first_sums
    before = []
    for ks in ([0], list(range(1, half - 1)), [half - 1]):
        columns = [array(rows, NB) for _ in before]
        out = [array(NB, width) for _ in ks]
        out += [jax.ShapeDtypeStruct((NB, 6 * (k + 1) * NB), BF16) for k in ks]
        out += [array(NB, width) for _ in ks] + [array(width, width), array(width, width)]
        if before:
            kernel, scratch = functools.partial(next_kernel, ks, before), [(NB, NB)]
            args = (scalars, own, other, *inverse_rows[before[0] :], *rest)
        else:
            kernel, scratch = functools.partial(start_kernel, ks), [(NB, NB), (2, first_rows, NB)]
            args = (scalars, *rest)
        *made, rest_rows, rest_inverse = call(kernel, "factor_rows", columns + out, scratch, *args)
        rest = (rest_rows, rest_inverse)
        solved += made[: len(before)]
        made = made[len(before) :]
        for group, number in ((uppers, 0), (lefts, 1), (inverse_rows, 2)):
            group += made[number * len(ks) : (number + 1) * len(ks)]
        before = ks

    for gate in (uppers[0], uppers[-2]):
        second_sums = two.send(gate)
    scale = float(rows * n_rows) ** 0.5
    scratch = [(2, second_rows, NB), (width, width), (width, width), (NB, width), (rows, width), (NB, NB), (rows, NB)]
    return call(
        functools.partial(last_kernel, scale),
        "factor_last",
        (array(rows, width), array(cols, width)),
        scratch,
        *(scalars, *second_sums, own, other, *uppers, *lefts, *solved, *inverse_rows[before[0] :]),
    )


def solution(mesh):
    spec = P(("groups", "rows"), "tensor")
    return jax.shard_map(
        functools.partial(shards, mesh.shape["rows"]),
        mesh=mesh,
        in_specs=(spec,),
        out_specs=(spec, P("groups", "tensor")),
        check_vma=False,
    )
```

time: 77.8 us -> 75.2 us (0.967)
  waiting for transfers between devices: 25.1 us -> 18.5 us
  Pallas kernels: 31.6 us -> 36.5 us
  local copies, waits for them, and re-layouts: 2.21 us -> 1.17 us
    ppermute x10, waiting for transfers between devices: 23.6 us -> 16.6 us  [exchange(): return lax.ppermute(x, ('rows', 'tensor'), perm)]
    pallas_call x3 -> x7, Pallas kernels: 31.6 us -> 36.5 us  [call(): pl.pallas_call(kernel, out_shape=out_shape, in_specs=[smem if s else vmem...]
    ppermute x2, starting transfers between devices: 0.58 us -> 1.79 us  [sum_rows(): lax.ppermute(total, 'tensor', swap)]
    ppermute x10, starting transfers between devices: 16.6 us -> 15.4 us  [exchange(): return lax.ppermute(x, ('rows', 'tensor'), perm)]
    unnamed x6 -> x2, local copies, waits for them, and re-layouts: 2.09 us -> 1.04 us
  transfers between devices with their start and end apart: 15 -> 15, of which waited for: 10 -> 8; matrix products, arithmetic and copies ran while one was open for 0% -> 0% of each run, Pallas kernels for 3% -> 21%
where the time goes in v4:
time: 75.2 us; the launch traced here: 75 us
  Pallas kernels  36.5 us (49%)
  waiting for transfers between devices  18.5 us (25%)
  starting transfers between devices  17.8 us (24%)
  local copies, waits for them, and re-layouts  1.17 us (2%)
  between operations  0.76 us (1%)
    pallas_call x7, Pallas kernels, call(): pl.pallas_call(kernel, out_shape=out_shape, in_specs=[smem if s else vmem...  36.5 us
    ppermute x10, waiting for transfers between devices, exchange(): return lax.ppermute(x, ('rows', 'tensor'), perm)  16.6 us
    ppermute x10, starting transfers between devices, exchange(): return lax.ppermute(x, ('rows', 'tensor'), perm)  15.4 us
    ppermute x2, starting transfers between devices, sum_rows(): lax.ppermute(total, 'tensor', swap)  1.79 us
  transfers between devices with their start and end apart: 15, of which 8 were waited for; matrix products, arithmetic and copies ran while one was open for 0% of the time, Pallas kernels for 21%

profile of v4, /device:TPU:0, one launch (start us, length us, event | category | flops | bytes accessed | tf_op | source)
XLA Modules:
  0.0 75.0 jit_solution(12953394735866599836)
XLA Ops:
  0.6 0.5 collective-permute-start
  1.1 0.0 copy-start
  1.1 1.0 %copy-done = f32[256,512]{1,0:T(8,128)S(1)} copy-done((f32[256,512]{1,0:T(8,128)S(1)}, f32[256,512]{1,0:T(8,128)}, u32[]{:S(2)}) %copy-start) | copy-done | bytes 524312
  2.2 0.1 stack.23.s_ref
  2.3 0.6 collective-permute-done.other_ref.refs_5_
  2.9 1.6 %gram_second.1 = (f32[784,128]{1,0:T(8,128)S(1)}, f32[784,128]{1,0:T(8,128)S(1)}) custom-call(s32[5]{0:T(128)S(1)} %stack.23.s_ref, f32[256,512]{1,0:T(8,128)S(1)} %own_copy.1.own_ref.refs_4_, f32[256,512]{1,0:T(8,128)S(1)} %collective-permute-done.other_ref.refs_5_), custom_call_target="tpu_custom_call" | custom-call | tf_op jit(solution)/shard_map/gram_second/pallas_call | solution.py:449
  4.5 1.3 %gram_first.1 = (f32[272,128]{1,0:T(8,128)S(1)}, f32[272,128]{1,0:T(8,128)S(1)}) custom-call(s32[5]{0:T(128)S(1)} %stack.23.s_ref, f32[256,512]{1,0:T(8,128)S(1)} %own_copy.1.own_ref.refs_4_, f32[256,512]{1,0:T(8,128)S(1)} %collective-permute-done.other_ref.refs_5_), custom_call_target="tpu_custom_call" | custom-call | tf_op jit(solution)/shard_map/gram_first/pallas_call | solution.py:449
  5.8 3.0 %collective-permute-start.1 = (f32[784,128]{1,0:T(8,128)S(1)}, f32[784,128]{1,0:T(8,128)S(1)}, u32[]{:S(2)}, u32[]{:S(2)}) collective-permute-start(f32[784,128]{1,0:T(8,128)S(1)} %get-tuple-element.34), channel_id=1, source_target_pairs={{0,8},{2,6},{4,12},{6,2},{8,0},{10,14},{12,4},{14,10},{16,24},{18,... | collective-permute-start | bytes 1204232 | tf_op jit(solution)/shard_map/ppermute | solution.py:415
  8.8 1.5 %collective-permute-start.5 = (f32[272,128]{1,0:T(8,128)S(1)}, f32[272,128]{1,0:T(8,128)S(1)}, u32[]{:S(2)}, u32[]{:S(2)}) collective-permute-start(f32[272,128]{1,0:T(8,128)S(1)} %get-tuple-element.36), channel_id=1, source_target_pairs={{0,4},{2,10},{4,0},{6,14},{8,12},{10,2},{12,8},{14,6},{16,20},{18,... | collective-permute-start | bytes 417800 | tf_op jit(solution)/shard_map/ppermute | solution.py:415
  10.3 5.1 %collective-permute-done.5 = f32[272,128]{1,0:T(8,128)S(1)} collective-permute-done((f32[272,128]{1,0:T(8,128)S(1)}, f32[272,128]{1,0:T(8,128)S(1)}, u32[]{:S(2)}, u32[]{:S(2)}) %collective-permute-start.5) | collective-permute-done | bytes 139296 | tf_op jit(solution)/shard_map/ppermute | solution.py:415
  15.4 0.1 collective-permute-start.6
  15.5 0.6 collective-permute-done.1
  16.1 0.1 add.55
  16.2 1.4 %collective-permute-start.2 = (f32[392,128]{1,0:T(8,128)S(1)}, f32[392,128]{1,0:T(8,128)S(1)}, u32[]{:S(2)}, u32[]{:S(2)}) collective-permute-start(f32[392,128]{1,0:T(8,128)S(1)} %constant_dynamic-slice_fusion.1), channel_id=1, source_target_pairs={{0,4},{2,10},{4,0},{6,14},{8,12},{10,2},{12,8},{14,6},{16,20},{18,... | collective-permute-start | bytes 602120 | tf_op jit(solution)/shard_map/ppermute | solution.py:415
  17.6 2.9 %collective-permute-done.6 = f32[136,128]{1,0:T(8,128)S(1)} collective-permute-done((f32[136,128]{1,0:T(8,128)S(1)}, f32[136,128]{1,0:T(8,128)S(1)}, u32[]{:S(2)}, u32[]{:S(2)}) %collective-permute-start.6) | collective-permute-done | bytes 69664 | tf_op jit(solution)/shard_map/ppermute | solution.py:415
  20.5 2.6 %collective-permute-start.7 = (f32[136,128]{1,0:T(8,128)S(1)}, f32[136,128]{1,0:T(8,128)S(1)}, u32[]{:S(2)}, u32[]{:S(2)}) collective-permute-start(f32[136,128]{1,0:T(8,128)S(1)} %dynamic-slice_add_fusion.1), channel_id=1, source_target_pairs={{0,16},{2,18},{4,20},{6,22},{8,24},{10,26},{12,28},{14,30},{16,0},... | collective-permute-start | bytes 208904 | tf_op jit(solution)/shard_map/ppermute | solution.py:415
  23.1 2.6 %collective-permute-done.7 = f32[136,128]{1,0:T(8,128)S(1)} collective-permute-done((f32[136,128]{1,0:T(8,128)S(1)}, f32[136,128]{1,0:T(8,128)S(1)}, u32[]{:S(2)}, u32[]{:S(2)}) %collective-permute-start.7) | collective-permute-done | bytes 69664 | tf_op jit(solution)/shard_map/ppermute | solution.py:415
  25.8 0.1 collective-permute-start.8
  25.9 0.0 collective-permute-done.2
  25.9 2.6 %collective-permute-start.3 = (f32[392,128]{1,0:T(8,128)S(1)}, f32[392,128]{1,0:T(8,128)S(1)}, u32[]{:S(2)}, u32[]{:S(2)}) collective-permute-start(f32[392,128]{1,0:T(8,128)S(1)} %dynamic-slice_add_fusion), channel_id=1, source_target_pairs={{0,16},{2,18},{4,20},{6,22},{8,24},{10,26},{12,28},{14,30},{16,0},... | collective-permute-start | bytes 602120 | tf_op jit(solution)/shard_map/ppermute | solution.py:415
  28.5 2.4 %collective-permute-done.8 = f32[136,128]{1,0:T(8,128)S(1)} collective-permute-done((f32[136,128]{1,0:T(8,128)S(1)}, f32[136,128]{1,0:T(8,128)S(1)}, u32[]{:S(2)}, u32[]{:S(2)}) %collective-permute-start.8) | collective-permute-done | bytes 69664 | tf_op jit(solution)/shard_map/ppermute | solution.py:415
  31.0 3.8 %collective-permute-start.9 = (f32[272,128]{1,0:T(8,128)S(1)}, f32[272,128]{1,0:T(8,128)S(1)}, u32[]{:S(2)}, u32[]{:S(2)}) collective-permute-start(f32[272,128]{1,0:T(8,128)S(1)} %pad_maximum_fusion.1.p0), channel_id=1, source_target_pairs={{0,4},{2,10},{4,0},{6,14},{8,12},{10,2},{12,8},{14,6},{16,20},{18,... | collective-permute-start | bytes 417800 | tf_op jit(solution)/shard_map/ppermute | solution.py:415
  34.8 0.0 collective-permute-done.3
  34.8 0.1 collective-permute-start.4
  34.9 0.1 collective-permute-start.10
  35.0 2.8 %collective-permute-done.9.p1 = f32[272,128]{1,0:T(8,128)S(1)} collective-permute-done((f32[272,128]{1,0:T(8,128)S(1)}, f32[272,128]{1,0:T(8,128)S(1)}, u32[]{:S(2)}, u32[]{:S(2)}) %collective-permute-start.9) | collective-permute-done | bytes 139296 | tf_op jit(solution)/shard_map/ppermute | solution.py:415
  37.8 0.0 collective-permute-start.11
  37.8 0.0 collective-permute-done.10.p2
  37.8 1.4 %collective-permute-done.11.p3 = f32[272,128]{1,0:T(8,128)S(1)} collective-permute-done((f32[272,128]{1,0:T(8,128)S(1)}, f32[272,128]{1,0:T(8,128)S(1)}, u32[]{:S(2)}, u32[]{:S(2)}) %collective-permute-start.11) | collective-permute-done | bytes 139296 | tf_op jit(solution)/shard_map/ppermute | solution.py:438
  39.2 3.9 %factor_rows.3 = (f32[128,512]{1,0:T(8,128)S(1)}, bf16[128,768]{1,0:T(8,128)(2,1)S(1)}, f32[128,512]{1,0:T(8,128)S(1)}, f32[512,512]{1,0:T(8,128)S(1)}, f32[512,512]{1,0:T(8,128)S(1)}) custom-call(s32[5]{0:T(128)S(1)} %stack.23.s_ref, f32[272,128]{1,0:T(8,128)S(1)} %pad_maximum_fusion.1.p0, f32[272,128]{1,0:T(8,128)S(1)} %collective-permute-done.9.p1, ...), custom_call_target="tpu_custom_call" | custom-call | tf_op jit(solution)/shard_map/factor_rows/pallas_call | solution.py:449
  43.0 0.0 collective-permute-done.4
  43.0 0.1 broadcast_select_fusion.1
  43.1 0.3 collective-permute-start.12
  43.4 6.8 %factor_rows.4 = (f32[256,128]{1,0:T(8,128)S(1)}, f32[128,512]{1,0:T(8,128)S(1)}, f32[128,512]{1,0:T(8,128)S(1)}, bf16[128,1536]{1,0:T(8,128)(2,1)S(1)}, bf16[12...) custom-call(s32[5]{0:T(128)S(1)} %stack.23.s_ref, ...), custom_call_target="tpu_custom_call" | custom-call | tf_op jit(solution)/shard_map/factor_rows/pallas_call | solution.py:449
  50.2 1.7 %collective-permute-start.13 = (f32[784,128]{1,0:T(8,128)S(1)}, f32[784,128]{1,0:T(8,128)S(1)}, u32[]{:S(2)}, u32[]{:S(2)}) collective-permute-start(f32[784,128]{1,0:T(8,128)S(1)} %pad_maximum_fusion.refs_0_), channel_id=1, source_target_pairs={{0,2},{2,0},{1,3},{3,1},{4,6},{6,4},{5,7},{7,5},{8,10},{10,8},{9,1... | collective-permute-start | bytes 1204232 | tf_op jit(solution)/shard_map/ppermute | solution.py:438
  51.9 0.0 collective-permute-done.12.refs_1_
  51.9 0.1 collective-permute-start.14
  52.0 4.8 %factor_rows.5 = (f32[256,128]{1,0:T(8,128)S(1)}, f32[256,128]{1,0:T(8,128)S(1)}, f32[128,512]{1,0:T(8,128)S(1)}, bf16[128,3072]{1,0:T(8,128)(2,1)S(1)}, f32[128...) custom-call(s32[5]{0:T(128)S(1)} %stack.23.s_ref, f32[256,512]{1,0:T(8,128)S(1)} %own_copy.1.own_ref.refs_4_, ...), custom_call_target="tpu_custom_call" | custom-call | tf_op jit(solution)/shard_map/factor_rows/pallas_call | solution.py:449
  56.8 0.0 collective-permute-done.13.refs_2_
  56.8 0.0 collective-permute-done.14.refs_3_
  56.8 18.2 %factor_last.1 = (f32[256,512]{1,0:T(8,128)}, f32[1024,512]{1,0:T(8,128)}) custom-call(s32[5]{0:T(128)S(1)} %stack.23.s_ref, f32[784,128]{1,0:T(8,128)S(1)} %pad_maximum_fusion.refs_0_, f32[784,128]{1,0:T(8,128)S(1)} %collective-permute-done.12.refs_1_, f32[784,128]{1,0:T(8,128)S(1)} %collective-permute-done.13.refs_2_, ...), custom_call_target="tpu_custom_call" | custom-call | tf_op jit(solution)/shard_map/factor_last/pallas_call | solution.py:449
  (11 shorter events, 0.2 us)
Async XLA Ops:
  0.6 2.3 %collective-permute-start = (f32[256,512]{1,0:T(8,128)}, f32[256,512]{1,0:T(8,128)S(1)}, u32[]{:S(2)}, u32[]{:S(2)}) collective-permute-start(f32[256,512]{1,0:T(8,128)} %x_ref.1), channel_id=1, source_target_pairs={{0,2},{2,0},{1,3},{3,1},{4,6},{6,4},{5,7},{7,5},{8,10},{10,8},{9,1... | collective-permute-start | bytes 1572872 | tf_op jit(solution)/shard_map/ppermute | solution.py:468
  1.1 1.0 %copy-start = (f32[256,512]{1,0:T(8,128)S(1)}, f32[256,512]{1,0:T(8,128)}, u32[]{:S(2)}) copy-start(f32[256,512]{1,0:T(8,128)} %x_ref.1) | copy-start | bytes 1572868
  5.8 10.3 %collective-permute-start.1 = (f32[784,128]{1,0:T(8,128)S(1)}, f32[784,128]{1,0:T(8,128)S(1)}, u32[]{:S(2)}, u32[]{:S(2)}) collective-permute-start(f32[784,128]{1,0:T(8,128)S(1)} %get-tuple-element.34), channel_id=1, source_target_pairs={{0,8},{2,6},{4,12},{6,2},{8,0},{10,14},{12,4},{14,10},{16,24},{18,... | collective-permute-start | bytes 1204232 | tf_op jit(solution)/shard_map/ppermute | solution.py:415
  8.8 6.6 %collective-permute-start.5 = (f32[272,128]{1,0:T(8,128)S(1)}, f32[272,128]{1,0:T(8,128)S(1)}, u32[]{:S(2)}, u32[]{:S(2)}) collective-permute-start(f32[272,128]{1,0:T(8,128)S(1)} %get-tuple-element.36), channel_id=1, source_target_pairs={{0,4},{2,10},{4,0},{6,14},{8,12},{10,2},{12,8},{14,6},{16,20},{18,... | collective-permute-start | bytes 417800 | tf_op jit(solution)/shard_map/ppermute | solution.py:415
  15.4 5.1 %collective-permute-start.6 = (f32[136,128]{1,0:T(8,128)S(1)}, f32[136,128]{1,0:T(8,128)S(1)}, u32[]{:S(2)}, u32[]{:S(2)}) collective-permute-start(f32[136,128]{1,0:T(8,128)S(1)} %constant_dynamic-slice_fusion), channel_id=1, source_target_pairs={{0,8},{2,6},{4,12},{6,2},{8,0},{10,14},{12,4},{14,10},{16,24},{18,... | collective-permute-start | bytes 208904 | tf_op jit(solution)/shard_map/ppermute | solution.py:415
  16.2 9.7 %collective-permute-start.2 = (f32[392,128]{1,0:T(8,128)S(1)}, f32[392,128]{1,0:T(8,128)S(1)}, u32[]{:S(2)}, u32[]{:S(2)}) collective-permute-start(f32[392,128]{1,0:T(8,128)S(1)} %constant_dynamic-slice_fusion.1), channel_id=1, source_target_pairs={{0,4},{2,10},{4,0},{6,14},{8,12},{10,2},{12,8},{14,6},{16,20},{18,... | collective-permute-start | bytes 602120 | tf_op jit(solution)/shard_map/ppermute | solution.py:415
  20.5 5.3 %collective-permute-start.7 = (f32[136,128]{1,0:T(8,128)S(1)}, f32[136,128]{1,0:T(8,128)S(1)}, u32[]{:S(2)}, u32[]{:S(2)}) collective-permute-start(f32[136,128]{1,0:T(8,128)S(1)} %dynamic-slice_add_fusion.1), channel_id=1, source_target_pairs={{0,16},{2,18},{4,20},{6,22},{8,24},{10,26},{12,28},{14,30},{16,0},... | collective-permute-start | bytes 208904 | tf_op jit(solution)/shard_map/ppermute | solution.py:415
  25.8 5.2 %collective-permute-start.8 = (f32[136,128]{1,0:T(8,128)S(1)}, f32[136,128]{1,0:T(8,128)S(1)}, u32[]{:S(2)}, u32[]{:S(2)}) collective-permute-start(f32[136,128]{1,0:T(8,128)S(1)} %add.64), channel_id=1, source_target_pairs={{0,8},{2,6},{4,12},{6,2},{8,0},{10,14},{12,4},{14,10},{16,24},{18,... | collective-permute-start | bytes 208904 | tf_op jit(solution)/shard_map/ppermute | solution.py:415
  25.9 8.8 %collective-permute-start.3 = (f32[392,128]{1,0:T(8,128)S(1)}, f32[392,128]{1,0:T(8,128)S(1)}, u32[]{:S(2)}, u32[]{:S(2)}) collective-permute-start(f32[392,128]{1,0:T(8,128)S(1)} %dynamic-slice_add_fusion), channel_id=1, source_target_pairs={{0,16},{2,18},{4,20},{6,22},{8,24},{10,26},{12,28},{14,30},{16,0},... | collective-permute-start | bytes 602120 | tf_op jit(solution)/shard_map/ppermute | solution.py:415
  31.0 6.8 %collective-permute-start.9 = (f32[272,128]{1,0:T(8,128)S(1)}, f32[272,128]{1,0:T(8,128)S(1)}, u32[]{:S(2)}, u32[]{:S(2)}) collective-permute-start(f32[272,128]{1,0:T(8,128)S(1)} %pad_maximum_fusion.1.p0), channel_id=1, source_target_pairs={{0,4},{2,10},{4,0},{6,14},{8,12},{10,2},{12,8},{14,6},{16,20},{18,... | collective-permute-start | bytes 417800 | tf_op jit(solution)/shard_map/ppermute | solution.py:415
  34.8 8.2 %collective-permute-start.4 = (f32[392,128]{1,0:T(8,128)S(1)}, f32[392,128]{1,0:T(8,128)S(1)}, u32[]{:S(2)}, u32[]{:S(2)}) collective-permute-start(f32[392,128]{1,0:T(8,128)S(1)} %add.59), channel_id=1, source_target_pairs={{0,4},{2,10},{4,0},{6,14},{8,12},{10,2},{12,8},{14,6},{16,20},{18,... | collective-permute-start | bytes 602120 | tf_op jit(solution)/shard_map/ppermute | solution.py:415
  34.9 2.9 %collective-permute-start.10 = (f32[272,128]{1,0:T(8,128)S(1)}, f32[272,128]{1,0:T(8,128)S(1)}, u32[]{:S(2)}, u32[]{:S(2)}) collective-permute-start(f32[272,128]{1,0:T(8,128)S(1)} %pad_maximum_fusion.1.p0), channel_id=1, source_target_pairs={{0,2},{2,0},{1,3},{3,1},{4,6},{6,4},{5,7},{7,5},{8,10},{10,8},{9,1... | collective-permute-start | bytes 417800 | tf_op jit(solution)/shard_map/ppermute | solution.py:438
  37.8 1.4 %collective-permute-start.11 = (f32[272,128]{1,0:T(8,128)S(1)}, f32[272,128]{1,0:T(8,128)S(1)}, u32[]{:S(2)}, u32[]{:S(2)}) collective-permute-start(f32[272,128]{1,0:T(8,128)S(1)} %collective-permute-done.9.p1), channel_id=1, source_target_pairs={{0,2},{2,0},{1,3},{3,1},{4,6},{6,4},{5,7},{7,5},{8,10},{10,8},{9,1... | collective-permute-start | bytes 417800 | tf_op jit(solution)/shard_map/ppermute | solution.py:438
  43.1 8.8 %collective-permute-start.12 = (f32[784,128]{1,0:T(8,128)S(1)}, f32[784,128]{1,0:T(8,128)S(1)}, u32[]{:S(2)}, u32[]{:S(2)}) collective-permute-start(f32[784,128]{1,0:T(8,128)S(1)} %pad_maximum_fusion.refs_0_), channel_id=1, source_target_pairs={{0,8},{2,6},{4,12},{6,2},{8,0},{10,14},{12,4},{14,10},{16,24},{18,... | collective-permute-start | bytes 1204232 | tf_op jit(solution)/shard_map/ppermute | solution.py:415
  50.2 6.6 %collective-permute-start.13 = (f32[784,128]{1,0:T(8,128)S(1)}, f32[784,128]{1,0:T(8,128)S(1)}, u32[]{:S(2)}, u32[]{:S(2)}) collective-permute-start(f32[784,128]{1,0:T(8,128)S(1)} %pad_maximum_fusion.refs_0_), channel_id=1, source_target_pairs={{0,2},{2,0},{1,3},{3,1},{4,6},{6,4},{5,7},{7,5},{8,10},{10,8},{9,1... | collective-permute-start | bytes 1204232 | tf_op jit(solution)/shard_map/ppermute | solution.py:438
  51.9 4.9 %collective-permute-start.14 = (f32[784,128]{1,0:T(8,128)S(1)}, f32[784,128]{1,0:T(8,128)S(1)}, u32[]{:S(2)}, u32[]{:S(2)}) collective-permute-start(f32[784,128]{1,0:T(8,128)S(1)} %collective-permute-done.12.refs_1_), channel_id=1, source_target_pairs={{0,2},{2,0},{1,3},{3,1},{4,6},{6,4},{5,7},{7,5},{8,10},{10,8},{9,1... | collective-permute-start | bytes 1204232 | tf_op jit(solution)/shard_map/ppermute | solution.py:438

commit v5 on v4

--- a/solution.py
+++ b/solution.py
@@ -32,6 +32,15 @@
 
 def product(left, right):
     return jnp.dot(left, right, preferred_element_type=F32)
+
+
+def column_parts(x):
+    h, m, l = split(x)
+    return jnp.concatenate([h, h, m, m, h, l], axis=0), jnp.concatenate([h, m, h, m, l, h], axis=0)
+
+
+def product_of_columns(left, right):
+    return lax.dot_general(left, right, (((0,), (0,)), ((), ())), preferred_element_type=F32)
 
 
 def row_of(x, k):
@@ -86,7 +95,12 @@
     return pivots, taken
 
 
-def factor_block(rows, put_upper, put_inverse):
+def run_share(pending, turns):
+    for _ in range(-(-len(pending) // turns)):
+        pending.pop(0)()
+
+
+def factor_block(rows, put_upper, put_inverse, pending):
     lane = lax.broadcasted_iota(jnp.int32, (SUB, NB), 1)
     sub = lax.broadcasted_iota(jnp.int32, (SUB, NB), 0)
     mine = [sub == k for k in range(SUB)]
@@ -105,6 +119,7 @@
         col1 = [lane_of(rows[g + 1], b + k) for k in range(2 * SUB)]
         near = range(g + 2, min(count, g + 4))
         factors = {h: [lane_of(rows[h], b + k) for k in range(2 * SUB)] for h in near}
+        run_share(pending, (count - g) // 2)
         group = (lane >= b) & (lane < b + 2 * SUB)
         a = [rows[g], rows[g + 1]]
         w = [
@@ -248,7 +263,7 @@
         out_ref[core, pl.ds(pl.multiple_of(which * size, SUB), size), :] = ref[...]
 
 
-def factor_step(k, n, read, upper_ref, inv_ref, write):
+def factor_step(k, n, read, upper_ref, inv_ref, write, pending):
     source = read(k, k)
 
     def put_upper(g, v):
@@ -257,57 +272,76 @@
     def put_inverse(g, v):
         inv_ref[at(g, SUB), :] = v
 
-    factor_block([source[at(h, SUB), :] for h in range(NB // SUB)], put_upper, put_inverse)
+    factor_block([source[at(h, SUB), :] for h in range(NB // SUB)], put_upper, put_inverse, pending)
     if k:
         upper_ref[:, : k * NB] = jnp.zeros((NB, k * NB), F32)
     inverse = inv_ref[...]
     lowers, rights = {}, {}
     if k + 1 < n:
         inverse_left = left_parts(inverse)
-        for j in range(k + 1, n):
+
+        def upper_block(j):
             upper = product(inverse_left, right_parts(read(k, j)))
-            lowers[j] = left_parts(upper.T)
-            rights[j] = right_parts(upper)
+            lowers[j], rights[j] = column_parts(upper)
             upper_ref[:, at(j)] = upper
-        for i in range(k + 1, n):
-            update = product(lowers[i], jnp.concatenate([rights[j] for j in range(i, n)], axis=1))
-            for j in range(i, n):
-                write(i, j, read(i, j) - update[:, at(j - i)])
+
+        def update(i, columns):
+            change = product_of_columns(lowers[i], jnp.concatenate([rights[j] for j in columns], axis=1))
+            for number, j in enumerate(columns):
+                write(i, j, read(i, j) - change[:, at(number)])
+
+        upper_block(k + 1)
+        update(k + 1, [k + 1])
+        pending += [functools.partial(upper_block, j) for j in range(k + 2, n)]
+        if k + 2 < n:
+            pending.append(functools.partial(update, k + 1, range(k + 2, n)))
+        pending += [functools.partial(update, i, range(i, n)) for i in range(k + 2, n)]
     return inverse, lowers, rights
 
 
-def invert_step(k, n, inverse, lowers, read, write, out_ref):
-    left = left_parts(inverse)
-    row = [product(left, right_parts(read(k, j))) for j in range(k)] + [inverse]
-    for j, block in enumerate(row):
-        out_ref[:, at(j)] = block
-    if k + 1 < n:
-        out_ref[:, (k + 1) * NB :] = jnp.zeros((NB, (n - k - 1) * NB), F32)
-        right = right_parts(jnp.concatenate(row, axis=1))
-        for i in range(k + 1, n):
-            update = product(lowers[i], right)
-            for j in range(k + 1):
-                write(i, j, (read(i, j) if j < k else F32(0)) - update[:, at(j)])
+def invert_step(k, n, inverse, lowers, read, write, out_ref, left_ref, pending):
+    right = []
+
+    def own_row():
+        left = left_parts(inverse)
+        row = [product(left, right_parts(read(k, j))) for j in range(k)] + [inverse]
+        for j, block in enumerate(row):
+            out_ref[:, at(j)] = block
+        if k + 1 < n:
+            out_ref[:, (k + 1) * NB :] = jnp.zeros((NB, (n - k - 1) * NB), F32)
+        row = jnp.concatenate(row, axis=1)
+        right.append(right_parts(row))
+        left_ref[...] = left_parts(row)
+
+    def update(i):
+        change = product_of_columns(lowers[i], right[0])
+        for j in range(k + 1):
+            write(i, j, (read(i, j) if j < k else F32(0)) - change[:, at(j)])
+
+    pending.append(own_row)
+    pending += [functools.partial(update, i) for i in range(k + 1, n)]
 
 
 def solve_columns(first, own_ref, other_ref, row_refs, out_refs, start):
-    for k, row_ref, out_ref in zip(range(start, start + len(row_refs)), row_refs, out_refs):
+    def column(k, row_ref, out_ref):
         depth = (k + 1) * NB
         effects = jnp.where(first, own_ref[:, :depth], other_ref[:, :depth])
         out_ref[...] = product(left_parts(effects), right_parts(row_ref[:, :depth].T))
+
+    return [functools.partial(column, k, *refs) for k, *refs in zip(range(start, start + len(row_refs)), row_refs, out_refs)]
 
 
 def start_kernel(ks, s_ref, p0, p1, p2, p3, *refs):
     sums_ref = refs[-1]
     n = refs[0].shape[1] // NB
     gather_halves(s_ref[0], s_ref, 1, (p0, p1, p2, p3), sums_ref)
-    row_steps(ks, n, square_blocks(sums_ref, 0, n), None, *refs[:-1])
+    row_steps(ks, n, square_blocks(sums_ref, 0, n), None, [], *refs[:-1])
 
 
 def next_kernel(ks, before, s_ref, own_ref, other_ref, *refs):
     row_refs, (rest_in, inv_rest_in), refs = refs[: len(before)], refs[len(before) : len(before) + 2], refs[len(before) + 2 :]
     n = own_ref.shape[1] // NB
-    solve_columns(s_ref[0] == 0, own_ref, other_ref, row_refs, refs[: len(before)], before[0])
+    pending = solve_columns(s_ref[0] == 0, own_ref, other_ref, row_refs, refs[: len(before)], before[0])
 
     def gram(i, j):
         return rest_in[at(i), at(j)]
@@ -315,10 +349,10 @@
     def inv_gram(i, j):
         return inv_rest_in[at(i), at(j)]
 
-    row_steps(ks, n, gram, inv_gram, *refs[len(before) :])
-
-
-def row_steps(ks, n, gram, inv_gram, *refs):
+    row_steps(ks, n, gram, inv_gram, pending, *refs[len(before) :])
+
+
+def row_steps(ks, n, gram, inv_gram, pending, *refs):
     rest_ref, inv_rest_ref, inv_ref = refs[3 * len(ks) :]
 
     def rest(i, j):
@@ -329,19 +363,19 @@
 
     for number, k in enumerate(ks):
         sources = (gram, inv_gram) if number == 0 else (rest, inv_rest)
-        one_step(k, n, *sources, *refs[number : 3 * len(ks) : len(ks)], rest_ref, inv_rest_ref, inv_ref)
-
-
-def one_step(k, n, gram, inv_gram, upper_ref, left_ref, row_ref, rest_ref, inv_rest_ref, inv_ref):
+        one_step(k, n, *sources, pending, *refs[number : 3 * len(ks) : len(ks)], rest_ref, inv_rest_ref, inv_ref)
+    run_share(pending, 1)
+
+
+def one_step(k, n, gram, inv_gram, pending, upper_ref, left_ref, row_ref, rest_ref, inv_rest_ref, inv_ref):
     def write(i, j, v):
         rest_ref[at(i), at(j)] = v
 
     def inv_write(i, j, v):
         inv_rest_ref[at(i), at(j)] = v
 
-    inverse, lowers, _ = factor_step(k, n, gram, upper_ref, inv_ref, write)
-    invert_step(k, n, inverse, lowers, inv_gram, inv_write, row_ref)
-    left_ref[...] = left_parts(row_ref[:, : (k + 1) * NB])
+    inverse, lowers, _ = factor_step(k, n, gram, upper_ref, inv_ref, write, pending)
+    invert_step(k, n, inverse, lowers, inv_gram, inv_write, row_ref, left_ref, pending)
 
 
 def last_kernel(scale, s_ref, *refs):
@@ -353,46 +387,60 @@
     t = s_ref[0]
     gather_halves(t, s_ref, 3, parts, sums_ref)
     gram = square_blocks(sums_ref, n * (n // 2) * NB, n)
-    inverse_lefts = [ref[...] for ref in left_refs]
-    lowers, rights = [], []
-    for j in range(n):
+    first = t == 0
+    lowers, rights = {}, {}
+
+    def cross_column(j):
         core, col = divmod(j, n // 2)
         parts = split(jnp.concatenate([sums_ref[core, at(i * (n // 2) + col), :] for i in range(n)], axis=0))
         column = []
         for k in range(n):
             h, m, l = (x[: (k + 1) * NB, :] for x in parts)
-            column.append(product(inverse_lefts[k], jnp.concatenate([h, m, h, m, l, h], axis=0)))
+            column.append(product(left_refs[k][...], jnp.concatenate([h, m, h, m, l, h], axis=0)))
             cross_upper_ref[at(k), at(j)] = column[k]
         column = jnp.concatenate(column, axis=0)
-        lowers.append(left_parts(column.T))
-        rights.append(right_parts(column))
-    for i in range(n):
-        update = product(lowers[i], jnp.concatenate(rights[i:], axis=1))
-        for j in range(i, n):
-            work_ref[at(i), at(j)] = gram(i, j) - update[:, at(j - i)]
-    solve_columns(t == 0, own_ref, other_ref, [inv_row_ref], [column_ref], n - 1)
-    first_refs = (*first_refs, column_ref)
-    solved = jnp.concatenate([ref[...] for ref in first_refs], axis=1)
-    effects = jnp.where(t == 0, other_ref[...], own_ref[...])
-    e_ref[...] = effects - product(left_parts(solved), jnp.concatenate(rights, axis=1))
-
-    def read(i, j):
-        return work_ref[at(i), at(j)]
-
-    def write(i, j, v):
-        work_ref[at(i), at(j)] = v
-
-    first = t == 0
-    for k in range(n):
+        lowers[j], rights[j] = column_parts(column)
+
+    def take_off(i, columns):
+        change = product_of_columns(lowers[i], jnp.concatenate([rights[j] for j in columns], axis=1))
+        for number, j in enumerate(columns):
+            work_ref[at(i), at(j)] = gram(i, j) - change[:, at(number)]
+
+    def take_off_effects():
+        solved = jnp.concatenate([ref[...] for ref in (*first_refs, column_ref)], axis=1)
+        effects = jnp.where(first, other_ref[...], own_ref[...])
+        e_ref[...] = effects - product(left_parts(solved), jnp.concatenate([rights[j] for j in range(n)], axis=1))
+
+    def upper_rows(k):
         tri_ref[at(k), :] = jnp.where(first, upper_refs[k][...], cross_upper_ref[at(k), :]) * (1.0 / scale)
-    for k in range(n):
-        inverse, _, rights = factor_step(k, n, read, row_ref, inv_ref, write)
+
+    def solve_effects(k, inverse, rights):
         solved = product(left_parts(e_ref[:, at(k)]), right_parts(inverse.T))
         if k + 1 < n:
             later = jnp.concatenate([rights[j] for j in range(k + 1, n)], axis=1)
             e_ref[:, (k + 1) * NB :] -= product(left_parts(solved), later)
-        basis_ref[:, at(k)] = jnp.where(first, first_refs[k][...], solved) * scale
-        tri_ref[at(n + k), :] = jnp.where(first, F32(0), row_ref[...] * (1.0 / scale))
+        done = first_refs[k] if k + 1 < n else column_ref
+        basis_ref[:, at(k)] = jnp.where(first, done[...], solved) * scale
+        tri_ref[at(n + k), :] = jnp.where(first, F32(0), row_ref[k % 2] * (1.0 / scale))
+
+    def read(i, j):
+        return work_ref[at(i), at(j)]
+
+    def write(i, j, v):
+        work_ref[at(i), at(j)] = v
+
+    cross_column(0)
+    take_off(0, [0])
+    pending = [functools.partial(cross_column, j) for j in range(1, n)]
+    pending.append(functools.partial(take_off, 0, range(1, n)))
+    pending += [functools.partial(take_off, i, range(i, n)) for i in range(1, n)]
+    pending += solve_columns(first, own_ref, other_ref, [inv_row_ref], [column_ref], n - 1)
+    pending.append(take_off_effects)
+    pending += [functools.partial(upper_rows, k) for k in range(n)]
+    for k in range(n):
+        inverse, _, row_rights = factor_step(k, n, read, row_ref.at[k % 2], inv_ref, write, pending)
+        pending.append(functools.partial(solve_effects, k, inverse, row_rights))
+    run_share(pending, 1)
 
 
 def shards(n_rows, effects):
@@ -488,15 +536,17 @@
         columns = [array(rows, NB) for _ in before]
         out = [array(NB, width) for _ in ks]
         out += [jax.ShapeDtypeStruct((NB, 6 * (k + 1) * NB), BF16) for k in ks]
-        out += [array(NB, width) for _ in ks] + [array(width, width), array(width, width)]
+        out += [array(NB, width) for _ in ks]
+        final = ks[-1] == half - 1
+        out += [] if final else [array(width, width), array(width, width)]
         if before:
-            kernel, scratch = functools.partial(next_kernel, ks, before), [(NB, NB)]
+            kernel, scratch = functools.partial(next_kernel, ks, before), ([(SUB, NB)] * 2 if final else []) + [(NB, NB)]
             args = (scalars, own, other, *inverse_rows[before[0] :], *rest)
         else:
             kernel, scratch = functools.partial(start_kernel, ks), [(NB, NB), (2, first_rows, NB)]
             args = (scalars, *rest)
-        *made, rest_rows, rest_inverse = call(kernel, "factor_rows", columns + out, scratch, *args)
-        rest = (rest_rows, rest_inverse)
+        made = call(kernel, "factor_rows", columns + out, scratch, *args)
+        rest = made[-2:]
         solved += made[: len(before)]
         made = made[len(before) :]
         for group, number in ((uppers, 0), (lefts, 1), (inverse_rows, 2)):
@@ -506,7 +556,7 @@
     for gate in (uppers[0], uppers[-2]):
         second_sums = two.send(gate)
     scale = float(rows * n_rows) ** 0.5
-    scratch = [(2, second_rows, NB), (width, width), (width, width), (NB, width), (rows, width), (NB, NB), (rows, NB)]
+    scratch = [(2, second_rows, NB), (width, width), (width, width), (2, NB, width), (rows, width), (NB, NB), (rows, NB)]
     return call(
         functools.partial(last_kernel, scale),
         "factor_last",

time: 75.2 us -> 74 us (0.984)
  Pallas kernels: 36.5 us -> 35.3 us
    pallas_call x7, Pallas kernels: 36.5 us -> 35.3 us  [call(): pl.pallas_call(kernel, out_shape=out_shape, in_specs=[smem if s else vmem...]
  transfers between devices with their start and end apart: 15 -> 15, of which waited for: 8 -> 8; matrix products, arithmetic and copies ran while one was open for 0% -> 0% of each run, Pallas kernels for 21% -> 20%
where the time goes in v5:
time: 74 us; the launch traced here: 73.8 us
  Pallas kernels  35.3 us (48%)
  waiting for transfers between devices  18.5 us (25%)
  starting transfers between devices  17.8 us (24%)
  local copies, waits for them, and re-layouts  1.17 us (2%)
  between operations  0.79 us (1%)
    pallas_call x7, Pallas kernels, call(): pl.pallas_call(kernel, out_shape=out_shape, in_specs=[smem if s else vmem...  35.3 us
    ppermute x10, waiting for transfers between devices, exchange(): return lax.ppermute(x, ('rows', 'tensor'), perm)  16.6 us
    ppermute x10, starting transfers between devices, exchange(): return lax.ppermute(x, ('rows', 'tensor'), perm)  15.4 us
    ppermute x2, starting transfers between devices, sum_rows(): lax.ppermute(total, 'tensor', swap)  1.8 us
  transfers between devices with their start and end apart: 15, of which 8 were waited for; matrix products, arithmetic and copies ran while one was open for 0% of the time, Pallas kernels for 20%

profile of v5, /device:TPU:0, one launch (start us, length us, event | category | flops | bytes accessed | tf_op | source)
XLA Modules:
  0.0 73.8 jit_solution(18339584859896826742)
XLA Ops:
  0.6 0.5 collective-permute-start
  1.1 0.0 copy-start
  1.1 1.0 %copy-done = f32[256,512]{1,0:T(8,128)S(1)} copy-done((f32[256,512]{1,0:T(8,128)S(1)}, f32[256,512]{1,0:T(8,128)}, u32[]{:S(2)}) %copy-start) | copy-done | bytes 524312
  2.2 0.1 stack.23.s_ref
  2.3 0.6 collective-permute-done.other_ref.refs_5_
  2.9 1.6 %gram_second.1 = (f32[784,128]{1,0:T(8,128)S(1)}, f32[784,128]{1,0:T(8,128)S(1)}) custom-call(s32[5]{0:T(128)S(1)} %stack.23.s_ref, f32[256,512]{1,0:T(8,128)S(1)} %own_copy.1.own_ref.refs_4_, f32[256,512]{1,0:T(8,128)S(1)} %collective-permute-done.other_ref.refs_5_), custom_call_target="tpu_custom_call" | custom-call | tf_op jit(solution)/shard_map/gram_second/pallas_call | solution.py:497
  4.5 1.3 %gram_first.1 = (f32[272,128]{1,0:T(8,128)S(1)}, f32[272,128]{1,0:T(8,128)S(1)}) custom-call(s32[5]{0:T(128)S(1)} %stack.23.s_ref, f32[256,512]{1,0:T(8,128)S(1)} %own_copy.1.own_ref.refs_4_, f32[256,512]{1,0:T(8,128)S(1)} %collective-permute-done.other_ref.refs_5_), custom_call_target="tpu_custom_call" | custom-call | tf_op jit(solution)/shard_map/gram_first/pallas_call | solution.py:497
  5.8 3.0 %collective-permute-start.1 = (f32[784,128]{1,0:T(8,128)S(1)}, f32[784,128]{1,0:T(8,128)S(1)}, u32[]{:S(2)}, u32[]{:S(2)}) collective-permute-start(f32[784,128]{1,0:T(8,128)S(1)} %get-tuple-element.34), channel_id=1, source_target_pairs={{0,8},{2,6},{4,12},{6,2},{8,0},{10,14},{12,4},{14,10},{16,24},{18,... | collective-permute-start | bytes 1204232 | tf_op jit(solution)/shard_map/ppermute | solution.py:463
  8.8 1.5 %collective-permute-start.5 = (f32[272,128]{1,0:T(8,128)S(1)}, f32[272,128]{1,0:T(8,128)S(1)}, u32[]{:S(2)}, u32[]{:S(2)}) collective-permute-start(f32[272,128]{1,0:T(8,128)S(1)} %get-tuple-element.36), channel_id=1, source_target_pairs={{0,4},{2,10},{4,0},{6,14},{8,12},{10,2},{12,8},{14,6},{16,20},{18,... | collective-permute-start | bytes 417800 | tf_op jit(solution)/shard_map/ppermute | solution.py:463
  10.3 5.1 %collective-permute-done.5 = f32[272,128]{1,0:T(8,128)S(1)} collective-permute-done((f32[272,128]{1,0:T(8,128)S(1)}, f32[272,128]{1,0:T(8,128)S(1)}, u32[]{:S(2)}, u32[]{:S(2)}) %collective-permute-start.5) | collective-permute-done | bytes 139296 | tf_op jit(solution)/shard_map/ppermute | solution.py:463
  15.4 0.1 collective-permute-start.6
  15.5 0.6 collective-permute-done.1
  16.1 0.1 add.55
  16.2 1.4 %collective-permute-start.2 = (f32[392,128]{1,0:T(8,128)S(1)}, f32[392,128]{1,0:T(8,128)S(1)}, u32[]{:S(2)}, u32[]{:S(2)}) collective-permute-start(f32[392,128]{1,0:T(8,128)S(1)} %constant_dynamic-slice_fusion.1), channel_id=1, source_target_pairs={{0,4},{2,10},{4,0},{6,14},{8,12},{10,2},{12,8},{14,6},{16,20},{18,... | collective-permute-start | bytes 602120 | tf_op jit(solution)/shard_map/ppermute | solution.py:463
  17.6 2.9 %collective-permute-done.6 = f32[136,128]{1,0:T(8,128)S(1)} collective-permute-done((f32[136,128]{1,0:T(8,128)S(1)}, f32[136,128]{1,0:T(8,128)S(1)}, u32[]{:S(2)}, u32[]{:S(2)}) %collective-permute-start.6) | collective-permute-done | bytes 69664 | tf_op jit(solution)/shard_map/ppermute | solution.py:463
  20.5 2.6 %collective-permute-start.7 = (f32[136,128]{1,0:T(8,128)S(1)}, f32[136,128]{1,0:T(8,128)S(1)}, u32[]{:S(2)}, u32[]{:S(2)}) collective-permute-start(f32[136,128]{1,0:T(8,128)S(1)} %dynamic-slice_add_fusion.1), channel_id=1, source_target_pairs={{0,16},{2,18},{4,20},{6,22},{8,24},{10,26},{12,28},{14,30},{16,0},... | collective-permute-start | bytes 208904 | tf_op jit(solution)/shard_map/ppermute | solution.py:463
  23.1 2.6 %collective-permute-done.7 = f32[136,128]{1,0:T(8,128)S(1)} collective-permute-done((f32[136,128]{1,0:T(8,128)S(1)}, f32[136,128]{1,0:T(8,128)S(1)}, u32[]{:S(2)}, u32[]{:S(2)}) %collective-permute-start.7) | collective-permute-done | bytes 69664 | tf_op jit(solution)/shard_map/ppermute | solution.py:463
  25.8 0.1 collective-permute-start.8
  25.9 0.0 collective-permute-done.2
  25.9 2.6 %collective-permute-start.3 = (f32[392,128]{1,0:T(8,128)S(1)}, f32[392,128]{1,0:T(8,128)S(1)}, u32[]{:S(2)}, u32[]{:S(2)}) collective-permute-start(f32[392,128]{1,0:T(8,128)S(1)} %dynamic-slice_add_fusion), channel_id=1, source_target_pairs={{0,16},{2,18},{4,20},{6,22},{8,24},{10,26},{12,28},{14,30},{16,0},... | collective-permute-start | bytes 602120 | tf_op jit(solution)/shard_map/ppermute | solution.py:463
  28.5 2.4 %collective-permute-done.8 = f32[136,128]{1,0:T(8,128)S(1)} collective-permute-done((f32[136,128]{1,0:T(8,128)S(1)}, f32[136,128]{1,0:T(8,128)S(1)}, u32[]{:S(2)}, u32[]{:S(2)}) %collective-permute-start.8) | collective-permute-done | bytes 69664 | tf_op jit(solution)/shard_map/ppermute | solution.py:463
  31.0 3.8 %collective-permute-start.9 = (f32[272,128]{1,0:T(8,128)S(1)}, f32[272,128]{1,0:T(8,128)S(1)}, u32[]{:S(2)}, u32[]{:S(2)}) collective-permute-start(f32[272,128]{1,0:T(8,128)S(1)} %pad_maximum_fusion.1.p0), channel_id=1, source_target_pairs={{0,4},{2,10},{4,0},{6,14},{8,12},{10,2},{12,8},{14,6},{16,20},{18,... | collective-permute-start | bytes 417800 | tf_op jit(solution)/shard_map/ppermute | solution.py:463
  34.8 0.0 collective-permute-done.3
  34.8 0.1 collective-permute-start.4
  34.9 0.1 collective-permute-start.10
  35.0 2.8 %collective-permute-done.9.p1 = f32[272,128]{1,0:T(8,128)S(1)} collective-permute-done((f32[272,128]{1,0:T(8,128)S(1)}, f32[272,128]{1,0:T(8,128)S(1)}, u32[]{:S(2)}, u32[]{:S(2)}) %collective-permute-start.9) | collective-permute-done | bytes 139296 | tf_op jit(solution)/shard_map/ppermute | solution.py:463
  37.8 0.0 collective-permute-start.11
  37.8 0.0 collective-permute-done.10.p2
  37.8 1.4 %collective-permute-done.11.p3 = f32[272,128]{1,0:T(8,128)S(1)} collective-permute-done((f32[272,128]{1,0:T(8,128)S(1)}, f32[272,128]{1,0:T(8,128)S(1)}, u32[]{:S(2)}, u32[]{:S(2)}) %collective-permute-start.11) | collective-permute-done | bytes 139296 | tf_op jit(solution)/shard_map/ppermute | solution.py:486
  39.2 4.1 %factor_rows.3 = (f32[128,512]{1,0:T(8,128)S(1)}, bf16[128,768]{1,0:T(8,128)(2,1)S(1)}, f32[128,512]{1,0:T(8,128)S(1)}, f32[512,512]{1,0:T(8,128)S(1)}, f32[512,512]{1,0:T(8,128)S(1)}) custom-call(s32[5]{0:T(128)S(1)} %stack.23.s_ref, f32[272,128]{1,0:T(8,128)S(1)} %pad_maximum_fusion.1.p0, f32[272,128]{1,0:T(8,128)S(1)} %collective-permute-done.9.p1, ...), custom_call_target="tpu_custom_call" | custom-call | tf_op jit(solution)/shard_map/factor_rows/pallas_call | solution.py:497
  43.3 0.0 collective-permute-done.4
  43.3 0.1 broadcast_select_fusion.1
  43.4 0.3 collective-permute-start.12
  43.6 6.7 %factor_rows.4 = (f32[256,128]{1,0:T(8,128)S(1)}, f32[128,512]{1,0:T(8,128)S(1)}, f32[128,512]{1,0:T(8,128)S(1)}, bf16[128,1536]{1,0:T(8,128)(2,1)S(1)}, bf16[12...) custom-call(s32[5]{0:T(128)S(1)} %stack.23.s_ref, ...), custom_call_target="tpu_custom_call" | custom-call | tf_op jit(solution)/shard_map/factor_rows/pallas_call | solution.py:497
  50.4 1.7 %collective-permute-start.13 = (f32[784,128]{1,0:T(8,128)S(1)}, f32[784,128]{1,0:T(8,128)S(1)}, u32[]{:S(2)}, u32[]{:S(2)}) collective-permute-start(f32[784,128]{1,0:T(8,128)S(1)} %pad_maximum_fusion.refs_0_), channel_id=1, source_target_pairs={{0,2},{2,0},{1,3},{3,1},{4,6},{6,4},{5,7},{7,5},{8,10},{10,8},{9,1... | collective-permute-start | bytes 1204232 | tf_op jit(solution)/shard_map/ppermute | solution.py:486
  52.1 0.0 collective-permute-done.12.refs_1_
  52.1 0.1 collective-permute-start.14
  52.2 3.6 %factor_rows.5 = (f32[256,128]{1,0:T(8,128)S(1)}, f32[256,128]{1,0:T(8,128)S(1)}, f32[128,512]{1,0:T(8,128)S(1)}, bf16[128,3072]{1,0:T(8,128)(2,1)S(1)}, f32[128,512]{1,0:T(8,128)S(1)}) custom-call(s32[5]{0:T(128)S(1)} %stack.23.s_ref, f32[256,512]{1,0:T(8,128)S(1)} %own_copy.1.own_ref.refs_4_, f32[256,512]{1,0:T(8,128)S(1)} %collective-permute-done.other_ref.refs_5_, ...), custom_call_target="tpu_custom_call" | custom-call | tf_op jit(solution)/shard_map/factor_rows/pallas_call | solution.py:497
  55.8 0.0 collective-permute-done.13.refs_2_
  55.8 0.0 collective-permute-done.14.refs_3_
  55.8 18.0 %factor_last.1 = (f32[256,512]{1,0:T(8,128)}, f32[1024,512]{1,0:T(8,128)}) custom-call(s32[5]{0:T(128)S(1)} %stack.23.s_ref, f32[784,128]{1,0:T(8,128)S(1)} %pad_maximum_fusion.refs_0_, f32[784,128]{1,0:T(8,128)S(1)} %collective-permute-done.12.refs_1_, f32[784,128]{1,0:T(8,128)S(1)} %collective-permute-done.13.refs_2_, ...), custom_call_target="tpu_custom_call" | custom-call | tf_op jit(solution)/shard_map/factor_last/pallas_call | solution.py:497
  (11 shorter events, 0.2 us)
Async XLA Ops:
  0.6 2.3 %collective-permute-start = (f32[256,512]{1,0:T(8,128)}, f32[256,512]{1,0:T(8,128)S(1)}, u32[]{:S(2)}, u32[]{:S(2)}) collective-permute-start(f32[256,512]{1,0:T(8,128)} %x_ref.1), channel_id=1, source_target_pairs={{0,2},{2,0},{1,3},{3,1},{4,6},{6,4},{5,7},{7,5},{8,10},{10,8},{9,1... | collective-permute-start | bytes 1572872 | tf_op jit(solution)/shard_map/ppermute | solution.py:516
  1.1 1.0 %copy-start = (f32[256,512]{1,0:T(8,128)S(1)}, f32[256,512]{1,0:T(8,128)}, u32[]{:S(2)}) copy-start(f32[256,512]{1,0:T(8,128)} %x_ref.1) | copy-start | bytes 1572868
  5.8 10.3 %collective-permute-start.1 = (f32[784,128]{1,0:T(8,128)S(1)}, f32[784,128]{1,0:T(8,128)S(1)}, u32[]{:S(2)}, u32[]{:S(2)}) collective-permute-start(f32[784,128]{1,0:T(8,128)S(1)} %get-tuple-element.34), channel_id=1, source_target_pairs={{0,8},{2,6},{4,12},{6,2},{8,0},{10,14},{12,4},{14,10},{16,24},{18,... | collective-permute-start | bytes 1204232 | tf_op jit(solution)/shard_map/ppermute | solution.py:463
  8.8 6.6 %collective-permute-start.5 = (f32[272,128]{1,0:T(8,128)S(1)}, f32[272,128]{1,0:T(8,128)S(1)}, u32[]{:S(2)}, u32[]{:S(2)}) collective-permute-start(f32[272,128]{1,0:T(8,128)S(1)} %get-tuple-element.36), channel_id=1, source_target_pairs={{0,4},{2,10},{4,0},{6,14},{8,12},{10,2},{12,8},{14,6},{16,20},{18,... | collective-permute-start | bytes 417800 | tf_op jit(solution)/shard_map/ppermute | solution.py:463
  15.4 5.1 %collective-permute-start.6 = (f32[136,128]{1,0:T(8,128)S(1)}, f32[136,128]{1,0:T(8,128)S(1)}, u32[]{:S(2)}, u32[]{:S(2)}) collective-permute-start(f32[136,128]{1,0:T(8,128)S(1)} %constant_dynamic-slice_fusion), channel_id=1, source_target_pairs={{0,8},{2,6},{4,12},{6,2},{8,0},{10,14},{12,4},{14,10},{16,24},{18,... | collective-permute-start | bytes 208904 | tf_op jit(solution)/shard_map/ppermute | solution.py:463
  16.2 9.7 %collective-permute-start.2 = (f32[392,128]{1,0:T(8,128)S(1)}, f32[392,128]{1,0:T(8,128)S(1)}, u32[]{:S(2)}, u32[]{:S(2)}) collective-permute-start(f32[392,128]{1,0:T(8,128)S(1)} %constant_dynamic-slice_fusion.1), channel_id=1, source_target_pairs={{0,4},{2,10},{4,0},{6,14},{8,12},{10,2},{12,8},{14,6},{16,20},{18,... | collective-permute-start | bytes 602120 | tf_op jit(solution)/shard_map/ppermute | solution.py:463
  20.5 5.3 %collective-permute-start.7 = (f32[136,128]{1,0:T(8,128)S(1)}, f32[136,128]{1,0:T(8,128)S(1)}, u32[]{:S(2)}, u32[]{:S(2)}) collective-permute-start(f32[136,128]{1,0:T(8,128)S(1)} %dynamic-slice_add_fusion.1), channel_id=1, source_target_pairs={{0,16},{2,18},{4,20},{6,22},{8,24},{10,26},{12,28},{14,30},{16,0},... | collective-permute-start | bytes 208904 | tf_op jit(solution)/shard_map/ppermute | solution.py:463
  25.8 5.2 %collective-permute-start.8 = (f32[136,128]{1,0:T(8,128)S(1)}, f32[136,128]{1,0:T(8,128)S(1)}, u32[]{:S(2)}, u32[]{:S(2)}) collective-permute-start(f32[136,128]{1,0:T(8,128)S(1)} %add.64), channel_id=1, source_target_pairs={{0,8},{2,6},{4,12},{6,2},{8,0},{10,14},{12,4},{14,10},{16,24},{18,... | collective-permute-start | bytes 208904 | tf_op jit(solution)/shard_map/ppermute | solution.py:463
  25.9 8.8 %collective-permute-start.3 = (f32[392,128]{1,0:T(8,128)S(1)}, f32[392,128]{1,0:T(8,128)S(1)}, u32[]{:S(2)}, u32[]{:S(2)}) collective-permute-start(f32[392,128]{1,0:T(8,128)S(1)} %dynamic-slice_add_fusion), channel_id=1, source_target_pairs={{0,16},{2,18},{4,20},{6,22},{8,24},{10,26},{12,28},{14,30},{16,0},... | collective-permute-start | bytes 602120 | tf_op jit(solution)/shard_map/ppermute | solution.py:463
  31.0 6.8 %collective-permute-start.9 = (f32[272,128]{1,0:T(8,128)S(1)}, f32[272,128]{1,0:T(8,128)S(1)}, u32[]{:S(2)}, u32[]{:S(2)}) collective-permute-start(f32[272,128]{1,0:T(8,128)S(1)} %pad_maximum_fusion.1.p0), channel_id=1, source_target_pairs={{0,4},{2,10},{4,0},{6,14},{8,12},{10,2},{12,8},{14,6},{16,20},{18,... | collective-permute-start | bytes 417800 | tf_op jit(solution)/shard_map/ppermute | solution.py:463
  34.8 8.5 %collective-permute-start.4 = (f32[392,128]{1,0:T(8,128)S(1)}, f32[392,128]{1,0:T(8,128)S(1)}, u32[]{:S(2)}, u32[]{:S(2)}) collective-permute-start(f32[392,128]{1,0:T(8,128)S(1)} %add.59), channel_id=1, source_target_pairs={{0,4},{2,10},{4,0},{6,14},{8,12},{10,2},{12,8},{14,6},{16,20},{18,... | collective-permute-start | bytes 602120 | tf_op jit(solution)/shard_map/ppermute | solution.py:463
  34.9 2.9 %collective-permute-start.10 = (f32[272,128]{1,0:T(8,128)S(1)}, f32[272,128]{1,0:T(8,128)S(1)}, u32[]{:S(2)}, u32[]{:S(2)}) collective-permute-start(f32[272,128]{1,0:T(8,128)S(1)} %pad_maximum_fusion.1.p0), channel_id=1, source_target_pairs={{0,2},{2,0},{1,3},{3,1},{4,6},{6,4},{5,7},{7,5},{8,10},{10,8},{9,1... | collective-permute-start | bytes 417800 | tf_op jit(solution)/shard_map/ppermute | solution.py:486
  37.8 1.4 %collective-permute-start.11 = (f32[272,128]{1,0:T(8,128)S(1)}, f32[272,128]{1,0:T(8,128)S(1)}, u32[]{:S(2)}, u32[]{:S(2)}) collective-permute-start(f32[272,128]{1,0:T(8,128)S(1)} %collective-permute-done.9.p1), channel_id=1, source_target_pairs={{0,2},{2,0},{1,3},{3,1},{4,6},{6,4},{5,7},{7,5},{8,10},{10,8},{9,1... | collective-permute-start | bytes 417800 | tf_op jit(solution)/shard_map/ppermute | solution.py:486
  43.4 8.8 %collective-permute-start.12 = (f32[784,128]{1,0:T(8,128)S(1)}, f32[784,128]{1,0:T(8,128)S(1)}, u32[]{:S(2)}, u32[]{:S(2)}) collective-permute-start(f32[784,128]{1,0:T(8,128)S(1)} %pad_maximum_fusion.refs_0_), channel_id=1, source_target_pairs={{0,8},{2,6},{4,12},{6,2},{8,0},{10,14},{12,4},{14,10},{16,24},{18,... | collective-permute-start | bytes 1204232 | tf_op jit(solution)/shard_map/ppermute | solution.py:463
  50.4 5.4 %collective-permute-start.13 = (f32[784,128]{1,0:T(8,128)S(1)}, f32[784,128]{1,0:T(8,128)S(1)}, u32[]{:S(2)}, u32[]{:S(2)}) collective-permute-start(f32[784,128]{1,0:T(8,128)S(1)} %pad_maximum_fusion.refs_0_), channel_id=1, source_target_pairs={{0,2},{2,0},{1,3},{3,1},{4,6},{6,4},{5,7},{7,5},{8,10},{10,8},{9,1... | collective-permute-start | bytes 1204232 | tf_op jit(solution)/shard_map/ppermute | solution.py:486
  52.1 3.7 %collective-permute-start.14 = (f32[784,128]{1,0:T(8,128)S(1)}, f32[784,128]{1,0:T(8,128)S(1)}, u32[]{:S(2)}, u32[]{:S(2)}) collective-permute-start(f32[784,128]{1,0:T(8,128)S(1)} %collective-permute-done.12.refs_1_), channel_id=1, source_target_pairs={{0,2},{2,0},{1,3},{3,1},{4,6},{6,4},{5,7},{7,5},{8,10},{10,8},{9,1... | collective-permute-start | bytes 1204232 | tf_op jit(solution)/shard_map/ppermute | solution.py:486

commit v6 on v5

--- a/solution.py
+++ b/solution.py
@@ -11,6 +11,7 @@
 BF16 = jnp.bfloat16
 NB = 128
 SUB = 8
+ROOT_SCALE = 2.0**20
 
 
 def split(x):
@@ -264,13 +265,13 @@
 
 
 def factor_step(k, n, read, upper_ref, inv_ref, write, pending):
-    source = read(k, k)
+    source = read(k, k) * F32(ROOT_SCALE**2)
 
     def put_upper(g, v):
-        upper_ref[at(g, SUB), at(k)] = v
+        upper_ref[at(g, SUB), at(k)] = v * F32(1 / ROOT_SCALE)
 
     def put_inverse(g, v):
-        inv_ref[at(g, SUB), :] = v
+        inv_ref[at(g, SUB), :] = v * F32(ROOT_SCALE)
 
     factor_block([source[at(h, SUB), :] for h in range(NB // SUB)], put_upper, put_inverse, pending)
     if k:

time: 74 us -> 74 us (level)
  no operation moved by 1% of the time
where the time goes in v6:
time: 74 us; the launch traced here: 73.8 us
  Pallas kernels  35.3 us (48%)
  waiting for transfers between devices  18.5 us (25%)
  starting transfers between devices  17.8 us (24%)
  local copies, waits for them, and re-layouts  1.17 us (2%)
  between operations  0.79 us (1%)
    pallas_call x7, Pallas kernels, call(): pl.pallas_call(kernel, out_shape=out_shape, in_specs=[smem if s else vmem...  35.3 us
    ppermute x10, waiting for transfers between devices, exchange(): return lax.ppermute(x, ('rows', 'tensor'), perm)  16.6 us
    ppermute x10, starting transfers between devices, exchange(): return lax.ppermute(x, ('rows', 'tensor'), perm)  15.4 us
    ppermute x2, starting transfers between devices, sum_rows(): lax.ppermute(total, 'tensor', swap)  1.79 us
  transfers between devices with their start and end apart: 15, of which 8 were waited for; matrix products, arithmetic and copies ran while one was open for 0% of the time, Pallas kernels for 20%

profile of v6, /device:TPU:0, one launch (start us, length us, event | category | flops | bytes accessed | tf_op | source)
XLA Modules:
  0.0 73.8 jit_solution(7096546960514629049)
XLA Ops:
  0.6 0.5 collective-permute-start
  1.1 0.0 copy-start
  1.1 1.0 %copy-done = f32[256,512]{1,0:T(8,128)S(1)} copy-done((f32[256,512]{1,0:T(8,128)S(1)}, f32[256,512]{1,0:T(8,128)}, u32[]{:S(2)}) %copy-start) | copy-done | bytes 524312
  2.2 0.1 stack.23.s_ref
  2.3 0.6 collective-permute-done.other_ref.refs_5_
  2.9 1.6 %gram_second.1 = (f32[784,128]{1,0:T(8,128)S(1)}, f32[784,128]{1,0:T(8,128)S(1)}) custom-call(s32[5]{0:T(128)S(1)} %stack.23.s_ref, f32[256,512]{1,0:T(8,128)S(1)} %own_copy.1.own_ref.refs_4_, f32[256,512]{1,0:T(8,128)S(1)} %collective-permute-done.other_ref.refs_5_), custom_call_target="tpu_custom_call" | custom-call | tf_op jit(solution)/shard_map/gram_second/pallas_call | solution.py:498
  4.5 1.3 %gram_first.1 = (f32[272,128]{1,0:T(8,128)S(1)}, f32[272,128]{1,0:T(8,128)S(1)}) custom-call(s32[5]{0:T(128)S(1)} %stack.23.s_ref, f32[256,512]{1,0:T(8,128)S(1)} %own_copy.1.own_ref.refs_4_, f32[256,512]{1,0:T(8,128)S(1)} %collective-permute-done.other_ref.refs_5_), custom_call_target="tpu_custom_call" | custom-call | tf_op jit(solution)/shard_map/gram_first/pallas_call | solution.py:498
  5.8 3.0 %collective-permute-start.1 = (f32[784,128]{1,0:T(8,128)S(1)}, f32[784,128]{1,0:T(8,128)S(1)}, u32[]{:S(2)}, u32[]{:S(2)}) collective-permute-start(f32[784,128]{1,0:T(8,128)S(1)} %get-tuple-element.34), channel_id=1, source_target_pairs={{0,8},{2,6},{4,12},{6,2},{8,0},{10,14},{12,4},{14,10},{16,24},{18,... | collective-permute-start | bytes 1204232 | tf_op jit(solution)/shard_map/ppermute | solution.py:464
  8.8 1.5 %collective-permute-start.5 = (f32[272,128]{1,0:T(8,128)S(1)}, f32[272,128]{1,0:T(8,128)S(1)}, u32[]{:S(2)}, u32[]{:S(2)}) collective-permute-start(f32[272,128]{1,0:T(8,128)S(1)} %get-tuple-element.36), channel_id=1, source_target_pairs={{0,4},{2,10},{4,0},{6,14},{8,12},{10,2},{12,8},{14,6},{16,20},{18,... | collective-permute-start | bytes 417800 | tf_op jit(solution)/shard_map/ppermute | solution.py:464
  10.3 5.1 %collective-permute-done.5 = f32[272,128]{1,0:T(8,128)S(1)} collective-permute-done((f32[272,128]{1,0:T(8,128)S(1)}, f32[272,128]{1,0:T(8,128)S(1)}, u32[]{:S(2)}, u32[]{:S(2)}) %collective-permute-start.5) | collective-permute-done | bytes 139296 | tf_op jit(solution)/shard_map/ppermute | solution.py:464
  15.4 0.1 collective-permute-start.6
  15.5 0.6 collective-permute-done.1
  16.1 0.1 add.55
  16.2 1.4 %collective-permute-start.2 = (f32[392,128]{1,0:T(8,128)S(1)}, f32[392,128]{1,0:T(8,128)S(1)}, u32[]{:S(2)}, u32[]{:S(2)}) collective-permute-start(f32[392,128]{1,0:T(8,128)S(1)} %constant_dynamic-slice_fusion.1), channel_id=1, source_target_pairs={{0,4},{2,10},{4,0},{6,14},{8,12},{10,2},{12,8},{14,6},{16,20},{18,... | collective-permute-start | bytes 602120 | tf_op jit(solution)/shard_map/ppermute | solution.py:464
  17.6 2.9 %collective-permute-done.6 = f32[136,128]{1,0:T(8,128)S(1)} collective-permute-done((f32[136,128]{1,0:T(8,128)S(1)}, f32[136,128]{1,0:T(8,128)S(1)}, u32[]{:S(2)}, u32[]{:S(2)}) %collective-permute-start.6) | collective-permute-done | bytes 69664 | tf_op jit(solution)/shard_map/ppermute | solution.py:464
  20.5 2.6 %collective-permute-start.7 = (f32[136,128]{1,0:T(8,128)S(1)}, f32[136,128]{1,0:T(8,128)S(1)}, u32[]{:S(2)}, u32[]{:S(2)}) collective-permute-start(f32[136,128]{1,0:T(8,128)S(1)} %dynamic-slice_add_fusion.1), channel_id=1, source_target_pairs={{0,16},{2,18},{4,20},{6,22},{8,24},{10,26},{12,28},{14,30},{16,0},... | collective-permute-start | bytes 208904 | tf_op jit(solution)/shard_map/ppermute | solution.py:464
  23.1 2.6 %collective-permute-done.7 = f32[136,128]{1,0:T(8,128)S(1)} collective-permute-done((f32[136,128]{1,0:T(8,128)S(1)}, f32[136,128]{1,0:T(8,128)S(1)}, u32[]{:S(2)}, u32[]{:S(2)}) %collective-permute-start.7) | collective-permute-done | bytes 69664 | tf_op jit(solution)/shard_map/ppermute | solution.py:464
  25.8 0.1 collective-permute-start.8
  25.9 0.0 collective-permute-done.2
  25.9 2.6 %collective-permute-start.3 = (f32[392,128]{1,0:T(8,128)S(1)}, f32[392,128]{1,0:T(8,128)S(1)}, u32[]{:S(2)}, u32[]{:S(2)}) collective-permute-start(f32[392,128]{1,0:T(8,128)S(1)} %dynamic-slice_add_fusion), channel_id=1, source_target_pairs={{0,16},{2,18},{4,20},{6,22},{8,24},{10,26},{12,28},{14,30},{16,0},... | collective-permute-start | bytes 602120 | tf_op jit(solution)/shard_map/ppermute | solution.py:464
  28.5 2.4 %collective-permute-done.8 = f32[136,128]{1,0:T(8,128)S(1)} collective-permute-done((f32[136,128]{1,0:T(8,128)S(1)}, f32[136,128]{1,0:T(8,128)S(1)}, u32[]{:S(2)}, u32[]{:S(2)}) %collective-permute-start.8) | collective-permute-done | bytes 69664 | tf_op jit(solution)/shard_map/ppermute | solution.py:464
  31.0 3.8 %collective-permute-start.9 = (f32[272,128]{1,0:T(8,128)S(1)}, f32[272,128]{1,0:T(8,128)S(1)}, u32[]{:S(2)}, u32[]{:S(2)}) collective-permute-start(f32[272,128]{1,0:T(8,128)S(1)} %pad_maximum_fusion.1.p0), channel_id=1, source_target_pairs={{0,4},{2,10},{4,0},{6,14},{8,12},{10,2},{12,8},{14,6},{16,20},{18,... | collective-permute-start | bytes 417800 | tf_op jit(solution)/shard_map/ppermute | solution.py:464
  34.8 0.0 collective-permute-done.3
  34.8 0.1 collective-permute-start.4
  34.9 0.1 collective-permute-start.10
  35.0 2.8 %collective-permute-done.9.p1 = f32[272,128]{1,0:T(8,128)S(1)} collective-permute-done((f32[272,128]{1,0:T(8,128)S(1)}, f32[272,128]{1,0:T(8,128)S(1)}, u32[]{:S(2)}, u32[]{:S(2)}) %collective-permute-start.9) | collective-permute-done | bytes 139296 | tf_op jit(solution)/shard_map/ppermute | solution.py:464
  37.8 0.0 collective-permute-start.11
  37.8 0.0 collective-permute-done.10.p2
  37.8 1.4 %collective-permute-done.11.p3 = f32[272,128]{1,0:T(8,128)S(1)} collective-permute-done((f32[272,128]{1,0:T(8,128)S(1)}, f32[272,128]{1,0:T(8,128)S(1)}, u32[]{:S(2)}, u32[]{:S(2)}) %collective-permute-start.11) | collective-permute-done | bytes 139296 | tf_op jit(solution)/shard_map/ppermute | solution.py:487
  39.2 4.1 %factor_rows.3 = (f32[128,512]{1,0:T(8,128)S(1)}, bf16[128,768]{1,0:T(8,128)(2,1)S(1)}, f32[128,512]{1,0:T(8,128)S(1)}, f32[512,512]{1,0:T(8,128)S(1)}, f32[512,512]{1,0:T(8,128)S(1)}) custom-call(s32[5]{0:T(128)S(1)} %stack.23.s_ref, f32[272,128]{1,0:T(8,128)S(1)} %pad_maximum_fusion.1.p0, f32[272,128]{1,0:T(8,128)S(1)} %collective-permute-done.9.p1, ...), custom_call_target="tpu_custom_call" | custom-call | tf_op jit(solution)/shard_map/factor_rows/pallas_call | solution.py:498
  43.3 0.0 collective-permute-done.4
  43.3 0.1 broadcast_select_fusion.1
  43.4 0.3 collective-permute-start.12
  43.7 6.8 %factor_rows.4 = (f32[256,128]{1,0:T(8,128)S(1)}, f32[128,512]{1,0:T(8,128)S(1)}, f32[128,512]{1,0:T(8,128)S(1)}, bf16[128,1536]{1,0:T(8,128)(2,1)S(1)}, bf16[12...) custom-call(s32[5]{0:T(128)S(1)} %stack.23.s_ref, ...), custom_call_target="tpu_custom_call" | custom-call | tf_op jit(solution)/shard_map/factor_rows/pallas_call | solution.py:498
  50.4 1.7 %collective-permute-start.13 = (f32[784,128]{1,0:T(8,128)S(1)}, f32[784,128]{1,0:T(8,128)S(1)}, u32[]{:S(2)}, u32[]{:S(2)}) collective-permute-start(f32[784,128]{1,0:T(8,128)S(1)} %pad_maximum_fusion.refs_0_), channel_id=1, source_target_pairs={{0,2},{2,0},{1,3},{3,1},{4,6},{6,4},{5,7},{7,5},{8,10},{10,8},{9,1... | collective-permute-start | bytes 1204232 | tf_op jit(solution)/shard_map/ppermute | solution.py:487
  52.1 0.0 collective-permute-done.12.refs_1_
  52.1 0.1 collective-permute-start.14
  52.2 3.6 %factor_rows.5 = (f32[256,128]{1,0:T(8,128)S(1)}, f32[256,128]{1,0:T(8,128)S(1)}, f32[128,512]{1,0:T(8,128)S(1)}, bf16[128,3072]{1,0:T(8,128)(2,1)S(1)}, f32[128,512]{1,0:T(8,128)S(1)}) custom-call(s32[5]{0:T(128)S(1)} %stack.23.s_ref, f32[256,512]{1,0:T(8,128)S(1)} %own_copy.1.own_ref.refs_4_, f32[256,512]{1,0:T(8,128)S(1)} %collective-permute-done.other_ref.refs_5_, ...), custom_call_target="tpu_custom_call" | custom-call | tf_op jit(solution)/shard_map/factor_rows/pallas_call | solution.py:498
  55.8 0.0 collective-permute-done.13.refs_2_
  55.8 0.0 collective-permute-done.14.refs_3_
  55.8 18.0 %factor_last.1 = (f32[256,512]{1,0:T(8,128)}, f32[1024,512]{1,0:T(8,128)}) custom-call(s32[5]{0:T(128)S(1)} %stack.23.s_ref, f32[784,128]{1,0:T(8,128)S(1)} %pad_maximum_fusion.refs_0_, f32[784,128]{1,0:T(8,128)S(1)} %collective-permute-done.12.refs_1_, f32[784,128]{1,0:T(8,128)S(1)} %collective-permute-done.13.refs_2_, ...), custom_call_target="tpu_custom_call" | custom-call | tf_op jit(solution)/shard_map/factor_last/pallas_call | solution.py:498
  (11 shorter events, 0.2 us)
Async XLA Ops:
  0.6 2.3 %collective-permute-start = (f32[256,512]{1,0:T(8,128)}, f32[256,512]{1,0:T(8,128)S(1)}, u32[]{:S(2)}, u32[]{:S(2)}) collective-permute-start(f32[256,512]{1,0:T(8,128)} %x_ref.1), channel_id=1, source_target_pairs={{0,2},{2,0},{1,3},{3,1},{4,6},{6,4},{5,7},{7,5},{8,10},{10,8},{9,1... | collective-permute-start | bytes 1572872 | tf_op jit(solution)/shard_map/ppermute | solution.py:517
  1.1 1.0 %copy-start = (f32[256,512]{1,0:T(8,128)S(1)}, f32[256,512]{1,0:T(8,128)}, u32[]{:S(2)}) copy-start(f32[256,512]{1,0:T(8,128)} %x_ref.1) | copy-start | bytes 1572868
  5.8 10.3 %collective-permute-start.1 = (f32[784,128]{1,0:T(8,128)S(1)}, f32[784,128]{1,0:T(8,128)S(1)}, u32[]{:S(2)}, u32[]{:S(2)}) collective-permute-start(f32[784,128]{1,0:T(8,128)S(1)} %get-tuple-element.34), channel_id=1, source_target_pairs={{0,8},{2,6},{4,12},{6,2},{8,0},{10,14},{12,4},{14,10},{16,24},{18,... | collective-permute-start | bytes 1204232 | tf_op jit(solution)/shard_map/ppermute | solution.py:464
  8.8 6.6 %collective-permute-start.5 = (f32[272,128]{1,0:T(8,128)S(1)}, f32[272,128]{1,0:T(8,128)S(1)}, u32[]{:S(2)}, u32[]{:S(2)}) collective-permute-start(f32[272,128]{1,0:T(8,128)S(1)} %get-tuple-element.36), channel_id=1, source_target_pairs={{0,4},{2,10},{4,0},{6,14},{8,12},{10,2},{12,8},{14,6},{16,20},{18,... | collective-permute-start | bytes 417800 | tf_op jit(solution)/shard_map/ppermute | solution.py:464
  15.4 5.1 %collective-permute-start.6 = (f32[136,128]{1,0:T(8,128)S(1)}, f32[136,128]{1,0:T(8,128)S(1)}, u32[]{:S(2)}, u32[]{:S(2)}) collective-permute-start(f32[136,128]{1,0:T(8,128)S(1)} %constant_dynamic-slice_fusion), channel_id=1, source_target_pairs={{0,8},{2,6},{4,12},{6,2},{8,0},{10,14},{12,4},{14,10},{16,24},{18,... | collective-permute-start | bytes 208904 | tf_op jit(solution)/shard_map/ppermute | solution.py:464
  16.2 9.7 %collective-permute-start.2 = (f32[392,128]{1,0:T(8,128)S(1)}, f32[392,128]{1,0:T(8,128)S(1)}, u32[]{:S(2)}, u32[]{:S(2)}) collective-permute-start(f32[392,128]{1,0:T(8,128)S(1)} %constant_dynamic-slice_fusion.1), channel_id=1, source_target_pairs={{0,4},{2,10},{4,0},{6,14},{8,12},{10,2},{12,8},{14,6},{16,20},{18,... | collective-permute-start | bytes 602120 | tf_op jit(solution)/shard_map/ppermute | solution.py:464
  20.5 5.3 %collective-permute-start.7 = (f32[136,128]{1,0:T(8,128)S(1)}, f32[136,128]{1,0:T(8,128)S(1)}, u32[]{:S(2)}, u32[]{:S(2)}) collective-permute-start(f32[136,128]{1,0:T(8,128)S(1)} %dynamic-slice_add_fusion.1), channel_id=1, source_target_pairs={{0,16},{2,18},{4,20},{6,22},{8,24},{10,26},{12,28},{14,30},{16,0},... | collective-permute-start | bytes 208904 | tf_op jit(solution)/shard_map/ppermute | solution.py:464
  25.8 5.2 %collective-permute-start.8 = (f32[136,128]{1,0:T(8,128)S(1)}, f32[136,128]{1,0:T(8,128)S(1)}, u32[]{:S(2)}, u32[]{:S(2)}) collective-permute-start(f32[136,128]{1,0:T(8,128)S(1)} %add.64), channel_id=1, source_target_pairs={{0,8},{2,6},{4,12},{6,2},{8,0},{10,14},{12,4},{14,10},{16,24},{18,... | collective-permute-start | bytes 208904 | tf_op jit(solution)/shard_map/ppermute | solution.py:464
  25.9 8.8 %collective-permute-start.3 = (f32[392,128]{1,0:T(8,128)S(1)}, f32[392,128]{1,0:T(8,128)S(1)}, u32[]{:S(2)}, u32[]{:S(2)}) collective-permute-start(f32[392,128]{1,0:T(8,128)S(1)} %dynamic-slice_add_fusion), channel_id=1, source_target_pairs={{0,16},{2,18},{4,20},{6,22},{8,24},{10,26},{12,28},{14,30},{16,0},... | collective-permute-start | bytes 602120 | tf_op jit(solution)/shard_map/ppermute | solution.py:464
  31.0 6.8 %collective-permute-start.9 = (f32[272,128]{1,0:T(8,128)S(1)}, f32[272,128]{1,0:T(8,128)S(1)}, u32[]{:S(2)}, u32[]{:S(2)}) collective-permute-start(f32[272,128]{1,0:T(8,128)S(1)} %pad_maximum_fusion.1.p0), channel_id=1, source_target_pairs={{0,4},{2,10},{4,0},{6,14},{8,12},{10,2},{12,8},{14,6},{16,20},{18,... | collective-permute-start | bytes 417800 | tf_op jit(solution)/shard_map/ppermute | solution.py:464
  34.8 8.5 %collective-permute-start.4 = (f32[392,128]{1,0:T(8,128)S(1)}, f32[392,128]{1,0:T(8,128)S(1)}, u32[]{:S(2)}, u32[]{:S(2)}) collective-permute-start(f32[392,128]{1,0:T(8,128)S(1)} %add.59), channel_id=1, source_target_pairs={{0,4},{2,10},{4,0},{6,14},{8,12},{10,2},{12,8},{14,6},{16,20},{18,... | collective-permute-start | bytes 602120 | tf_op jit(solution)/shard_map/ppermute | solution.py:464
  34.9 2.9 %collective-permute-start.10 = (f32[272,128]{1,0:T(8,128)S(1)}, f32[272,128]{1,0:T(8,128)S(1)}, u32[]{:S(2)}, u32[]{:S(2)}) collective-permute-start(f32[272,128]{1,0:T(8,128)S(1)} %pad_maximum_fusion.1.p0), channel_id=1, source_target_pairs={{0,2},{2,0},{1,3},{3,1},{4,6},{6,4},{5,7},{7,5},{8,10},{10,8},{9,1... | collective-permute-start | bytes 417800 | tf_op jit(solution)/shard_map/ppermute | solution.py:487
  37.8 1.4 %collective-permute-start.11 = (f32[272,128]{1,0:T(8,128)S(1)}, f32[272,128]{1,0:T(8,128)S(1)}, u32[]{:S(2)}, u32[]{:S(2)}) collective-permute-start(f32[272,128]{1,0:T(8,128)S(1)} %collective-permute-done.9.p1), channel_id=1, source_target_pairs={{0,2},{2,0},{1,3},{3,1},{4,6},{6,4},{5,7},{7,5},{8,10},{10,8},{9,1... | collective-permute-start | bytes 417800 | tf_op jit(solution)/shard_map/ppermute | solution.py:487
  43.4 8.8 %collective-permute-start.12 = (f32[784,128]{1,0:T(8,128)S(1)}, f32[784,128]{1,0:T(8,128)S(1)}, u32[]{:S(2)}, u32[]{:S(2)}) collective-permute-start(f32[784,128]{1,0:T(8,128)S(1)} %pad_maximum_fusion.refs_0_), channel_id=1, source_target_pairs={{0,8},{2,6},{4,12},{6,2},{8,0},{10,14},{12,4},{14,10},{16,24},{18,... | collective-permute-start | bytes 1204232 | tf_op jit(solution)/shard_map/ppermute | solution.py:464
  50.4 5.4 %collective-permute-start.13 = (f32[784,128]{1,0:T(8,128)S(1)}, f32[784,128]{1,0:T(8,128)S(1)}, u32[]{:S(2)}, u32[]{:S(2)}) collective-permute-start(f32[784,128]{1,0:T(8,128)S(1)} %pad_maximum_fusion.refs_0_), channel_id=1, source_target_pairs={{0,2},{2,0},{1,3},{3,1},{4,6},{6,4},{5,7},{7,5},{8,10},{10,8},{9,1... | collective-permute-start | bytes 1204232 | tf_op jit(solution)/shard_map/ppermute | solution.py:487
  52.1 3.7 %collective-permute-start.14 = (f32[784,128]{1,0:T(8,128)S(1)}, f32[784,128]{1,0:T(8,128)S(1)}, u32[]{:S(2)}, u32[]{:S(2)}) collective-permute-start(f32[784,128]{1,0:T(8,128)S(1)} %collective-permute-done.12.refs_1_), channel_id=1, source_target_pairs={{0,2},{2,0},{1,3},{3,1},{4,6},{6,4},{5,7},{7,5},{8,10},{10,8},{9,1... | collective-permute-start | bytes 1204232 | tf_op jit(solution)/shard_map/ppermute | solution.py:487
